TPU v7x, 32 devices: a whole 2x2x4 slice. The times are simulated.
32 devices in a mesh: sec: 2 (over x), grp: 4 (over y, core), rank: 4 (over z).
Axes of the slice: x: 2, y: 2, z: 4, core: 2. Of those that a mesh axis runs over, the one named last changes fastest.
Arguments:
- queries: bfloat16 [8, 128, 8192], P(('sec', 'grp')), may hold values from -6 to 14
- kv_cache: bfloat16 [8, 4096, 2048], P(('sec', 'grp'), 'rank'), may hold values from -6 to 10
- key_scale: float32 [1024], replicated, may hold values from 0.5 to 2
- fresh_input: bfloat16 [8, 128, 8192], P(('sec', 'grp'), None, 'rank'), may hold values from -6 to 6
- kv_weight: bfloat16 [8192, 2048], P('rank'), may hold values from -0.0625 to 0.0625
- lengths: int32 [8, 1], P(('sec', 'grp')), may hold values from 1 to 4096
- page_list: int32 [512], P(('sec', 'grp', 'rank')), may hold values from 0 to 63, as said below
- owners: int32 [512, 1], P(('sec', 'grp', 'rank')), may hold values from 0 to 3; in each aligned block of 16 rows (0 to 15, 16 to 31, ...) at most 8 rows name the same one
Outputs:
- attended: bfloat16 [8, 128, 8192], P(('sec', 'grp'), None, 'rank')
- handed: bfloat16 [32, 32, 16, 2048], P(('sec', 'grp', 'rank'))
Inputs may be any that keep to these rules, and one draw needn't show every extreme that they name: `page_list`: the 16 entries of one device are distinct page numbers of its own cache. `owners`: among the 16 entries of one device at most 8 name the same owner, and some device has exactly 8 for one owner.
All inputs are finite; a program needn't handle non-finite values.
Results may differ from a plain program's by a relative error of at most 0.0045.
The roundings to bfloat16 on the way count: a program that leaves them out, or rounds other values in their place, can miss the bound.
Values may be sent and summed in bfloat16 or wider, within the bound.
No kernel may reach another device: no remote copies, remote signals or barrier semaphores. Data moves between devices by JAX's collectives and lax.ppermute only.
A program may use at most 192 MiB of HBM per device.

v0:
```python
import math

import jax
import jax.numpy as jnp
from jax import lax
from jax.sharding import PartitionSpec as P

HEADS = 64
KVH = 8
HD = 128
ROWS = 128
CTX = 1024
PAGE = 16
GQ = 8
KVW = 1024


ROPE_BASE = 500000.0
NEG_FILL = -1e30


def passed_along(value, axis, by):
    devices = lax.axis_size(axis)
    pairs = [(i, i + by) for i in range(devices) if 0 <= i + by < devices]
    return lax.ppermute(value, axis, pairs)


def combined_all(part, axis, combine):
    gathered = jax.tree.map(lambda a: lax.all_gather(a, axis), part)

    def take(source):
        return jax.tree.map(lambda a: lax.dynamic_index_in_dim(a, source, 0, False), gathered)

    return lax.fori_loop(
        1, lax.axis_size(axis), lambda source, state: combine(state, take(source)), take(0)
    )


def rope_tables(positions):
    half_width = HD // 2
    steps_index = jnp.arange(half_width, dtype=jnp.float32)
    inverse = jnp.exp(steps_index * (-2.0 * math.log(ROPE_BASE) / HD))
    angles = positions.astype(jnp.float32)[:, None] * inverse[None, :]
    return (jnp.cos(angles)[:, None, :], jnp.sin(angles)[:, None, :])


def rotate_heads(values, cosine, sine_part):
    half_width = HD // 2
    first_half = values[..., :half_width]
    second_half = values[..., half_width:]
    return jnp.concatenate(
        [
            first_half * cosine - second_half * sine_part,
            second_half * cosine + first_half * sine_part,
        ],
        axis=-1,
    )


def combine_parts(earlier, latter):
    row_top = jnp.maximum(earlier[0], latter[0])
    first_factor = jnp.exp(earlier[0] - row_top)
    second_factor = jnp.exp(latter[0] - row_top)
    return (
        row_top,
        earlier[1] * first_factor + latter[1] * second_factor,
        earlier[2] * first_factor[..., None] + latter[2] * second_factor[..., None],
    )


def shards(queries, kv_cache, key_scale, fresh_input, kv_weight, lengths, page_list, owners):
    rank_count = lax.axis_size("rank")
    position = lax.axis_index("rank")
    row_share = ROWS // rank_count
    heads_here = HEADS // rank_count
    cache_rows = kv_cache[0]
    entries = page_list.shape[0]
    slot_count = 2 * entries // rank_count
    page_blocks = cache_rows.reshape(CTX // PAGE, PAGE, 2 * KVW)
    owner_ids = owners[:, 0]
    targets = jnp.arange(rank_count, dtype=jnp.int32)
    onehot = (owner_ids[:, None] == targets[None, :]).astype(jnp.int32)
    running = jnp.cumsum(onehot, axis=0)
    slot_index = jnp.sum(onehot * running, axis=1) - 1
    places = jnp.arange(slot_count, dtype=jnp.int32)
    matches = (owner_ids[None, None, :] == targets[:, None, None]) & (
        slot_index[None, None, :] == places[None, :, None]
    )
    present = jnp.any(matches, axis=-1)
    chosen = jnp.sum(jnp.where(matches, page_list[None, None, :], 0), axis=-1)
    outgoing = jnp.where(present[..., None, None], page_blocks[chosen], jnp.zeros((), jnp.bfloat16))
    routed = lax.all_to_all(outgoing, "rank", split_axis=0, concat_axis=0, tiled=True)
    handed = passed_along(routed, "sec", 1)
    handed = handed.reshape(1, rank_count * slot_count, PAGE, 2 * KVW)
    rows_in = fresh_input[0]
    summed = lax.psum(jnp.dot(rows_in, kv_weight, preferred_element_type=jnp.float32), "rank")
    fresh_sum = lax.dynamic_slice_in_dim(summed, position * row_share, row_share, 0)
    fresh_kv = fresh_sum.astype(jnp.bfloat16)
    length = lengths[0, 0]
    row_ids = jnp.arange(ROWS, dtype=jnp.int32)
    cosine, sine_part = rope_tables(length + row_ids)
    query_rot = rotate_heads(
        queries[0].astype(jnp.float32).reshape(ROWS, HEADS, HD), cosine, sine_part
    ).astype(jnp.bfloat16)
    fresh_ids = position * row_share + jnp.arange(row_share, dtype=jnp.int32)
    fresh_cos, fresh_sin = rope_tables(length + fresh_ids)
    fresh_keys = rotate_heads(
        fresh_kv[:, :KVW].astype(jnp.float32).reshape(row_share, KVH, HD), fresh_cos, fresh_sin
    ).astype(jnp.bfloat16)
    cache_pos = position * CTX + jnp.arange(CTX, dtype=jnp.int32)
    cache_cos, cache_sin = rope_tables(cache_pos)
    scaled = (cache_rows[:, :KVW].astype(jnp.float32) * key_scale[None, :]).reshape(CTX, KVH, HD)
    cache_keys = rotate_heads(scaled, cache_cos, cache_sin).astype(jnp.bfloat16)
    keys_all = jnp.concatenate([cache_keys, fresh_keys], axis=0).transpose(1, 0, 2)
    vals_all = jnp.concatenate(
        [cache_rows[:, KVW:].reshape(CTX, KVH, HD), fresh_kv[:, KVW:].reshape(row_share, KVH, HD)],
        axis=0,
    ).transpose(1, 0, 2)
    allowed = jnp.concatenate(
        [
            jnp.broadcast_to((cache_pos < length)[None, :], (ROWS, CTX)),
            fresh_ids[None, :] <= row_ids[:, None],
        ],
        axis=1,
    )
    allowed_rows = jnp.repeat(allowed, GQ, axis=0)
    query_groups = (
        query_rot.reshape(ROWS, KVH, GQ, HD).transpose(1, 0, 2, 3).reshape(KVH, ROWS * GQ, HD)
    )

    def per_head(head_item):
        query_head, key_head, value_head = head_item
        scores = jnp.dot(query_head, key_head.T, preferred_element_type=jnp.float32) / math.sqrt(HD)
        masked = jnp.where(allowed_rows, scores, NEG_FILL)
        row_peak = jnp.max(masked, axis=-1)
        weights = jnp.where(allowed_rows, jnp.exp(masked - row_peak[:, None]), 0.0)
        row_total = jnp.sum(weights, axis=-1)
        numerator = jnp.dot(
            weights.astype(jnp.bfloat16), value_head, preferred_element_type=jnp.float32
        )
        return (row_peak, row_total, numerator)

    peaks, totals, numerators = lax.map(per_head, (query_groups, keys_all, vals_all))
    peaks = peaks.reshape(KVH, ROWS, GQ).transpose(1, 0, 2).reshape(ROWS, HEADS)
    totals = totals.reshape(KVH, ROWS, GQ).transpose(1, 0, 2).reshape(ROWS, HEADS)
    numerators = (
        numerators.reshape(KVH, ROWS, GQ, HD).transpose(1, 0, 2, 3).reshape(ROWS, HEADS, HD)
    )
    merged = combined_all((peaks, totals, numerators), "rank", combine_parts)
    own_numerator = lax.dynamic_slice_in_dim(merged[2], position * heads_here, heads_here, 1)
    own_total = lax.dynamic_slice_in_dim(merged[1], position * heads_here, heads_here, 1)
    attended = (
        (own_numerator / own_total[..., None])
        .reshape(1, ROWS, heads_here * HD)
        .astype(jnp.bfloat16)
    )
    return (attended, handed)


def solution(mesh):
    return jax.shard_map(
        shards,
        mesh=mesh,
        in_specs=(
            P(("sec", "grp"), None, None),
            P(("sec", "grp"), "rank", None),
            P(),
            P(("sec", "grp"), None, "rank"),
            P("rank", None),
            P(("sec", "grp"), None),
            P(("sec", "grp", "rank")),
            P(("sec", "grp", "rank"), None),
        ),
        out_specs=(P(("sec", "grp"), None, "rank"), P(("sec", "grp", "rank"), None, None, None)),
        check_vma=False,
    )
```

profile of v0, /device:TPU:0, one launch (start us, length us, event | category | flops | bytes accessed | tf_op | source)
XLA Modules:
  0.0 524.2 jit_solution(11036770236323846488)
XLA Ops:
  7.3 0.9 copy-done
  8.2 4.6 fusion.27
  12.9 45.1 %all-reduce.1 = bf16[128,2048]{1,0:T(8,128)(2,1)S(1)} all-reduce(f32[128,2048]{1,0:T(8,128)S(1)} %fusion.27), channel_id=1, replica_groups=mesh['sec'=2,'grp'=4,'rank'=4] {'rank'}, use_global_device_ids=true, to_apply=%region_0.0 | all-reduce | flops 262144 | bytes 1572864 | tf_op jit(solution)/shard_map/psum | solution.py:96
  59.3 1.0 multiply_cosine_fusion
  60.3 6.4 %copy.69 = bf16[1,1024,2048]{1,2,0:T(8,128)(2,1)} copy(bf16[1,1024,2048]{2,1,0:T(8,128)(2,1)} %param.13) | data formatting | bytes 8388608 | tf_op args[1]
  66.7 3.3 slice.53
  70.3 0.7 subtract_convert_fusion
  71.3 2.4 copy.72
  74.0 4.3 copy.67
  78.3 2.8 subtract_convert_fusion.1
  81.3 2.8 copy.68
  84.3 1.8 maximum_bitcast_fusion.1
  86.1 2.5 copy.73
  88.7 63.7 %while.35 = (s32[]{:T(128)}, f32[8,1024]{1,0:T(8,128)S(1)}, f32[8,1024]{1,0:T(8,128)S(1)}, f32[8,1024,128]{2,1,0:T(8,128)}, bf16[8,1024,128]{2,1,0:T(8,128)(2,1)...) while((s32[]{:T(128)}, f32[8,1024]{1,0:T(8,128)S(1)}, ...), condition=%wide.region_4.5_spmd.clone, body=%wide.region_1.0_spmd.clone.sunk | while | flops 563378176 | bytes 20961388 | solution.py:143
  89.3 1.3 copy.91
  90.6 1.9 fusion.49
  92.5 2.9 fusion.51
  95.4 1.0 fusion.50
  96.7 0.5 broadcast_bitcast_fusion.2
  97.2 1.3 copy.91
  98.5 1.9 fusion.49
  100.4 2.9 fusion.51
  103.3 1.0 fusion.50
  104.6 0.5 broadcast_bitcast_fusion.2
  105.1 1.3 copy.91
  106.4 1.9 fusion.49
  108.4 2.9 fusion.51
  111.3 1.0 fusion.50
  113.1 1.3 copy.91
  114.4 1.9 fusion.49
  116.3 2.9 fusion.51
  119.2 1.0 fusion.50
  121.0 1.3 copy.91
  122.3 1.9 fusion.49
  124.3 2.9 fusion.51
  127.1 1.0 fusion.50
  128.9 1.3 copy.91
  130.2 1.9 fusion.49
  132.2 2.9 fusion.51
  135.1 1.0 fusion.50
  136.9 1.3 copy.91
  138.2 1.9 fusion.49
  140.1 2.9 fusion.51
  143.0 1.0 fusion.50
  144.8 1.3 copy.91
  146.1 1.9 fusion.49
  148.1 2.9 fusion.51
  150.9 1.0 fusion.50
  152.4 4.7 copy_bitcast_fusion
  157.1 0.6 copy-done.4
  158.3 2.9 gather_fusion
  161.6 102.7 %all_to_all.5 = bf16[4,8,16,2048]{3,2,1,0:T(8,128)(2,1)} all-to-all(bf16[4,8,16,2048]{3,2,1,0:T(8,128)(2,1)S(1)} %broadcast_select_fusion), channel_id=1, replica_groups=mesh['sec'=2,'grp'=4,'rank'=4] {'rank'}, dimensions={0} | all-to-all | bytes 4194304 | tf_op jit(solution)/shard_map/all_to_all | solution.py:92
  264.3 3.5 collective-permute-start
  268.3 23.8 %all_gather.9 = f32[4,128,64]{1,2,0:T(8,128)S(1)} all-gather(f32[1,128,64]{1,2,0:T(8,128)S(1)} %bitcast.121), channel_id=1, replica_groups=mesh['sec'=2,'grp'=4,'rank'=4] {'rank'}, dimensions={0}, use_global_device_ids=true | all-gather | bytes 163840 | tf_op jit(solution)/shard_map/all_gather | solution.py:29
  292.7 25.2 %all_gather.10 = f32[4,128,64]{1,2,0:T(8,128)S(1)} all-gather(f32[1,128,64]{1,2,0:T(8,128)S(1)} %bitcast.122), channel_id=1, replica_groups=mesh['sec'=2,'grp'=4,'rank'=4] {'rank'}, dimensions={0}, use_global_device_ids=true | all-gather | bytes 163840 | tf_op jit(solution)/shard_map/all_gather | solution.py:29
  318.0 165.8 %all-gather.2.cloned.1.call-done = f32[4,128,64,128]{3,2,1,0:T(8,128)} async-done(((f32[1,128,64,128]{3,2,1,0:T(8,128)}), f32[4,128,64,128]{3,2,1,0:T(8,128)}) %all-gather.2.cloned.1.call-update) | async-done | bytes 16777232 | tf_op jit(solution)/shard_map/all_gather | solution.py:29
  483.8 4.7 slice_bitcast_fusion
  488.5 24.8 %while.34 = (s32[]{:T(128)}, f32[128,64]{1,0:T(8,128)S(1)}, f32[128,64]{1,0:T(8,128)S(1)}, f32[128,64,128]{2,1,0:T(8,128)}, f32[4,128,64]{1,2,0:T(8,128)S(1)}, /...) while((s32[]{:T(128)}, f32[128,64]{1,0:T(8,128)S(1)}, ...), condition=%wide.region_6.7_spmd, body=%wide.region_5.6_spmd.sunk | while | flops 3194885 | bytes 13172887 | solution.py:34
  488.8 8.0 %fusion.46 = f32[128,64,128]{2,1,0:T(8,128)} fusion(f32[4,128,64,128]{3,2,1,0:T(8,128)} %get-tuple-element.525, s32[]{:T(128)S(6)} %select_n.75, f32[128,64,128]{2,1,0:T(8,128)} %get-tuple-element.512, f32[128,64]{1,0:T(8,128)S(1)} %get-tuple-element.457, f32[128,64]{1,0:T(8,128)S(1)} %get-tuple-element.458), kind=kLoop, calls=%fused_computation.3.clone.1 | loop fusion | flops 3145728 | bytes 12648452 | tf_op jit(solution)/shard_map/while/body/eval_jaxpr/add | solution.py:67
  497.0 8.0 %fusion.46 = f32[128,64,128]{2,1,0:T(8,128)} fusion(f32[4,128,64,128]{3,2,1,0:T(8,128)} %get-tuple-element.525, s32[]{:T(128)S(6)} %select_n.75, f32[128,64,128]{2,1,0:T(8,128)} %get-tuple-element.512, f32[128,64]{1,0:T(8,128)S(1)} %get-tuple-element.457, f32[128,64]{1,0:T(8,128)S(1)} %get-tuple-element.458), kind=kLoop, calls=%fused_computation.3.clone.1 | loop fusion | flops 3145728 | bytes 12648452 | tf_op jit(solution)/shard_map/while/body/eval_jaxpr/add | solution.py:67
  505.3 8.0 %fusion.46 = f32[128,64,128]{2,1,0:T(8,128)} fusion(f32[4,128,64,128]{3,2,1,0:T(8,128)} %get-tuple-element.525, s32[]{:T(128)S(6)} %select_n.75, f32[128,64,128]{2,1,0:T(8,128)} %get-tuple-element.512, f32[128,64]{1,0:T(8,128)S(1)} %get-tuple-element.457, f32[128,64]{1,0:T(8,128)S(1)} %get-tuple-element.458), kind=kLoop, calls=%fused_computation.3.clone.1 | loop fusion | flops 3145728 | bytes 12648452 | tf_op jit(solution)/shard_map/while/body/eval_jaxpr/add | solution.py:67
  513.4 1.6 divide_convert_fusion
  515.0 1.0 convert_element_type.67
  516.0 1.3 copy.127
  (91 shorter events, 9.7 us)
Async XLA Ops:
  7.2 1.1 copy-start
  7.2 476.6 %all-gather.2.cloned.1.call-start = ((), (), s32[]{:S(2)}) async-start(), calls=%async_computation.1 | async-start | bytes 20971520 | tf_op jit(solution)/shard_map/all_gather | solution.py:29
  60.3 9.7 %copy-start.3 = (f32[1024]{0:T(1024)S(1)}, f32[1024]{0:T(1024)}, u32[]{:S(2)}) copy-start(f32[1024]{0:T(1024)} %param.14) | copy-start | bytes 12292
  66.7 3.3 copy-start.2
  157.1 0.7 copy-start.4
  157.1 1.0 copy-start.5
  264.3 53.7 %collective-permute-start = (bf16[4,8,16,2048]{3,2,1,0:T(8,128)(2,1)}, bf16[4,8,16,2048]{3,2,1,0:T(8,128)(2,1)S(1)}, u32[]{:S(2)}, u32[]{:S(2)}) collective-permute-start(bf16[4,8,16,2048]{3,2,1,0:T(8,128)(2,1)} %all_to_all.5), channel_id=1, source_target_pairs={{0,16},{1,17},{2,18},{3,19},{4,20},{5,21},{6,22},{7,23},{8,24},{9,... | collective-permute-start | bytes 6291464 | tf_op jit(solution)/shard_map/ppermute | solution.py:25
  515.0 2.4 copy-start.1
Sparse Core Ops, SparseCore 0:
  157.2 326.5 all-gather.1
where the time goes:
time: 526 us; the launch traced here: 524 us
  blocking collectives  197 us (37%)
  waiting for transfers between devices  166 us (32%)
  local copies, waits for them, and re-layouts  56.5 us (11%)
  matrix products  43.2 us (8%)
  other arithmetic  42.5 us (8%)
  between operations  15 us (3%)
    all_gather x1, waiting for transfers between devices, combined_all(): gathered = jax.tree.map(lambda a: lax.all_gather(a, axis), part)  166 us
    all_to_all x1, blocking collectives, shards(): lax.all_to_all(outgoing, 'rank', split_axis=0, concat_axis=0, tiled=True)  103 us
    all_gather x2, blocking collectives, combined_all(): gathered = jax.tree.map(lambda a: lax.all_gather(a, axis), part)  49 us
    psum x1, blocking collectives, shards(): lax.psum(jnp.dot(rows_in, kv_weight, preferred_element_type=jnp.float32),...  45.1 us
    add x3, other arithmetic, combine_parts(): earlier[2] * first_factor[..., None] + latter[2] * second_factor[..., None]  24 us
    dot_general x8, matrix products, per_head(): jnp.dot(weights.astype(jnp.bfloat16), value_head, preferred_element_type=...  23.1 us
    dot_general x8, matrix products, per_head(): jnp.dot(query_head, key_head.T, preferred_element_type=jnp.float32)  15.5 us
    reshape x16, local copies, waits for them, and re-layouts, shards(): allowed_rows = jnp.repeat(allowed, GQ, axis=0)  14.6 us
  transfers between devices with their start and end apart: 2, of which 1 were waited for; matrix products, arithmetic and copies ran while one was open for 1% of the time, Pallas kernels for 0%

commit v1 on v0

v1 whole, which is shorter than its diff:
```python
import functools
import math

import jax
import jax.numpy as jnp
import numpy as np
from jax import lax
from jax.experimental import pallas as pl
from jax.experimental.pallas import tpu as pltpu
from jax.sharding import PartitionSpec as P

HEADS = 64
KVH = 8
HD = 128
ROWS = 128
CTX = 1024
PAGE = 16
GQ = 8
KVW = 1024

ROPE_BASE = 500000.0
NEG_FILL = -1e30
LOW = -1e29
TINY = 1.2e-38
NO_LEVEL = -16000.0
LEVELS = 32767.0
SCALE = 1.0 / math.sqrt(HD)
EXP2_SCALE = SCALE * math.log2(math.e)
LANES = 256
KEYS = 256
DEPTH = 512
TAIL = 8
CONTRACT_FIRST = (((0,), (0,)), ((), ()))
CONTRACT_LAST = (((1,), (1,)), ((), ()))
PARAMS = pltpu.CompilerParams(vmem_limit_bytes=60 << 20)
SMALL_PARAMS = pltpu.CompilerParams(vmem_limit_bytes=40 << 20)


def small_cost(flops):
    return pl.CostEstimate(flops=flops, bytes_accessed=1 << 16, transcendentals=0)


def inverse_frequencies():
    steps = np.arange(HD // 2, dtype=np.float32) * np.float32(-2.0 * math.log(ROPE_BASE) / HD)
    return np.exp(steps.astype(np.float64)).astype(np.float32)


def rope_tables(positions):
    inverse = jnp.asarray(np.tile(inverse_frequencies(), 2))
    sign = np.repeat(np.array([-1.0, 1.0], np.float32), HD // 2)
    angles = positions.astype(jnp.float32)[:, None] * inverse[None, :]
    return jnp.cos(angles), jnp.sin(angles) * sign[None, :]


def rotated(values, cosine, signed_sine):
    return values * cosine + pltpu.roll(values, HD // 2, 1) * signed_sine


def project_kernel(ranks, rank_ref, x_ref, w_ref, page_ref, owner_ref, cache_ref, *refs):
    out_refs, page_refs, there_ref = refs[:ranks], refs[ranks:2 * ranks], refs[2 * ranks]
    weight, total, sems, counts, page_sems = refs[2 * ranks + 1:]
    entries = page_ref.shape[0]
    share = out_refs[0].shape[0]
    chunks = weight.shape[0]

    def weight_copy(j):
        rows = pl.ds(j * weight.shape[1], weight.shape[1])
        return pltpu.make_async_copy(w_ref.at[rows, :], weight.at[j], sems.at[j])

    def page_rows(e):
        return pl.ds(pl.multiple_of(page_ref[e] * PAGE, PAGE), PAGE)

    def kept(e, slot):
        return pltpu.make_async_copy(cache_ref.at[page_rows(e), :], page_refs[0].at[slot], page_sems.at[e])

    def near(e, k, slot):
        source = cache_ref.at[page_rows(e), pl.ds(0, KVW)]
        return pltpu.make_async_copy(source, page_refs[k].at[slot], page_sems.at[e])

    def far(e, k, slot):
        source = cache_ref.at[page_rows(e), pl.ds(KVW, KVW)]
        return pltpu.make_async_copy(source, there_ref.at[k - 1, slot], page_sems.at[e])

    for j in range(chunks):
        weight_copy(j).start()
    for ref in [*page_refs, there_ref]:
        ref[...] = jnp.zeros_like(ref)
    for r in range(ranks):
        counts[r] = 0

    def begin(e, carry):
        owner = owner_ref[e]
        slot = counts[owner]
        counts[owner] = slot + 1
        place = lax.rem(owner - rank_ref[0] + ranks, ranks)

        @pl.when(place == 0)
        def _():
            kept(e, slot).start()

        for k in range(1, ranks):
            @pl.when(place == k)
            def _():
                near(e, k, slot).start()
                far(e, k, slot).start()
        return carry

    lax.fori_loop(0, entries, begin, 0)
    for j in range(chunks):
        weight_copy(j).wait()
        depth = weight.shape[1]
        part = jnp.dot(
            x_ref[:, j * depth:(j + 1) * depth], weight[j], preferred_element_type=jnp.float32
        )
        if j:
            part = part + total[...]
        total[...] = part
    for k in range(ranks):
        dest = lax.rem(rank_ref[0] + k, ranks)
        out_refs[k][...] = total[pl.ds(pl.multiple_of(dest * share, share), share), :]

    def end(e, carry):
        kept(e, 0).wait()
        return carry

    lax.fori_loop(0, entries, end, 0)


def project(me, x, weight, page_list, owner_ids, cache, ranks):
    share = ROWS // ranks
    depth = weight.shape[0]
    block = min(depth, DEPTH)
    entries = page_list.shape[0]
    slots = 2 * entries // ranks
    smem = pl.BlockSpec(memory_space=pltpu.SMEM)
    vmem = pl.BlockSpec(memory_space=pltpu.VMEM)
    anywhere = pl.BlockSpec(memory_space=pl.ANY)
    out_shape = [jax.ShapeDtypeStruct((share, 2 * KVW), jnp.float32)] * ranks
    out_shape += [jax.ShapeDtypeStruct((slots, PAGE, 2 * KVW), jnp.bfloat16)]
    out_shape += [jax.ShapeDtypeStruct((slots, PAGE, KVW), jnp.bfloat16)] * (ranks - 1)
    out_shape += [jax.ShapeDtypeStruct((ranks - 1, slots, PAGE, KVW), jnp.bfloat16)]
    out = pl.pallas_call(
        functools.partial(project_kernel, ranks),
        in_specs=[smem, vmem, anywhere, smem, smem, anywhere],
        out_specs=[vmem] * len(out_shape),
        out_shape=out_shape,
        scratch_shapes=[
            pltpu.VMEM((depth // block, block, 2 * KVW), jnp.bfloat16),
            pltpu.VMEM((ROWS, 2 * KVW), jnp.float32),
            pltpu.SemaphoreType.DMA((depth // block,)),
            pltpu.SMEM((ranks,), jnp.int32),
            pltpu.SemaphoreType.DMA((entries,)),
        ],
        compiler_params=PARAMS,
        cost_estimate=small_cost(1 << 20),
        name="project",
    )(me.reshape(1), x, weight, page_list, owner_ids, cache)
    return out[:ranks], out[ranks:2 * ranks], out[2 * ranks]


def prepare_kernel(q_ref, k_ref, scale_ref, qc_ref, qs_ref, kc_ref, ks_ref, q_out, k_out):
    for g in range(GQ):
        q = rotated(q_ref[:, g * HD:(g + 1) * HD].astype(jnp.float32), qc_ref[...], qs_ref[...])
        q_out[g * ROWS:(g + 1) * ROWS, :] = q.astype(jnp.bfloat16)
    for h in range(KVH):
        columns = slice(h * HD, (h + 1) * HD)
        key = k_ref[:, columns].astype(jnp.float32) * scale_ref[:, columns]
        k_out[h] = rotated(key, kc_ref[...], ks_ref[...]).astype(jnp.bfloat16)


def prepare(queries, cache, key_scale, q_tables, k_tables):
    fixed = lambda j: (0, 0)
    rows = CTX // KVH
    return pl.pallas_call(
        prepare_kernel,
        grid=(KVH,),
        in_specs=[
            pl.BlockSpec((ROWS, GQ * HD), lambda j: (0, j)),
            pl.BlockSpec((rows, KVW), lambda j: (j, 0)),
            pl.BlockSpec((1, KVW), fixed),
            pl.BlockSpec((ROWS, HD), fixed),
            pl.BlockSpec((ROWS, HD), fixed),
            pl.BlockSpec((rows, HD), lambda j: (j, 0)),
            pl.BlockSpec((rows, HD), lambda j: (j, 0)),
        ],
        out_specs=[
            pl.BlockSpec((GQ * ROWS, HD), lambda j: (j, 0)),
            pl.BlockSpec((KVH, rows, HD), lambda j: (0, j, 0)),
        ],
        out_shape=[
            jax.ShapeDtypeStruct((HEADS * ROWS, HD), jnp.bfloat16),
            jax.ShapeDtypeStruct((KVH, CTX, HD), jnp.bfloat16),
        ],
        compiler_params=PARAMS,
        cost_estimate=small_cost(1 << 20),
        name="prepare",
    )(queries, cache, key_scale, *q_tables, *k_tables)


def split_level(level):
    doubled = jnp.maximum(level, NO_LEVEL) * 2.0
    high = jnp.floor(doubled)
    return [high, (doubled - high) * 65536.0 - 32768.0]


def joined_level(high, low):
    return (high + (low + 32768.0) * (1.0 / 65536.0)) * 0.5


def code_into(out_ref, lanes, top, total, numerator):
    largest = jnp.maximum(jnp.max(jnp.abs(numerator), axis=0, keepdims=True), TINY)
    coded = jnp.round(numerator * (1.0 / largest) * LEVELS)
    out_ref[:HD, lanes] = coded.astype(jnp.int32).astype(jnp.int16)
    tail = split_level(top + jnp.log2(largest)) + split_level(top + jnp.log2(total))
    tail = jnp.concatenate(tail + [jnp.zeros((TAIL - 4, top.shape[1]), jnp.float32)], axis=0)
    out_ref[HD:, lanes] = tail.astype(jnp.int32).astype(jnp.int16)


def decode(ref, lanes):
    tail = ref[HD:, lanes].astype(jnp.int32).astype(jnp.float32)
    values = ref[:HD, lanes].astype(jnp.int32).astype(jnp.float32)
    return joined_level(tail[0:1], tail[1:2]), joined_level(tail[2:3], tail[3:4]), values


def merged(top, total, numerator, parts):
    peak = functools.reduce(jnp.maximum, [p[1] for p in parts], top)
    if total is not None:
        factor = jnp.exp2(top - peak)
        total, numerator = total * factor, numerator * factor
    for level, weight, values in parts:
        more = jnp.exp2(weight - peak)
        part = values * (jnp.exp2(level - peak) * (1.0 / LEVELS))
        total = more if total is None else total + more
        numerator = part if numerator is None else numerator + part
    return peak, total, numerator


def fold_rows(values, combine):
    rows, cols = values.shape
    return combine(values.reshape(rows // 8, 8, cols), axis=0)


def attend_kernel(ranks, is_open, info, q_ref, k_ref, v_ref, qc_ref, qs_ref, *refs):
    fk_refs, refs = refs[:ranks], refs[ranks:]
    fv_refs, refs = refs[:ranks], refs[ranks:]
    if is_open:
        num_ref, stat_ref, scores = refs
    else:
        out_ref, scores = refs
    fresh_value = sum(ref[...] for ref in fv_refs).astype(jnp.bfloat16)
    rank = info[1]
    share = fk_refs[0].shape[0]
    valid = info[0] - rank * CTX
    first = pl.multiple_of(rank * share, share)
    fresh_key = sum(ref[...] for ref in fk_refs).astype(jnp.bfloat16).astype(jnp.float32)
    fresh_key = rotated(
        fresh_key, qc_ref[pl.ds(first, share), :], qs_ref[pl.ds(first, share), :]
    ).astype(jnp.bfloat16)
    cols = q_ref.shape[0]
    queries = q_ref[...]
    key_id = first + lax.broadcasted_iota(jnp.int32, (share, cols), 0)
    row_id = lax.broadcasted_iota(jnp.int32, (share, cols), 1) % ROWS
    fs = lax.dot_general(fresh_key, queries, CONTRACT_LAST, preferred_element_type=jnp.float32)
    fs = jnp.where(key_id <= row_id, fs, NEG_FILL)
    peak = fold_rows(fs, jnp.max)
    for t in range(CTX // KEYS):
        rows = slice(t * KEYS, (t + 1) * KEYS)
        s = lax.dot_general(
            k_ref[0, rows, :], queries, CONTRACT_LAST, preferred_element_type=jnp.float32
        )
        position = t * KEYS + lax.broadcasted_iota(jnp.int32, (KEYS, cols), 0)
        s = jnp.where(position < valid, s, NEG_FILL)
        scores[rows, :] = s
        peak = jnp.maximum(peak, fold_rows(s, jnp.max))
    peak = jnp.max(peak, axis=0, keepdims=True)
    base = jnp.maximum(peak, LOW)
    w = jnp.exp((fs - base) * SCALE)
    total = fold_rows(w, jnp.sum)
    numerator = lax.dot_general(
        fresh_value, w.astype(jnp.bfloat16), CONTRACT_FIRST, preferred_element_type=jnp.float32
    )
    for t in range(CTX // KEYS):
        rows = slice(t * KEYS, (t + 1) * KEYS)
        w = jnp.exp((scores[rows, :] - base) * SCALE)
        total = total + fold_rows(w, jnp.sum)
        numerator = numerator + lax.dot_general(
            v_ref[rows, :], w.astype(jnp.bfloat16), CONTRACT_FIRST, preferred_element_type=jnp.float32
        )
    total = jnp.sum(total, axis=0, keepdims=True)
    top = jnp.maximum(peak * EXP2_SCALE, NO_LEVEL)
    if is_open:
        num_ref[0] = numerator
        stat_ref[0] = jnp.concatenate([top, total, jnp.zeros((6, cols), jnp.float32)], axis=0)
    else:
        code_into(out_ref, slice(0, cols), top, total, numerator)


def layout(ranks):
    heads_here = HEADS // ranks
    pieces = max(1, heads_here // GQ)
    heads = heads_here // pieces
    return pieces, heads, heads * ROWS, ROWS // ranks


def whole(j, s):
    return (0, 0)


def opened_specs(cols):
    place = lambda j, s: (j, 0, 0)
    return [pl.BlockSpec((1, HD, cols), place), pl.BlockSpec((1, 8, cols), place)]


def attend(info, queries, keys, cache, q_tables, fresh, ranks, is_open):
    _, _, cols, share = layout(ranks)
    steps = (info.shape[0] - 2) // 2
    if is_open:
        out_specs = opened_specs(cols)
        out_shape = [
            jax.ShapeDtypeStruct((steps, HD, cols), jnp.float32),
            jax.ShapeDtypeStruct((steps, 8, cols), jnp.float32),
        ]
    else:
        out_specs = pl.BlockSpec((HD + TAIL, cols), lambda j, s: (0, j))
        out_shape = jax.ShapeDtypeStruct((HD + TAIL, steps * cols), jnp.int16)
    return pl.pallas_call(
        functools.partial(attend_kernel, ranks, is_open),
        grid_spec=pltpu.PrefetchScalarGridSpec(
            num_scalar_prefetch=1,
            grid=(steps,),
            in_specs=[
                pl.BlockSpec((cols, HD), lambda j, s: (s[2 + 2 * j], 0)),
                pl.BlockSpec((1, CTX, HD), lambda j, s: (s[3 + 2 * j], 0, 0)),
                pl.BlockSpec((CTX, HD), lambda j, s: (0, KVH + s[3 + 2 * j])),
                pl.BlockSpec((ROWS, HD), whole),
                pl.BlockSpec((ROWS, HD), whole),
            ]
            + [pl.BlockSpec((share, HD), lambda j, s: (0, s[3 + 2 * j]))] * ranks
            + [pl.BlockSpec((share, HD), lambda j, s: (0, KVH + s[3 + 2 * j]))] * ranks,
            out_specs=out_specs,
            scratch_shapes=[pltpu.VMEM((CTX, cols), jnp.float32)],
        ),
        out_shape=out_shape,
        compiler_params=PARAMS,
        cost_estimate=small_cost(1 << 31),
        name="attend_open" if is_open else "attend",
    )(info, queries, keys, cache, *q_tables, *fresh, *fresh)


def close_kernel(is_last, num_ref, stat_ref, *refs):
    in_refs, out_ref = refs[:-1], refs[-1]
    for b in range(out_ref.shape[1] // LANES):
        lanes = slice(b * LANES, (b + 1) * LANES)
        top, total, numerator = stat_ref[0, 0:1, lanes], stat_ref[0, 1:2, lanes], num_ref[0, :, lanes]
        parts = [decode(ref, lanes) for ref in in_refs]
        top, total, numerator = merged(top, total, numerator, parts)
        if not is_last:
            code_into(out_ref, lanes, top, total, numerator)
            continue
        numerator = numerator / total
        for h in range(LANES // ROWS):
            column = b * LANES + h * HD
            out_ref[:, column:column + HD] = (
                numerator[:, h * ROWS:(h + 1) * ROWS].T.astype(jnp.bfloat16)
            )


def close(opened, received, ranks, is_last=False):
    pieces, _, cols, _ = layout(ranks)
    rows, kind = (ROWS, jnp.bfloat16) if is_last else (HD + TAIL, jnp.int16)
    place = lambda j: (j, 0, 0)
    return pl.pallas_call(
        functools.partial(close_kernel, is_last),
        grid=(pieces,),
        in_specs=[pl.BlockSpec((1, HD, cols), place), pl.BlockSpec((1, 8, cols), place)]
        + [pl.BlockSpec((HD + TAIL, cols), lambda j: (0, j))] * len(received),
        out_specs=pl.BlockSpec((rows, cols), lambda j: (0, j)),
        out_shape=jax.ShapeDtypeStruct((rows, pieces * cols), kind),
        compiler_params=PARAMS,
        cost_estimate=small_cost(1 << 18),
        name="finish" if is_last else "close",
    )(*opened, *received)


def choose_kernel(sec_ref, *refs):
    count = (len(refs) - 2) // 2
    near, there_ref, out_refs, sems = refs[:count], refs[count], refs[count + 1:-1], refs[-1]
    first = sec_ref[0] == 0
    for k in range(count):
        @pl.when(first)
        def _():
            pltpu.make_async_copy(near[k], out_refs[k], sems.at[k]).start()

        @pl.when(jnp.logical_not(first))
        def _():
            pltpu.make_async_copy(there_ref.at[k], out_refs[k], sems.at[k]).start()

    for k in range(count):
        pltpu.make_async_copy(near[k], out_refs[k], sems.at[k]).wait()


def choose(sec, near, there):
    count = len(near)
    return pl.pallas_call(
        choose_kernel,
        in_specs=[pl.BlockSpec(memory_space=pltpu.SMEM)] + [pl.BlockSpec(memory_space=pl.ANY)] * (count + 1),
        out_specs=[pl.BlockSpec(memory_space=pltpu.VMEM)] * count,
        out_shape=[jax.ShapeDtypeStruct(there.shape[1:], there.dtype)] * count,
        scratch_shapes=[pltpu.SemaphoreType.DMA((count,))],
        compiler_params=SMALL_PARAMS,
        cost_estimate=small_cost(1 << 18),
        name="choose",
    )(sec.reshape(1), *near, there)


def stack_kernel(*refs):
    out_ref, sems = refs[-2:]
    copies = [
        pltpu.make_async_copy(ref, out_ref.at[k], sems.at[k]) for k, ref in enumerate(refs[:-2])
    ]
    for c in copies:
        c.start()
    for c in copies:
        c.wait()


def stack(values):
    count = len(values)
    return pl.pallas_call(
        stack_kernel,
        in_specs=[pl.BlockSpec(memory_space=pl.ANY)] * count,
        out_specs=pl.BlockSpec(memory_space=pltpu.VMEM),
        out_shape=jax.ShapeDtypeStruct((count,) + values[0].shape, values[0].dtype),
        scratch_shapes=[pltpu.SemaphoreType.DMA((count,))],
        compiler_params=SMALL_PARAMS,
        cost_estimate=small_cost(1 << 32),
        name="stack",
    )(*values)


def arrange_kernel(place_ref, kept_ref, crossed_ref, routed_ref, out_ref):
    count = crossed_ref.shape[0]
    shift = lax.rem(place_ref[1] - pl.program_id(0) + count + 1, count + 1)
    second = place_ref[0] > 0

    @pl.when(jnp.logical_not(second))
    def _():
        out_ref[...] = jnp.zeros_like(out_ref)

    @pl.when(jnp.logical_and(second, shift == 0))
    def _():
        out_ref[...] = kept_ref[...]

    @pl.when(jnp.logical_and(second, shift > 0))
    def _():
        out_ref[:, :, :KVW] = crossed_ref[shift - 1]
        out_ref[:, :, KVW:] = routed_ref[shift - 1]


def arrange(place, kept, crossed, routed):
    ranks = crossed.shape[0] + 1
    slots = kept.shape[0]
    return pl.pallas_call(
        arrange_kernel,
        grid=(ranks,),
        in_specs=[
            pl.BlockSpec(memory_space=pltpu.SMEM),
            pl.BlockSpec(kept.shape, lambda j: (0, 0, 0)),
            pl.BlockSpec(crossed.shape, lambda j: (0, 0, 0, 0)),
            pl.BlockSpec(routed.shape, lambda j: (0, 0, 0, 0)),
        ],
        out_specs=pl.BlockSpec((slots, PAGE, 2 * KVW), lambda j: (j, 0, 0)),
        out_shape=jax.ShapeDtypeStruct((ranks * slots, PAGE, 2 * KVW), jnp.bfloat16),
        compiler_params=PARAMS,
        cost_estimate=small_cost(1 << 18),
        name="arrange",
    )(place, kept, crossed, routed)


def after(value, earlier):
    return lax.optimization_barrier((value, earlier))[0]


def shards(queries, kv_cache, key_scale, fresh_input, kv_weight, lengths, page_list, owners):
    ranks = lax.axis_size("rank")
    secs = lax.axis_size("sec")
    me = lax.axis_index("rank").astype(jnp.int32)
    sec = lax.axis_index("sec").astype(jnp.int32)
    cache = kv_cache[0]
    length = lengths[0, 0]
    pieces, heads, _, _ = layout(ranks)

    def shifted(value, k):
        return lax.ppermute(value, "rank", [(i, (i + k) % ranks) for i in range(ranks)])

    def swapped(value, bit):
        return lax.ppermute(value, "rank", [(i, i ^ bit) for i in range(ranks)])

    def handed_on(value):
        return lax.ppermute(value, "sec", [(i, (i + 1) % secs) for i in range(secs)])

    part, (kept, *near), there = project(
        me, fresh_input[0], kv_weight, page_list, owners[:, 0], cache, ranks
    )
    fresh = [part[0]] + [shifted(part[k], k) for k in range(1, ranks)]

    q_tables = rope_tables(after(length, part) + jnp.arange(ROWS, dtype=jnp.int32))
    k_tables = rope_tables(after(me, part) * CTX + jnp.arange(CTX, dtype=jnp.int32))
    there = handed_on(there)
    kept = handed_on(kept)
    q_rot, keys = prepare(queries[0], cache, key_scale[None, :], q_tables, k_tables)
    chosen = choose(sec, near, after(there, q_rot))
    fresh = after(fresh, chosen)

    def attend_to(code, earlier, is_open):
        info = [length, me]
        for p in range(pieces):
            chosen = (me ^ code) * pieces + p
            info += [chosen, chosen * heads // GQ]
        return attend(
            jnp.stack(info), after(q_rot, earlier), keys, cache, q_tables, fresh, ranks, is_open
        )

    taken = {code: [] for code in range(ranks)}

    def send(value, code, bit):
        taken[code ^ bit].append(swapped(value, bit))

    routed = [shifted(c, k + 1) for k, c in enumerate(chosen)]
    last = chosen
    for code in range(ranks - 1, 1, -2):
        last = attend_to(code, last, False)
        send(last, code, 1)
    merging = {}
    for code in range(ranks - 2, 0, -2):
        last = merging[code] = attend_to(code, (last, kept), True)
    last = attend_to(1, last, False)
    send(last, 1, 1)
    both = stack(after(routed, last))
    bit = 2
    while bit < ranks:
        for code in range(ranks - bit, 0, -2 * bit):
            last = close(after(merging[code], both), taken[code], ranks)
            send(last, code, bit)
        bit *= 2
    crossed = handed_on(both)
    own = attend_to(0, last, True)

    handed = arrange(jnp.stack([sec, me]), kept, crossed, both)[None]
    attended = close(own, taken[0], ranks, is_last=True)[None]
    return (attended, handed)


def solution(mesh):
    return jax.shard_map(
        shards,
        mesh=mesh,
        in_specs=(
            P(("sec", "grp"), None, None),
            P(("sec", "grp"), "rank", None),
            P(),
            P(("sec", "grp"), None, "rank"),
            P("rank", None),
            P(("sec", "grp"), None),
            P(("sec", "grp", "rank")),
            P(("sec", "grp", "rank"), None),
        ),
        out_specs=(P(("sec", "grp"), None, "rank"), P(("sec", "grp", "rank"), None, None, None)),
        check_vma=False,
    )
```

time: 526 us -> 106 us (0.20)
  blocking collectives: 197 us -> 0 us
  waiting for transfers between devices: 166 us -> 12.8 us
  Pallas kernels: 0 us -> 52.8 us
  local copies, waits for them, and re-layouts: 56.5 us -> 4.4 us
  matrix products: 43.2 us -> 0 us
  other arithmetic: 42.5 us -> 4.67 us
  starting transfers between devices: 3.57 us -> 29.8 us
  between operations: 15 us -> 1.47 us
    all_gather x1 -> x0, waiting for transfers between devices: 166 us -> none  [combined_all(): gathered = jax.tree.map(lambda a: lax.all_gather(a, axis), part)]
    all_to_all x1 -> x0, blocking collectives: 103 us -> none  [shards(): lax.all_to_all(outgoing, 'rank', split_axis=0, concat_axis=0, tiled=True)]
    pallas_call x0 -> x11, Pallas kernels: none -> 52.8 us  [the longest x4 29.8 us: attend(): pl.pallas_call(functools.partial(attend_kernel, ranks, is_open), grid_spe...]
    all_gather x2 -> x0, blocking collectives: 49 us -> none  [combined_all(): gathered = jax.tree.map(lambda a: lax.all_gather(a, axis), part)]
    psum x1 -> x0, blocking collectives: 45.1 us -> none  [shards(): lax.psum(jnp.dot(rows_in, kv_weight, preferred_element_type=jnp.float32),...]
    dot_general x17 -> x0, matrix products: 43.2 us -> none  [the longest x8 23.1 us: per_head(): jnp.dot(weights.astype(jnp.bfloat16), value_head, preferred_element_type=...]
    ppermute x1 -> x12, starting transfers between devices: 3.53 us -> 29.8 us  [the longest x6 23.6 us: shifted(): lax.ppermute(value, 'rank', [(i, (i + k) % ranks) for i in range(ranks)])]
    add x6 -> x0, other arithmetic: 24.2 us -> none  [the longest x3 24 us: combine_parts(): earlier[2] * first_factor[..., None] + latter[2] * second_factor[..., None]]
  transfers between devices with their start and end apart: 2 -> 12, of which waited for: 1 -> 2; matrix products, arithmetic and copies ran while one was open for 1% -> 7% of each run, Pallas kernels for 0% -> 41%
where the time goes in v1:
time: 106 us
  Pallas kernels  52.8 us (50%)
  starting transfers between devices  29.8 us (28%)
  waiting for transfers between devices  12.8 us (12%)
  other arithmetic  4.67 us (4%)
  local copies, waits for them, and re-layouts  4.4 us (4%)
  between operations  1.47 us (1%)
    pallas_call x4, Pallas kernels, attend(): pl.pallas_call(functools.partial(attend_kernel, ranks, is_open), grid_spe...  29.8 us
    ppermute x6, starting transfers between devices, shifted(): lax.ppermute(value, 'rank', [(i, (i + k) % ranks) for i in range(ranks)])  23.6 us
    pallas_call x1, Pallas kernels, prepare(): pl.pallas_call(prepare_kernel, grid=(KVH,), in_specs=[pl.BlockSpec((ROWS,...  7.45 us
    ppermute x3, waiting for transfers between devices, swapped(): return lax.ppermute(value, 'rank', [(i, i ^ bit) for i in range(ranks)])  7.26 us
    pallas_call x1, Pallas kernels, project(): pl.pallas_call(functools.partial(project_kernel, ranks), in_specs=[smem,...  7.03 us
    ppermute x3, waiting for transfers between devices, handed_on(): lax.ppermute(value, 'sec', [(i, (i + 1) % secs) for i in range(secs)])  5.47 us
    pallas_call x2, Pallas kernels, close(): pl.pallas_call(functools.partial(close_kernel, is_last), grid=(pieces,),...  4.91 us
    ppermute x3, starting transfers between devices, handed_on(): lax.ppermute(value, 'sec', [(i, (i + 1) % secs) for i in range(secs)])  4.16 us
  transfers between devices with their start and end apart: 12, of which 2 were waited for; matrix products, arithmetic and copies ran while one was open for 7% of the time, Pallas kernels for 41%

profile of v1, /device:TPU:0, one launch (start us, length us, event | category | flops | bytes accessed | tf_op | source)
XLA Modules:
  0.0 105.9 jit_solution(14029073086520857782)
XLA Ops:
  0.6 0.0 copy-start.11
  0.6 0.0 copy-start.12
  0.7 7.0 %project.1 = (f32[32,2048]{1,0:T(8,128)}, f32[32,2048]{1,0:T(8,128)}, f32[32,2048]{1,0:T(8,128)}, f32[32,2048]{1,0:T(8,128)}, bf16[8,16,2048]{2,1,0:T(8,128)(2,1...) custom-call(s32[1]{0:T(128)} %bitcast.1.rank_ref, ...), custom_call_target="tpu_custom_call" | custom-call | flops 1048576 | bytes 65536 | tf_op jit(solution)/shard_map/project/pallas_call | solution.py:142
  7.7 3.0 %collective-permute-start = (bf16[3,8,16,1024]{3,2,1,0:T(8,128)(2,1)}, bf16[3,8,16,1024]{3,2,1,0:T(8,128)(2,1)S(1)}, u32[]{:S(2)}, u32[]{:S(2)}) collective-permute-start(bf16[3,8,16,1024]{3,2,1,0:T(8,128)(2,1)} %get-tuple-element.46), channel_id=1, source_target_pairs={{0,16},{16,0},{1,17},{17,1},{2,18},{18,2},{3,19},{19,3},{4,20},{20... | collective-permute-start | bytes 2359304 | tf_op jit(solution)/shard_map/ppermute | solution.py:500
  10.7 1.6 %collective-permute-start.1 = (f32[32,2048]{1,0:T(8,128)}, f32[32,2048]{1,0:T(8,128)S(1)}, u32[]{:S(2)}, u32[]{:S(2)}) collective-permute-start(f32[32,2048]{1,0:T(8,128)} %get-tuple-element.37), channel_id=1, source_target_pairs={{0,1},{1,2},{2,3},{3,0},{4,5},{5,6},{6,7},{7,4},{8,9},{9,10},{10,1... | collective-permute-start | bytes 786440 | tf_op jit(solution)/shard_map/ppermute | solution.py:494
  12.3 2.6 %collective-permute-start.2 = (f32[32,2048]{1,0:T(8,128)}, f32[32,2048]{1,0:T(8,128)S(1)}, u32[]{:S(2)}, u32[]{:S(2)}) collective-permute-start(f32[32,2048]{1,0:T(8,128)} %get-tuple-element.38), channel_id=1, source_target_pairs={{0,2},{1,3},{2,0},{3,1},{4,6},{5,7},{6,4},{7,5},{8,10},{9,11},{10,... | collective-permute-start | bytes 786440 | tf_op jit(solution)/shard_map/ppermute | solution.py:494
  14.9 1.3 %collective-permute-start.3 = (f32[32,2048]{1,0:T(8,128)}, f32[32,2048]{1,0:T(8,128)S(1)}, u32[]{:S(2)}, u32[]{:S(2)}) collective-permute-start(f32[32,2048]{1,0:T(8,128)} %get-tuple-element.39), channel_id=1, source_target_pairs={{0,3},{1,0},{2,1},{3,2},{4,7},{5,4},{6,5},{7,6},{8,11},{9,8},{10,9... | collective-permute-start | bytes 786440 | tf_op jit(solution)/shard_map/ppermute | solution.py:494
  16.2 0.5 collective-permute-start.4
  17.4 0.0 copy-done.11
  17.4 0.0 copy-done.12
  17.4 1.0 fusion.1
  18.4 0.6 stack.82.info
  19.0 0.6 stack.87.info
  19.6 0.6 stack.92.info
  20.2 3.0 %fusion = (f32[1024,128]{1,0:T(8,128)}, f32[1024,128]{1,0:T(8,128)}) fusion(f32[128]{0:T(128)S(1)} %copy-done.11, f32[128]{0:T(128)S(1)} %copy-done.12, f32[1024]{0:T(1024)S(1)} %add_convert_fusion), kind=kLoop, calls=%fused_computation.2 | loop fusion | flops 262144 | bytes 1053696 | tf_op jit(solution)/shard_map/mul | solution.py:52
  23.3 0.0 copy-start.1
  23.3 0.0 copy-start.2
  23.3 0.0 copy-start.3
  23.3 7.4 %prepare.1 = (bf16[8192,128]{1,0:T(8,128)(2,1)}, bf16[8,1024,128]{2,1,0:T(8,128)(2,1)}) custom-call(bf16[128,8192]{1,0:T(8,128)(2,1)} %bitcast.38, bf16[1024,2048]{1,0:T(8,128)(2,1)} %bitcast.33, f32[1,1024]{1,0:T(1,128)} %bitcast.42, f32[128,128]{1,0:T(8,128)} %get-tuple-element.73.qc_ref, f32[128,128]{1,0:T(8,128)} %get-tuple-element.72.qs_ref, ...), custom_call_target="tpu_custom_call" | custom-call | flops 1048576 | bytes 65536 | tf_op jit(solution)/shard_map/prepare/pallas_call | solution.py:174
  30.7 0.0 collective-permute-done.refs_3_
  30.7 0.0 copy-done.1
  30.7 0.0 copy-done.2
  30.7 0.0 copy-done.3
  30.8 0.1 choose.1
  30.9 0.7 collective-permute-start.5
  31.6 0.0 collective-permute-done.1.refs_1_.refs_5_
  31.6 0.0 copy-start.4
  31.6 2.6 %collective-permute-start.6 = (bf16[8,16,1024]{2,1,0:T(8,128)(2,1)S(1)}, bf16[8,16,1024]{2,1,0:T(8,128)(2,1)S(1)}, u32[]{:S(2)}, u32[]{:S(2)}) collective-permute-start(bf16[8,16,1024]{2,1,0:T(8,128)(2,1)S(1)} %get-tuple-element.49), channel_id=1, source_target_pairs={{0,2},{1,3},{2,0},{3,1},{4,6},{5,7},{6,4},{7,5},{8,10},{9,11},{10,... | collective-permute-start | bytes 786440 | tf_op jit(solution)/shard_map/ppermute | solution.py:494
  34.2 0.0 collective-permute-done.2.refs_2_.refs_6_
  34.2 0.0 copy-start.5
  34.2 14.7 %collective-permute-start.7 = (bf16[8,16,1024]{2,1,0:T(8,128)(2,1)S(1)}, bf16[8,16,1024]{2,1,0:T(8,128)(2,1)S(1)}, u32[]{:S(2)}, u32[]{:S(2)}) collective-permute-start(bf16[8,16,1024]{2,1,0:T(8,128)(2,1)S(1)} %get-tuple-element.50), channel_id=1, source_target_pairs={{0,3},{1,0},{2,1},{3,2},{4,7},{5,4},{6,5},{7,6},{8,11},{9,8},{10,9... | collective-permute-start | bytes 786440 | tf_op jit(solution)/shard_map/ppermute | solution.py:494
  49.0 0.0 collective-permute-done.3.refs_3_.refs_7_
  49.0 0.0 copy-start.6
  49.0 0.0 copy-done.4
  49.0 0.0 copy-done.5
  49.0 0.7 copy-done.6
  49.7 7.5 %attend.2 = s16[136,2048]{1,0:T(8,128)(2,1)} custom-call(s32[6]{0:T(128)} %stack.87.info, bf16[8192,128]{1,0:T(8,128)(2,1)} %get-tuple-element.67.q_ref, bf16[8,1024,128]{2,1,0:T(8,128)(2,1)} %get-tuple-element.52.k_ref, bf16[1024,2048]{1,0:T(8,128)(2,1)} %bitcast.34, f32[128,128]{1,0:T(8,128)} %get-tuple-element.73.qc_ref, ...), custom_call_target="tpu_custom_call" | custom-call | flops 2147483648 | bytes 65536 | tf_op jit(solution)/shard_map/attend/pallas_call | solution.py:326
  57.1 0.4 collective-permute-start.8
  57.5 0.0 collective-permute-done.4.kept_ref
  57.5 7.4 %attend_open.2 = (f32[2,128,1024]{2,1,0:T(8,128)}, f32[2,8,1024]{2,1,0:T(8,128)}) custom-call(s32[6]{0:T(128)} %stack.82.info, bf16[8192,128]{1,0:T(8,128)(2,1)} %get-tuple-element.67.q_ref, bf16[8,1024,128]{2,1,0:T(8,128)(2,1)} %get-tuple-element.52.k_ref, bf16[1024,2048]{1,0:T(8,128)(2,1)} %bitcast.35, f32[128,128]{1,0:T(8,128)} %get-tuple-element.73.qc_ref, ...), custom_call_target="tpu_custom_call" | custom-call | flops 2147483648 | bytes 65536 | tf_op jit(solution)/shard_map/attend_open/pallas_call | solution.py:326
  65.0 0.0 copy-done.10
  65.0 7.5 %attend.3 = s16[136,2048]{1,0:T(8,128)(2,1)} custom-call(s32[6]{0:T(128)} %stack.92.info, bf16[8192,128]{1,0:T(8,128)(2,1)} %get-tuple-element.67.q_ref, bf16[8,1024,128]{2,1,0:T(8,128)(2,1)} %get-tuple-element.52.k_ref, bf16[1024,2048]{1,0:T(8,128)(2,1)} %bitcast.36, f32[128,128]{1,0:T(8,128)} %get-tuple-element.73.qc_ref, ...), custom_call_target="tpu_custom_call" | custom-call | flops 2147483648 | bytes 65536 | tf_op jit(solution)/shard_map/attend/pallas_call | solution.py:326
  72.5 0.0 collective-permute-done.5.refs_0_
  72.5 0.0 collective-permute-done.6.refs_1_
  72.5 0.0 collective-permute-done.7.refs_2_
  72.5 0.1 stack.94.routed_ref
  72.6 0.0 copy-start
  72.6 0.6 collective-permute-start.11
  73.2 0.3 copy-done.8
  73.6 1.7 %collective-permute-start.9 = (s16[136,2048]{1,0:T(8,128)(2,1)S(1)}, s16[136,2048]{1,0:T(8,128)(2,1)S(1)}, u32[]{:S(2)}, u32[]{:S(2)}) collective-permute-start(s16[136,2048]{1,0:T(8,128)(2,1)S(1)} %copy-done.8), channel_id=1, source_target_pairs={{0,1},{1,0},{2,3},{3,2},{4,5},{5,4},{6,7},{7,6},{8,9},{9,8},{10,11... | collective-permute-start | bytes 1671176 | tf_op jit(solution)/shard_map/ppermute | solution.py:497
  75.2 0.0 collective-permute-done.8.refs_0_
  75.2 2.4 %close.1 = s16[136,2048]{1,0:T(8,128)(2,1)} custom-call(f32[2,128,1024]{2,1,0:T(8,128)} %get-tuple-element.65.num_ref, f32[2,8,1024]{2,1,0:T(8,128)} %get-tuple-element.66.stat_ref, s16[136,2048]{1,0:T(8,128)(2,1)} %collective-permute-done.8.refs_0_), custom_call_target="tpu_custom_call" | custom-call | flops 262144 | bytes 65536 | tf_op jit(solution)/shard_map/close/pallas_call | solution.py:372
  77.6 0.0 collective-permute-start.10
  77.6 0.6 stack.77.info
  78.2 0.6 pad_add_fusion.place_ref
  78.9 7.4 %attend_open.3 = (f32[2,128,1024]{2,1,0:T(8,128)}, f32[2,8,1024]{2,1,0:T(8,128)}) custom-call(s32[6]{0:T(128)} %stack.77.info, bf16[8192,128]{1,0:T(8,128)(2,1)} %get-tuple-element.67.q_ref, bf16[8,1024,128]{2,1,0:T(8,128)(2,1)} %get-tuple-element.52.k_ref, bf16[1024,2048]{1,0:T(8,128)(2,1)} %bitcast.37, f32[128,128]{1,0:T(8,128)} %get-tuple-element.73.qc_ref, ...), custom_call_target="tpu_custom_call" | custom-call | flops 2147483648 | bytes 65536 | tf_op jit(solution)/shard_map/attend_open/pallas_call | solution.py:326
  86.3 0.0 copy-done
  86.3 5.5 %collective-permute-done.11.crossed_ref = bf16[3,8,16,1024]{3,2,1,0:T(8,128)(2,1)S(1)} collective-permute-done((bf16[3,8,16,1024]{3,2,1,0:T(8,128)(2,1)S(1)}, bf16[3,8,16,1024]{3,2,1,0:T(8,128)(2,1)S(1)}, u32[]{:S(2)}, u32[]{:S(2)}) %collective-permute-start.11) | collective-permute-done | bytes 786464 | tf_op jit(solution)/shard_map/ppermute | solution.py:500
  91.8 0.9 copy-done.7
  92.7 3.4 %arrange.1 = bf16[32,16,2048]{2,1,0:T(8,128)(2,1)} custom-call(s32[2]{0:T(128)} %pad_add_fusion.place_ref, bf16[8,16,2048]{2,1,0:T(8,128)(2,1)} %copy-done.10, bf16[3,8,16,1024]{3,2,1,0:T(8,128)(2,1)} %copy-done.7, bf16[3,8,16,1024]{3,2,1,0:T(8,128)(2,1)} %copy-done), custom_call_target="tpu_custom_call" | custom-call | flops 262144 | bytes 65536 | tf_op jit(solution)/shard_map/arrange/pallas_call | solution.py:463
  96.1 0.0 collective-permute-done.9.refs_0_
  96.1 7.3 %collective-permute-done.10.refs_1_ = s16[136,2048]{1,0:T(8,128)(2,1)} collective-permute-done((s16[136,2048]{1,0:T(8,128)(2,1)}, s16[136,2048]{1,0:T(8,128)(2,1)}, u32[]{:S(2)}, u32[]{:S(2)}) %collective-permute-start.10) | collective-permute-done | bytes 557088 | tf_op jit(solution)/shard_map/ppermute | solution.py:497
  103.3 0.0 copy-done.9
  103.4 2.6 %finish.1 = bf16[128,2048]{1,0:T(8,128)(2,1)} custom-call(f32[2,128,1024]{2,1,0:T(8,128)} %get-tuple-element.68.num_ref, f32[2,8,1024]{2,1,0:T(8,128)} %get-tuple-element.69.stat_ref, s16[136,2048]{1,0:T(8,128)(2,1)} %copy-done.9, s16[136,2048]{1,0:T(8,128)(2,1)} %collective-permute-done.10.refs_1_), custom_call_target="tpu_custom_call" | custom-call | flops 262144 | bytes 65536 | tf_op jit(solution)/shard_map/finish/pallas_call | solution.py:372
  (6 shorter events, 0.0 us)
Async XLA Ops:
  0.6 16.8 %copy-start.11 = (f32[128]{0:T(128)S(1)}, f32[128]{0:T(128)}, u32[]{:S(2)}) copy-start(f32[128]{0:T(128)} %constant.99) | copy-start | bytes 1540
  0.6 16.8 %copy-start.12 = (f32[128]{0:T(128)S(1)}, f32[128]{0:T(128)}, u32[]{:S(2)}) copy-start(f32[128]{0:T(128)} %constant.91.clone) | copy-start | bytes 1540
  7.7 23.0 %collective-permute-start = (bf16[3,8,16,1024]{3,2,1,0:T(8,128)(2,1)}, bf16[3,8,16,1024]{3,2,1,0:T(8,128)(2,1)S(1)}, u32[]{:S(2)}, u32[]{:S(2)}) collective-permute-start(bf16[3,8,16,1024]{3,2,1,0:T(8,128)(2,1)} %get-tuple-element.46), channel_id=1, source_target_pairs={{0,16},{16,0},{1,17},{17,1},{2,18},{18,2},{3,19},{19,3},{4,20},{20... | collective-permute-start | bytes 2359304 | tf_op jit(solution)/shard_map/ppermute | solution.py:500
  10.7 20.9 %collective-permute-start.1 = (f32[32,2048]{1,0:T(8,128)}, f32[32,2048]{1,0:T(8,128)S(1)}, u32[]{:S(2)}, u32[]{:S(2)}) collective-permute-start(f32[32,2048]{1,0:T(8,128)} %get-tuple-element.37), channel_id=1, source_target_pairs={{0,1},{1,2},{2,3},{3,0},{4,5},{5,6},{6,7},{7,4},{8,9},{9,10},{10,1... | collective-permute-start | bytes 786440 | tf_op jit(solution)/shard_map/ppermute | solution.py:494
  12.3 21.9 %collective-permute-start.2 = (f32[32,2048]{1,0:T(8,128)}, f32[32,2048]{1,0:T(8,128)S(1)}, u32[]{:S(2)}, u32[]{:S(2)}) collective-permute-start(f32[32,2048]{1,0:T(8,128)} %get-tuple-element.38), channel_id=1, source_target_pairs={{0,2},{1,3},{2,0},{3,1},{4,6},{5,7},{6,4},{7,5},{8,10},{9,11},{10,... | collective-permute-start | bytes 786440 | tf_op jit(solution)/shard_map/ppermute | solution.py:494
  14.9 34.1 %collective-permute-start.3 = (f32[32,2048]{1,0:T(8,128)}, f32[32,2048]{1,0:T(8,128)S(1)}, u32[]{:S(2)}, u32[]{:S(2)}) collective-permute-start(f32[32,2048]{1,0:T(8,128)} %get-tuple-element.39), channel_id=1, source_target_pairs={{0,3},{1,0},{2,1},{3,2},{4,7},{5,4},{6,5},{7,6},{8,11},{9,8},{10,9... | collective-permute-start | bytes 786440 | tf_op jit(solution)/shard_map/ppermute | solution.py:494
  16.2 41.3 %collective-permute-start.4 = (bf16[8,16,2048]{2,1,0:T(8,128)(2,1)}, bf16[8,16,2048]{2,1,0:T(8,128)(2,1)S(1)}, u32[]{:S(2)}, u32[]{:S(2)}) collective-permute-start(bf16[8,16,2048]{2,1,0:T(8,128)(2,1)} %get-tuple-element.57), channel_id=1, source_target_pairs={{0,16},{16,0},{1,17},{17,1},{2,18},{18,2},{3,19},{19,3},{4,20},{20... | collective-permute-start | bytes 1572872 | tf_op jit(solution)/shard_map/ppermute | solution.py:500
  23.3 7.5 %copy-start.1 = (bf16[8,16,1024]{2,1,0:T(8,128)(2,1)S(1)}, bf16[8,16,1024]{2,1,0:T(8,128)(2,1)}, u32[]{:S(2)}) copy-start(bf16[8,16,1024]{2,1,0:T(8,128)(2,1)} %get-tuple-element.43.refs_0_) | copy-start | bytes 786436
  23.3 7.5 %copy-start.2 = (bf16[8,16,1024]{2,1,0:T(8,128)(2,1)S(1)}, bf16[8,16,1024]{2,1,0:T(8,128)(2,1)}, u32[]{:S(2)}) copy-start(bf16[8,16,1024]{2,1,0:T(8,128)(2,1)} %get-tuple-element.44.refs_1_) | copy-start | bytes 786436
  23.3 7.5 %copy-start.3 = (bf16[8,16,1024]{2,1,0:T(8,128)(2,1)S(1)}, bf16[8,16,1024]{2,1,0:T(8,128)(2,1)}, u32[]{:S(2)}) copy-start(bf16[8,16,1024]{2,1,0:T(8,128)(2,1)} %get-tuple-element.45.refs_2_) | copy-start | bytes 786436
  30.9 41.6 %collective-permute-start.5 = (bf16[8,16,1024]{2,1,0:T(8,128)(2,1)S(1)}, bf16[8,16,1024]{2,1,0:T(8,128)(2,1)S(1)}, u32[]{:S(2)}, u32[]{:S(2)}) collective-permute-start(bf16[8,16,1024]{2,1,0:T(8,128)(2,1)S(1)} %get-tuple-element.48), channel_id=1, source_target_pairs={{0,1},{1,2},{2,3},{3,0},{4,5},{5,6},{6,7},{7,4},{8,9},{9,10},{10,1... | collective-permute-start | bytes 786440 | tf_op jit(solution)/shard_map/ppermute | solution.py:494
  31.6 17.4 %copy-start.4 = (f32[32,2048]{1,0:T(8,128)}, f32[32,2048]{1,0:T(8,128)S(1)}, u32[]{:S(2)}) copy-start(f32[32,2048]{1,0:T(8,128)S(1)} %collective-permute-done.1.refs_1_.refs_5_) | copy-start | bytes 786436
  31.6 40.9 %collective-permute-start.6 = (bf16[8,16,1024]{2,1,0:T(8,128)(2,1)S(1)}, bf16[8,16,1024]{2,1,0:T(8,128)(2,1)S(1)}, u32[]{:S(2)}, u32[]{:S(2)}) collective-permute-start(bf16[8,16,1024]{2,1,0:T(8,128)(2,1)S(1)} %get-tuple-element.49), channel_id=1, source_target_pairs={{0,2},{1,3},{2,0},{3,1},{4,6},{5,7},{6,4},{7,5},{8,10},{9,11},{10,... | collective-permute-start | bytes 786440 | tf_op jit(solution)/shard_map/ppermute | solution.py:494
  34.2 14.8 %copy-start.5 = (f32[32,2048]{1,0:T(8,128)}, f32[32,2048]{1,0:T(8,128)S(1)}, u32[]{:S(2)}) copy-start(f32[32,2048]{1,0:T(8,128)S(1)} %collective-permute-done.2.refs_2_.refs_6_) | copy-start | bytes 786436
  34.2 38.3 %collective-permute-start.7 = (bf16[8,16,1024]{2,1,0:T(8,128)(2,1)S(1)}, bf16[8,16,1024]{2,1,0:T(8,128)(2,1)S(1)}, u32[]{:S(2)}, u32[]{:S(2)}) collective-permute-start(bf16[8,16,1024]{2,1,0:T(8,128)(2,1)S(1)} %get-tuple-element.50), channel_id=1, source_target_pairs={{0,3},{1,0},{2,1},{3,2},{4,7},{5,4},{6,5},{7,6},{8,11},{9,8},{10,9... | collective-permute-start | bytes 786440 | tf_op jit(solution)/shard_map/ppermute | solution.py:494
  49.0 0.7 copy-start.6
  57.1 18.1 %collective-permute-start.8 = (s16[136,2048]{1,0:T(8,128)(2,1)}, s16[136,2048]{1,0:T(8,128)(2,1)}, u32[]{:S(2)}, u32[]{:S(2)}) collective-permute-start(s16[136,2048]{1,0:T(8,128)(2,1)} %attend.2), channel_id=1, source_target_pairs={{0,1},{1,0},{2,3},{3,2},{4,5},{5,4},{6,7},{7,6},{8,9},{9,8},{10,11... | collective-permute-start | bytes 1671176 | tf_op jit(solution)/shard_map/ppermute | solution.py:497
  57.5 7.4 %copy-start.10 = (bf16[8,16,2048]{2,1,0:T(8,128)(2,1)}, bf16[8,16,2048]{2,1,0:T(8,128)(2,1)S(1)}, u32[]{:S(2)}) copy-start(bf16[8,16,2048]{2,1,0:T(8,128)(2,1)S(1)} %collective-permute-done.4.kept_ref) | copy-start | bytes 1572868
  72.5 1.1 %copy-start.8 = (s16[136,2048]{1,0:T(8,128)(2,1)S(1)}, s16[136,2048]{1,0:T(8,128)(2,1)}, u32[]{:S(2)}) copy-start(s16[136,2048]{1,0:T(8,128)(2,1)} %attend.3) | copy-start | bytes 1671172
  72.6 13.7 %copy-start = (bf16[3,8,16,1024]{3,2,1,0:T(8,128)(2,1)}, bf16[3,8,16,1024]{3,2,1,0:T(8,128)(2,1)S(1)}, u32[]{:S(2)}) copy-start(bf16[3,8,16,1024]{3,2,1,0:T(8,128)(2,1)S(1)} %stack.94.routed_ref) | copy-start | bytes 2359300
  72.6 19.2 %collective-permute-start.11 = (bf16[3,8,16,1024]{3,2,1,0:T(8,128)(2,1)S(1)}, bf16[3,8,16,1024]{3,2,1,0:T(8,128)(2,1)S(1)}, u32[]{:S(2)}, u32[]{:S(2)}) collective-permute-start(bf16[3,8,16,1024]{3,2,1,0:T(8,128)(2,1)S(1)} %stack.94.routed_ref), channel_id=1, source_target_pairs={{0,16},{16,0},{1,17},{17,1},{2,18},{18,2},{3,19},{19,3},{4,20},{20... | collective-permute-start | bytes 2359304 | tf_op jit(solution)/shard_map/ppermute | solution.py:500
  73.6 22.5 %collective-permute-start.9 = (s16[136,2048]{1,0:T(8,128)(2,1)S(1)}, s16[136,2048]{1,0:T(8,128)(2,1)S(1)}, u32[]{:S(2)}, u32[]{:S(2)}) collective-permute-start(s16[136,2048]{1,0:T(8,128)(2,1)S(1)} %copy-done.8), channel_id=1, source_target_pairs={{0,1},{1,0},{2,3},{3,2},{4,5},{5,4},{6,7},{7,6},{8,9},{9,8},{10,11... | collective-permute-start | bytes 1671176 | tf_op jit(solution)/shard_map/ppermute | solution.py:497
  77.6 25.7 %collective-permute-start.10 = (s16[136,2048]{1,0:T(8,128)(2,1)}, s16[136,2048]{1,0:T(8,128)(2,1)}, u32[]{:S(2)}, u32[]{:S(2)}) collective-permute-start(s16[136,2048]{1,0:T(8,128)(2,1)} %close.1), channel_id=1, source_target_pairs={{0,2},{1,3},{2,0},{3,1},{4,6},{5,7},{6,4},{7,5},{8,10},{9,11},{10,... | collective-permute-start | bytes 1671176 | tf_op jit(solution)/shard_map/ppermute | solution.py:497
  91.8 0.9 copy-start.7
  96.1 7.3 %copy-start.9 = (s16[136,2048]{1,0:T(8,128)(2,1)}, s16[136,2048]{1,0:T(8,128)(2,1)S(1)}, u32[]{:S(2)}) copy-start(s16[136,2048]{1,0:T(8,128)(2,1)S(1)} %collective-permute-done.9.refs_0_) | copy-start | bytes 1671172

commit v2 on v1

--- a/solution.py
+++ b/solution.py
@@ -240,22 +240,44 @@
     return combine(values.reshape(rows // 8, 8, cols), axis=0)
 
 
-def attend_kernel(ranks, is_open, info, q_ref, k_ref, v_ref, qc_ref, qs_ref, *refs):
-    fk_refs, refs = refs[:ranks], refs[ranks:]
-    fv_refs, refs = refs[:ranks], refs[ranks:]
+def gather_kernel(ranks, info, qc_ref, qs_ref, *refs):
+    key_out, value_out = refs[ranks:]
+    share = refs[0].shape[0]
+    mine = pl.ds(pl.multiple_of(info[1] * share, share), share)
+    cosine, signed_sine = qc_ref[mine, :], qs_ref[mine, :]
+    for h in range(KVH):
+        columns = slice(h * HD, (h + 1) * HD)
+        key = sum(ref[:, columns] for ref in refs[:ranks])
+        key = key.astype(jnp.bfloat16).astype(jnp.float32)
+        key_out[h] = rotated(key, cosine, signed_sine).astype(jnp.bfloat16)
+        columns = slice(KVW + h * HD, KVW + (h + 1) * HD)
+        value_out[h] = sum(ref[:, columns] for ref in refs[:ranks]).astype(jnp.bfloat16)
+
+
+def gather(info, q_tables, fresh):
+    share = fresh[0].shape[0]
+    vmem = pl.BlockSpec(memory_space=pltpu.VMEM)
+    return pl.pallas_call(
+        functools.partial(gather_kernel, len(fresh)),
+        in_specs=[pl.BlockSpec(memory_space=pltpu.SMEM)] + [vmem] * (2 + len(fresh)),
+        out_specs=[vmem] * 2,
+        out_shape=[jax.ShapeDtypeStruct((KVH, share, HD), jnp.bfloat16)] * 2,
+        compiler_params=SMALL_PARAMS,
+        cost_estimate=small_cost(1 << 18),
+        name="gather",
+    )(info, *q_tables, *fresh)
+
+
+def attend_kernel(is_open, info, q_ref, k_ref, v_ref, fk_ref, fv_ref, *refs):
     if is_open:
         num_ref, stat_ref, scores = refs
     else:
         out_ref, scores = refs
-    fresh_value = sum(ref[...] for ref in fv_refs).astype(jnp.bfloat16)
     rank = info[1]
-    share = fk_refs[0].shape[0]
+    share = fk_ref.shape[1]
     valid = info[0] - rank * CTX
-    first = pl.multiple_of(rank * share, share)
-    fresh_key = sum(ref[...] for ref in fk_refs).astype(jnp.bfloat16).astype(jnp.float32)
-    fresh_key = rotated(
-        fresh_key, qc_ref[pl.ds(first, share), :], qs_ref[pl.ds(first, share), :]
-    ).astype(jnp.bfloat16)
+    first = rank * share
+    fresh_key, fresh_value = fk_ref[0], fv_ref[0]
     cols = q_ref.shape[0]
     queries = q_ref[...]
     key_id = first + lax.broadcasted_iota(jnp.int32, (share, cols), 0)
@@ -311,32 +333,37 @@
     return [pl.BlockSpec((1, HD, cols), place), pl.BlockSpec((1, 8, cols), place)]
 
 
-def attend(info, queries, keys, cache, q_tables, fresh, ranks, is_open):
-    _, _, cols, share = layout(ranks)
-    steps = (info.shape[0] - 2) // 2
+def attend(info, code, queries, keys, cache, fresh, ranks, is_open):
+    pieces, heads, cols, share = layout(ranks)
+
+    def piece(j, s):
+        return (s[1] ^ code) * pieces + j
+
+    def key_head(j, s):
+        return piece(j, s) * heads // GQ
+
     if is_open:
         out_specs = opened_specs(cols)
         out_shape = [
-            jax.ShapeDtypeStruct((steps, HD, cols), jnp.float32),
-            jax.ShapeDtypeStruct((steps, 8, cols), jnp.float32),
+            jax.ShapeDtypeStruct((pieces, HD, cols), jnp.float32),
+            jax.ShapeDtypeStruct((pieces, 8, cols), jnp.float32),
         ]
     else:
         out_specs = pl.BlockSpec((HD + TAIL, cols), lambda j, s: (0, j))
-        out_shape = jax.ShapeDtypeStruct((HD + TAIL, steps * cols), jnp.int16)
-    return pl.pallas_call(
-        functools.partial(attend_kernel, ranks, is_open),
+        out_shape = jax.ShapeDtypeStruct((HD + TAIL, pieces * cols), jnp.int16)
+    own_head = lambda j, s: (key_head(j, s), 0, 0)
+    return pl.pallas_call(
+        functools.partial(attend_kernel, is_open),
         grid_spec=pltpu.PrefetchScalarGridSpec(
             num_scalar_prefetch=1,
-            grid=(steps,),
+            grid=(pieces,),
             in_specs=[
-                pl.BlockSpec((cols, HD), lambda j, s: (s[2 + 2 * j], 0)),
-                pl.BlockSpec((1, CTX, HD), lambda j, s: (s[3 + 2 * j], 0, 0)),
-                pl.BlockSpec((CTX, HD), lambda j, s: (0, KVH + s[3 + 2 * j])),
-                pl.BlockSpec((ROWS, HD), whole),
-                pl.BlockSpec((ROWS, HD), whole),
-            ]
-            + [pl.BlockSpec((share, HD), lambda j, s: (0, s[3 + 2 * j]))] * ranks
-            + [pl.BlockSpec((share, HD), lambda j, s: (0, KVH + s[3 + 2 * j]))] * ranks,
+                pl.BlockSpec((cols, HD), lambda j, s: (piece(j, s), 0)),
+                pl.BlockSpec((1, CTX, HD), own_head),
+                pl.BlockSpec((CTX, HD), lambda j, s: (0, KVH + key_head(j, s))),
+                pl.BlockSpec((1, share, HD), own_head),
+                pl.BlockSpec((1, share, HD), own_head),
+            ],
             out_specs=out_specs,
             scratch_shapes=[pltpu.VMEM((CTX, cols), jnp.float32)],
         ),
@@ -344,7 +371,7 @@
         compiler_params=PARAMS,
         cost_estimate=small_cost(1 << 31),
         name="attend_open" if is_open else "attend",
-    )(info, queries, keys, cache, *q_tables, *fresh, *fresh)
+    )(info, queries, keys, cache, *fresh)
 
 
 def close_kernel(is_last, num_ref, stat_ref, *refs):
@@ -510,23 +537,20 @@
     kept = handed_on(kept)
     q_rot, keys = prepare(queries[0], cache, key_scale[None, :], q_tables, k_tables)
     chosen = choose(sec, near, after(there, q_rot))
-    fresh = after(fresh, chosen)
+    arrived = after(fresh, chosen)
+    chosen = after(chosen, arrived)
+    routed = [shifted(c, k + 1) for k, c in enumerate(chosen)]
+    info = jnp.stack([length, me])
+    fresh = gather(info, q_tables, arrived)
 
     def attend_to(code, earlier, is_open):
-        info = [length, me]
-        for p in range(pieces):
-            chosen = (me ^ code) * pieces + p
-            info += [chosen, chosen * heads // GQ]
-        return attend(
-            jnp.stack(info), after(q_rot, earlier), keys, cache, q_tables, fresh, ranks, is_open
-        )
+        return attend(info, code, after(q_rot, earlier), keys, cache, fresh, ranks, is_open)
 
     taken = {code: [] for code in range(ranks)}
 
     def send(value, code, bit):
         taken[code ^ bit].append(swapped(value, bit))
 
-    routed = [shifted(c, k + 1) for k, c in enumerate(chosen)]
     last = chosen
     for code in range(ranks - 1, 1, -2):
         last = attend_to(code, last, False)

time: 106 us -> 112 us (1.057)
  waiting for transfers between devices: 12.8 us -> 28.8 us
  starting transfers between devices: 29.8 us -> 20.2 us
    ppermute x6, starting transfers between devices: 23.6 us -> 10.8 us  [shifted(): lax.ppermute(value, 'rank', [(i, (i + k) % ranks) for i in range(ranks)])]
    ppermute x3, waiting for transfers between devices: 5.47 us -> 15.5 us  [handed_on(): lax.ppermute(value, 'sec', [(i, (i + 1) % secs) for i in range(secs)])]
    ppermute x3, waiting for transfers between devices: 7.26 us -> 13.3 us  [swapped(): return lax.ppermute(value, 'rank', [(i, i ^ bit) for i in range(ranks)])]
    ppermute x3, starting transfers between devices: 2.09 us -> 5.75 us  [swapped(): return lax.ppermute(value, 'rank', [(i, i ^ bit) for i in range(ranks)])]
    another operation x4 -> x0, local copies, waits for them, and re-layouts: 2.41 us -> none  [attend_to(): jnp.stack(info)]
    unnamed x26 -> x34, local copies, waits for them, and re-layouts: 1.99 us -> 3.84 us
    pallas_call x4 -> x5, Pallas kernels: 29.8 us -> 29.3 us  [the longest x4 28.6 us: attend(): pl.pallas_call(functools.partial(attend_kernel, is_open), grid_spec=pltpu...]
  transfers between devices with their start and end apart: 12 -> 12, of which waited for: 2 -> 3; matrix products, arithmetic and copies ran while one was open for 7% -> 4% of each run, Pallas kernels for 41% -> 38%
where the time goes in v2:
time: 112 us; the launch traced here: 111 us
  Pallas kernels  52.3 us (47%)
  waiting for transfers between devices  28.8 us (26%)
  starting transfers between devices  20.2 us (18%)
  other arithmetic  4.77 us (4%)
  local copies, waits for them, and re-layouts  3.84 us (3%)
  between operations  1.51 us (1%)
    pallas_call x4, Pallas kernels, attend(): pl.pallas_call(functools.partial(attend_kernel, is_open), grid_spec=pltpu...  28.6 us
    ppermute x3, waiting for transfers between devices, handed_on(): lax.ppermute(value, 'sec', [(i, (i + 1) % secs) for i in range(secs)])  15.5 us
    ppermute x3, waiting for transfers between devices, swapped(): return lax.ppermute(value, 'rank', [(i, i ^ bit) for i in range(ranks)])  13.3 us
    ppermute x6, starting transfers between devices, shifted(): lax.ppermute(value, 'rank', [(i, (i + k) % ranks) for i in range(ranks)])  10.8 us
    pallas_call x1, Pallas kernels, prepare(): pl.pallas_call(prepare_kernel, grid=(KVH,), in_specs=[pl.BlockSpec((ROWS,...  7.5 us
    pallas_call x1, Pallas kernels, project(): pl.pallas_call(functools.partial(project_kernel, ranks), in_specs=[smem,...  7 us
    ppermute x3, starting transfers between devices, swapped(): return lax.ppermute(value, 'rank', [(i, i ^ bit) for i in range(ranks)])  5.75 us
    pallas_call x2, Pallas kernels, close(): pl.pallas_call(functools.partial(close_kernel, is_last), grid=(pieces,),...  4.92 us
  transfers between devices with their start and end apart: 12, of which 3 were waited for; matrix products, arithmetic and copies ran while one was open for 4% of the time, Pallas kernels for 38%

profile of v2, /device:TPU:0, one launch (start us, length us, event | category | flops | bytes accessed | tf_op | source)
XLA Modules:
  0.0 111.4 jit_solution(1541609154508106993)
XLA Ops:
  0.6 0.0 copy-start.15
  0.6 0.0 copy-start.16
  0.7 7.0 %project.1 = (f32[32,2048]{1,0:T(8,128)}, f32[32,2048]{1,0:T(8,128)}, f32[32,2048]{1,0:T(8,128)}, f32[32,2048]{1,0:T(8,128)}, bf16[8,16,2048]{2,1,0:T(8,128)(2,1...) custom-call(s32[1]{0:T(128)} %bitcast.1.rank_ref, ...), custom_call_target="tpu_custom_call" | custom-call | flops 1048576 | bytes 65536 | tf_op jit(solution)/shard_map/project/pallas_call | solution.py:142
  7.7 3.1 %collective-permute-start.1 = (f32[32,2048]{1,0:T(8,128)}, f32[32,2048]{1,0:T(8,128)S(1)}, u32[]{:S(2)}, u32[]{:S(2)}) collective-permute-start(f32[32,2048]{1,0:T(8,128)} %get-tuple-element.42), channel_id=1, source_target_pairs={{0,1},{1,2},{2,3},{3,0},{4,5},{5,6},{6,7},{7,4},{8,9},{9,10},{10,1... | collective-permute-start | bytes 786440 | tf_op jit(solution)/shard_map/ppermute | solution.py:521
  10.7 2.6 %collective-permute-start.2 = (f32[32,2048]{1,0:T(8,128)}, f32[32,2048]{1,0:T(8,128)S(1)}, u32[]{:S(2)}, u32[]{:S(2)}) collective-permute-start(f32[32,2048]{1,0:T(8,128)} %get-tuple-element.43), channel_id=1, source_target_pairs={{0,2},{1,3},{2,0},{3,1},{4,6},{5,7},{6,4},{7,5},{8,10},{9,11},{10,... | collective-permute-start | bytes 786440 | tf_op jit(solution)/shard_map/ppermute | solution.py:521
  13.3 1.3 %collective-permute-start.3 = (f32[32,2048]{1,0:T(8,128)}, f32[32,2048]{1,0:T(8,128)S(1)}, u32[]{:S(2)}, u32[]{:S(2)}) collective-permute-start(f32[32,2048]{1,0:T(8,128)} %get-tuple-element.44), channel_id=1, source_target_pairs={{0,3},{1,0},{2,1},{3,2},{4,7},{5,4},{6,5},{7,6},{8,11},{9,8},{10,9... | collective-permute-start | bytes 786440 | tf_op jit(solution)/shard_map/ppermute | solution.py:521
  14.7 1.5 %collective-permute-start.4 = (bf16[8,16,2048]{2,1,0:T(8,128)(2,1)}, bf16[8,16,2048]{2,1,0:T(8,128)(2,1)}, u32[]{:S(2)}, u32[]{:S(2)}) collective-permute-start(bf16[8,16,2048]{2,1,0:T(8,128)(2,1)} %get-tuple-element.67), channel_id=1, source_target_pairs={{0,16},{16,0},{1,17},{17,1},{2,18},{18,2},{3,19},{19,3},{4,20},{20... | collective-permute-start | bytes 1572872 | tf_op jit(solution)/shard_map/ppermute | solution.py:527
  16.2 0.5 collective-permute-start
  17.4 0.0 copy-done.15
  17.4 0.0 copy-done.16
  17.4 3.1 %fusion = (f32[1024,128]{1,0:T(8,128)}, f32[1024,128]{1,0:T(8,128)}) fusion(f32[128]{0:T(128)S(1)} %copy-done.15, f32[128]{0:T(128)S(1)} %copy-done.16, f32[1024]{0:T(1024)S(1)} %add_convert_fusion), kind=kLoop, calls=%fused_computation.2 | loop fusion | flops 262144 | bytes 1053696 | tf_op jit(solution)/shard_map/mul | solution.py:52
  20.5 1.0 fusion.1
  21.5 0.0 copy-start.4
  21.5 0.0 copy-start.5
  21.5 7.5 %prepare.1 = (bf16[8192,128]{1,0:T(8,128)(2,1)}, bf16[8,1024,128]{2,1,0:T(8,128)(2,1)}) custom-call(bf16[128,8192]{1,0:T(8,128)(2,1)} %bitcast.19, bf16[1024,2048]{1,0:T(8,128)(2,1)} %bitcast.14, f32[1,1024]{1,0:T(1,128)} %bitcast.23, f32[128,128]{1,0:T(8,128)} %get-tuple-element.83.qc_ref, f32[128,128]{1,0:T(8,128)} %get-tuple-element.82.qs_ref, ...), custom_call_target="tpu_custom_call" | custom-call | flops 1048576 | bytes 65536 | tf_op jit(solution)/shard_map/prepare/pallas_call | solution.py:174
  29.0 0.1 pad_add_fusion.info
  29.1 15.5 %collective-permute-done.refs_3_ = bf16[3,8,16,1024]{3,2,1,0:T(8,128)(2,1)S(1)} collective-permute-done((bf16[3,8,16,1024]{3,2,1,0:T(8,128)(2,1)}, bf16[3,8,16,1024]{3,2,1,0:T(8,128)(2,1)S(1)}, u32[]{:S(2)}, u32[]{:S(2)}) %collective-permute-start) | collective-permute-done | bytes 786464 | tf_op jit(solution)/shard_map/ppermute | solution.py:527
  44.6 0.0 copy-done.6
  44.6 0.0 copy-done.7
  44.6 0.0 copy-done.8
  44.6 0.1 choose.1
  44.7 0.0 collective-permute-done.1.refs_1_
  44.7 0.0 collective-permute-done.2.refs_2_
  44.7 0.0 collective-permute-done.3.refs_3_
  44.7 0.0 copy-done.3
  44.7 0.0 copy-done.4
  44.8 0.0 copy-done.5
  44.8 0.6 gather.1
  45.4 0.0 copy-start
  45.4 0.6 copy-done
  46.0 0.6 copy-done.1
  46.7 0.7 collective-permute-start.5
  47.4 0.3 collective-permute-start.6
  47.7 2.8 %collective-permute-start.7 = (bf16[8,16,1024]{2,1,0:T(8,128)(2,1)S(1)}, bf16[8,16,1024]{2,1,0:T(8,128)(2,1)S(1)}, u32[]{:S(2)}, u32[]{:S(2)}) collective-permute-start(bf16[8,16,1024]{2,1,0:T(8,128)(2,1)S(1)} %get-tuple-element.62), channel_id=1, source_target_pairs={{0,3},{1,0},{2,1},{3,2},{4,7},{5,4},{6,5},{7,6},{8,11},{9,8},{10,9... | collective-permute-start | bytes 786440 | tf_op jit(solution)/shard_map/ppermute | solution.py:521
  50.5 0.0 copy-done.9
  50.5 7.2 %attend.2 = s16[136,2048]{1,0:T(8,128)(2,1)} custom-call(s32[2]{0:T(128)} %copy-done.9, bf16[8192,128]{1,0:T(8,128)(2,1)} %get-tuple-element.77.q_ref, bf16[8,1024,128]{2,1,0:T(8,128)(2,1)} %get-tuple-element.64.k_ref, bf16[1024,2048]{1,0:T(8,128)(2,1)} %bitcast.15, bf16[8,32,128]{2,1,0:T(8,128)(2,1)} %copy-done, bf16[8,32,128]{2,1,0:T(8,128)(2,1)} %copy-done.1), custom_call_target="tpu_custom_call" | custom-call | flops 2147483648 | bytes 65536 | tf_op jit(solution)/shard_map/attend/pallas_call | solution.py:355
  57.7 0.5 collective-permute-start.8
  58.2 0.0 collective-permute-done.4.kept_ref
  58.2 7.1 %attend_open.2 = (f32[2,128,1024]{2,1,0:T(8,128)}, f32[2,8,1024]{2,1,0:T(8,128)}) custom-call(s32[2]{0:T(128)} %copy-done.9, bf16[8192,128]{1,0:T(8,128)(2,1)} %get-tuple-element.77.q_ref, bf16[8,1024,128]{2,1,0:T(8,128)(2,1)} %get-tuple-element.64.k_ref, bf16[1024,2048]{1,0:T(8,128)(2,1)} %bitcast.16, bf16[8,32,128]{2,1,0:T(8,128)(2,1)} %copy-done, ...), custom_call_target="tpu_custom_call" | custom-call | flops 2147483648 | bytes 65536 | tf_op jit(solution)/shard_map/attend_open/pallas_call | solution.py:355
  65.4 7.2 %attend.3 = s16[136,2048]{1,0:T(8,128)(2,1)} custom-call(s32[2]{0:T(128)} %copy-done.9, bf16[8192,128]{1,0:T(8,128)(2,1)} %get-tuple-element.77.q_ref, bf16[8,1024,128]{2,1,0:T(8,128)(2,1)} %get-tuple-element.64.k_ref, bf16[1024,2048]{1,0:T(8,128)(2,1)} %bitcast.17, bf16[8,32,128]{2,1,0:T(8,128)(2,1)} %copy-done, bf16[8,32,128]{2,1,0:T(8,128)(2,1)} %copy-done.1), custom_call_target="tpu_custom_call" | custom-call | flops 2147483648 | bytes 65536 | tf_op jit(solution)/shard_map/attend/pallas_call | solution.py:355
  72.5 0.0 collective-permute-done.5.refs_0_
  72.5 0.0 collective-permute-done.6.refs_1_
  72.5 0.0 collective-permute-done.7.refs_2_
  72.6 0.1 stack.15.routed_ref
  72.6 0.0 copy-start.2
  72.7 1.6 %collective-permute-start.11 = (bf16[3,8,16,1024]{3,2,1,0:T(8,128)(2,1)S(1)}, bf16[3,8,16,1024]{3,2,1,0:T(8,128)(2,1)S(1)}, u32[]{:S(2)}, u32[]{:S(2)}) collective-permute-start(bf16[3,8,16,1024]{3,2,1,0:T(8,128)(2,1)S(1)} %stack.15.routed_ref), channel_id=1, source_target_pairs={{0,16},{16,0},{1,17},{17,1},{2,18},{18,2},{3,19},{19,3},{4,20},{20... | collective-permute-start | bytes 2359304 | tf_op jit(solution)/shard_map/ppermute | solution.py:527
  74.2 0.0 copy-done.11
  74.2 1.5 %collective-permute-start.9 = (s16[136,2048]{1,0:T(8,128)(2,1)S(1)}, s16[136,2048]{1,0:T(8,128)(2,1)S(1)}, u32[]{:S(2)}, u32[]{:S(2)}) collective-permute-start(s16[136,2048]{1,0:T(8,128)(2,1)S(1)} %copy-done.11), channel_id=1, source_target_pairs={{0,1},{1,0},{2,3},{3,2},{4,5},{5,4},{6,7},{7,6},{8,9},{9,8},{10,11... | collective-permute-start | bytes 1671176 | tf_op jit(solution)/shard_map/ppermute | solution.py:524
  75.7 2.0 %collective-permute-done.8.refs_0_ = s16[136,2048]{1,0:T(8,128)(2,1)S(1)} collective-permute-done((s16[136,2048]{1,0:T(8,128)(2,1)}, s16[136,2048]{1,0:T(8,128)(2,1)S(1)}, u32[]{:S(2)}, u32[]{:S(2)}) %collective-permute-start.8) | collective-permute-done | bytes 557088 | tf_op jit(solution)/shard_map/ppermute | solution.py:524
  77.8 0.8 copy-done.13
  78.6 2.4 %close.1 = s16[136,2048]{1,0:T(8,128)(2,1)} custom-call(f32[2,128,1024]{2,1,0:T(8,128)} %get-tuple-element.75.num_ref, f32[2,8,1024]{2,1,0:T(8,128)} %get-tuple-element.76.stat_ref, s16[136,2048]{1,0:T(8,128)(2,1)} %copy-done.13), custom_call_target="tpu_custom_call" | custom-call | flops 262144 | bytes 65536 | tf_op jit(solution)/shard_map/close/pallas_call | solution.py:399
  81.0 3.7 %collective-permute-start.10 = (s16[136,2048]{1,0:T(8,128)(2,1)}, s16[136,2048]{1,0:T(8,128)(2,1)S(1)}, u32[]{:S(2)}, u32[]{:S(2)}) collective-permute-start(s16[136,2048]{1,0:T(8,128)(2,1)} %close.1), channel_id=1, source_target_pairs={{0,2},{1,3},{2,0},{3,1},{4,6},{5,7},{6,4},{7,5},{8,10},{9,11},{10,... | collective-permute-start | bytes 1671176 | tf_op jit(solution)/shard_map/ppermute | solution.py:524
  84.7 0.6 pad_add_fusion.1.place_ref
  85.3 7.1 %attend_open.3 = (f32[2,128,1024]{2,1,0:T(8,128)}, f32[2,8,1024]{2,1,0:T(8,128)}) custom-call(s32[2]{0:T(128)} %copy-done.9, bf16[8192,128]{1,0:T(8,128)(2,1)} %get-tuple-element.77.q_ref, bf16[8,1024,128]{2,1,0:T(8,128)(2,1)} %get-tuple-element.64.k_ref, bf16[1024,2048]{1,0:T(8,128)(2,1)} %bitcast.18, bf16[8,32,128]{2,1,0:T(8,128)(2,1)} %copy-done, ...), custom_call_target="tpu_custom_call" | custom-call | flops 2147483648 | bytes 65536 | tf_op jit(solution)/shard_map/attend_open/pallas_call | solution.py:355
  92.4 0.0 copy-done.2
  92.5 0.0 collective-permute-done.11.crossed_ref
  92.5 0.0 copy-start.10
  92.5 0.9 copy-done.10
  93.4 3.4 %arrange.1 = bf16[32,16,2048]{2,1,0:T(8,128)(2,1)} custom-call(s32[2]{0:T(128)} %pad_add_fusion.1.place_ref, bf16[8,16,2048]{2,1,0:T(8,128)(2,1)} %collective-permute-done.4.kept_ref, bf16[3,8,16,1024]{3,2,1,0:T(8,128)(2,1)} %copy-done.10, bf16[3,8,16,1024]{3,2,1,0:T(8,128)(2,1)} %copy-done.2), custom_call_target="tpu_custom_call" | custom-call | flops 262144 | bytes 65536 | tf_op jit(solution)/shard_map/arrange/pallas_call | solution.py:490
  96.8 0.0 collective-permute-done.9.refs_0_
  96.8 11.2 %collective-permute-done.10.refs_1_ = s16[136,2048]{1,0:T(8,128)(2,1)S(1)} collective-permute-done((s16[136,2048]{1,0:T(8,128)(2,1)}, s16[136,2048]{1,0:T(8,128)(2,1)S(1)}, u32[]{:S(2)}, u32[]{:S(2)}) %collective-permute-start.10) | collective-permute-done | bytes 557088 | tf_op jit(solution)/shard_map/ppermute | solution.py:524
  108.0 0.0 copy-done.12
  108.0 0.8 copy-done.14
  108.8 2.6 %finish.1 = bf16[128,2048]{1,0:T(8,128)(2,1)} custom-call(f32[2,128,1024]{2,1,0:T(8,128)} %get-tuple-element.78.num_ref, f32[2,8,1024]{2,1,0:T(8,128)} %get-tuple-element.79.stat_ref, s16[136,2048]{1,0:T(8,128)(2,1)} %copy-done.12, s16[136,2048]{1,0:T(8,128)(2,1)} %copy-done.14), custom_call_target="tpu_custom_call" | custom-call | flops 262144 | bytes 65536 | tf_op jit(solution)/shard_map/finish/pallas_call | solution.py:399
  (12 shorter events, 0.0 us)
Async XLA Ops:
  0.6 16.8 %copy-start.15 = (f32[128]{0:T(128)S(1)}, f32[128]{0:T(128)}, u32[]{:S(2)}) copy-start(f32[128]{0:T(128)} %constant.24) | copy-start | bytes 1540
  0.6 16.7 %copy-start.16 = (f32[128]{0:T(128)S(1)}, f32[128]{0:T(128)}, u32[]{:S(2)}) copy-start(f32[128]{0:T(128)} %constant.16.clone) | copy-start | bytes 1540
  7.7 37.0 %collective-permute-start.1 = (f32[32,2048]{1,0:T(8,128)}, f32[32,2048]{1,0:T(8,128)S(1)}, u32[]{:S(2)}, u32[]{:S(2)}) collective-permute-start(f32[32,2048]{1,0:T(8,128)} %get-tuple-element.42), channel_id=1, source_target_pairs={{0,1},{1,2},{2,3},{3,0},{4,5},{5,6},{6,7},{7,4},{8,9},{9,10},{10,1... | collective-permute-start | bytes 786440 | tf_op jit(solution)/shard_map/ppermute | solution.py:521
  10.7 34.0 %collective-permute-start.2 = (f32[32,2048]{1,0:T(8,128)}, f32[32,2048]{1,0:T(8,128)S(1)}, u32[]{:S(2)}, u32[]{:S(2)}) collective-permute-start(f32[32,2048]{1,0:T(8,128)} %get-tuple-element.43), channel_id=1, source_target_pairs={{0,2},{1,3},{2,0},{3,1},{4,6},{5,7},{6,4},{7,5},{8,10},{9,11},{10,... | collective-permute-start | bytes 786440 | tf_op jit(solution)/shard_map/ppermute | solution.py:521
  13.3 31.4 %collective-permute-start.3 = (f32[32,2048]{1,0:T(8,128)}, f32[32,2048]{1,0:T(8,128)S(1)}, u32[]{:S(2)}, u32[]{:S(2)}) collective-permute-start(f32[32,2048]{1,0:T(8,128)} %get-tuple-element.44), channel_id=1, source_target_pairs={{0,3},{1,0},{2,1},{3,2},{4,7},{5,4},{6,5},{7,6},{8,11},{9,8},{10,9... | collective-permute-start | bytes 786440 | tf_op jit(solution)/shard_map/ppermute | solution.py:521
  14.7 43.6 %collective-permute-start.4 = (bf16[8,16,2048]{2,1,0:T(8,128)(2,1)}, bf16[8,16,2048]{2,1,0:T(8,128)(2,1)}, u32[]{:S(2)}, u32[]{:S(2)}) collective-permute-start(bf16[8,16,2048]{2,1,0:T(8,128)(2,1)} %get-tuple-element.67), channel_id=1, source_target_pairs={{0,16},{16,0},{1,17},{17,1},{2,18},{18,2},{3,19},{19,3},{4,20},{20... | collective-permute-start | bytes 1572872 | tf_op jit(solution)/shard_map/ppermute | solution.py:527
  16.2 28.4 %collective-permute-start = (bf16[3,8,16,1024]{3,2,1,0:T(8,128)(2,1)}, bf16[3,8,16,1024]{3,2,1,0:T(8,128)(2,1)S(1)}, u32[]{:S(2)}, u32[]{:S(2)}) collective-permute-start(bf16[3,8,16,1024]{3,2,1,0:T(8,128)(2,1)} %get-tuple-element.51), channel_id=1, source_target_pairs={{0,16},{16,0},{1,17},{17,1},{2,18},{18,2},{3,19},{19,3},{4,20},{20... | collective-permute-start | bytes 2359304 | tf_op jit(solution)/shard_map/ppermute | solution.py:527
  21.4 23.1 %copy-start.6 = (bf16[8,16,1024]{2,1,0:T(8,128)(2,1)S(1)}, bf16[8,16,1024]{2,1,0:T(8,128)(2,1)}, u32[]{:S(2)}) copy-start(bf16[8,16,1024]{2,1,0:T(8,128)(2,1)} %get-tuple-element.48.refs_0_) | copy-start | bytes 786436
  21.4 23.1 %copy-start.7 = (bf16[8,16,1024]{2,1,0:T(8,128)(2,1)S(1)}, bf16[8,16,1024]{2,1,0:T(8,128)(2,1)}, u32[]{:S(2)}) copy-start(bf16[8,16,1024]{2,1,0:T(8,128)(2,1)} %get-tuple-element.49.refs_1_) | copy-start | bytes 786436
  21.4 23.1 %copy-start.8 = (bf16[8,16,1024]{2,1,0:T(8,128)(2,1)S(1)}, bf16[8,16,1024]{2,1,0:T(8,128)(2,1)}, u32[]{:S(2)}) copy-start(bf16[8,16,1024]{2,1,0:T(8,128)(2,1)} %get-tuple-element.50.refs_2_) | copy-start | bytes 786436
  21.4 23.3 %copy-start.3 = (f32[128,128]{1,0:T(8,128)S(1)}, f32[128,128]{1,0:T(8,128)}, u32[]{:S(2)}) copy-start(f32[128,128]{1,0:T(8,128)} %get-tuple-element.82.qs_ref) | copy-start | bytes 196612
  21.5 23.3 %copy-start.4 = (f32[128,128]{1,0:T(8,128)S(1)}, f32[128,128]{1,0:T(8,128)}, u32[]{:S(2)}) copy-start(f32[128,128]{1,0:T(8,128)} %get-tuple-element.83.qc_ref) | copy-start | bytes 196612
  21.5 23.3 %copy-start.5 = (f32[32,2048]{1,0:T(8,128)S(1)}, f32[32,2048]{1,0:T(8,128)}, u32[]{:S(2)}) copy-start(f32[32,2048]{1,0:T(8,128)} %get-tuple-element.56.refs_0_) | copy-start | bytes 786436
  29.1 21.5 %copy-start.9 = (s32[2]{0:T(128)}, s32[2]{0:T(128)S(1)}, u32[]{:S(2)}) copy-start(s32[2]{0:T(128)S(1)} %pad_add_fusion.info) | copy-start | bytes 28
  45.4 0.6 copy-start
  46.0 0.6 copy-start.1
  46.7 25.9 %collective-permute-start.5 = (bf16[8,16,1024]{2,1,0:T(8,128)(2,1)S(1)}, bf16[8,16,1024]{2,1,0:T(8,128)(2,1)S(1)}, u32[]{:S(2)}, u32[]{:S(2)}) collective-permute-start(bf16[8,16,1024]{2,1,0:T(8,128)(2,1)S(1)} %get-tuple-element.60), channel_id=1, source_target_pairs={{0,1},{1,2},{2,3},{3,0},{4,5},{5,6},{6,7},{7,4},{8,9},{9,10},{10,1... | collective-permute-start | bytes 786440 | tf_op jit(solution)/shard_map/ppermute | solution.py:521
  47.4 25.2 %collective-permute-start.6 = (bf16[8,16,1024]{2,1,0:T(8,128)(2,1)S(1)}, bf16[8,16,1024]{2,1,0:T(8,128)(2,1)S(1)}, u32[]{:S(2)}, u32[]{:S(2)}) collective-permute-start(bf16[8,16,1024]{2,1,0:T(8,128)(2,1)S(1)} %get-tuple-element.61), channel_id=1, source_target_pairs={{0,2},{1,3},{2,0},{3,1},{4,6},{5,7},{6,4},{7,5},{8,10},{9,11},{10,... | collective-permute-start | bytes 786440 | tf_op jit(solution)/shard_map/ppermute | solution.py:521
  47.7 24.9 %collective-permute-start.7 = (bf16[8,16,1024]{2,1,0:T(8,128)(2,1)S(1)}, bf16[8,16,1024]{2,1,0:T(8,128)(2,1)S(1)}, u32[]{:S(2)}, u32[]{:S(2)}) collective-permute-start(bf16[8,16,1024]{2,1,0:T(8,128)(2,1)S(1)} %get-tuple-element.62), channel_id=1, source_target_pairs={{0,3},{1,0},{2,1},{3,2},{4,7},{5,4},{6,5},{7,6},{8,11},{9,8},{10,9... | collective-permute-start | bytes 786440 | tf_op jit(solution)/shard_map/ppermute | solution.py:521
  57.7 20.1 %collective-permute-start.8 = (s16[136,2048]{1,0:T(8,128)(2,1)}, s16[136,2048]{1,0:T(8,128)(2,1)S(1)}, u32[]{:S(2)}, u32[]{:S(2)}) collective-permute-start(s16[136,2048]{1,0:T(8,128)(2,1)} %attend.2), channel_id=1, source_target_pairs={{0,1},{1,0},{2,3},{3,2},{4,5},{5,4},{6,7},{7,6},{8,9},{9,8},{10,11... | collective-permute-start | bytes 1671176 | tf_op jit(solution)/shard_map/ppermute | solution.py:524
  72.5 1.7 %copy-start.11 = (s16[136,2048]{1,0:T(8,128)(2,1)S(1)}, s16[136,2048]{1,0:T(8,128)(2,1)}, u32[]{:S(2)}) copy-start(s16[136,2048]{1,0:T(8,128)(2,1)} %attend.3) | copy-start | bytes 1671172
  72.6 19.8 %copy-start.2 = (bf16[3,8,16,1024]{3,2,1,0:T(8,128)(2,1)}, bf16[3,8,16,1024]{3,2,1,0:T(8,128)(2,1)S(1)}, u32[]{:S(2)}) copy-start(bf16[3,8,16,1024]{3,2,1,0:T(8,128)(2,1)S(1)} %stack.15.routed_ref) | copy-start | bytes 2359300
  72.7 19.8 %collective-permute-start.11 = (bf16[3,8,16,1024]{3,2,1,0:T(8,128)(2,1)S(1)}, bf16[3,8,16,1024]{3,2,1,0:T(8,128)(2,1)S(1)}, u32[]{:S(2)}, u32[]{:S(2)}) collective-permute-start(bf16[3,8,16,1024]{3,2,1,0:T(8,128)(2,1)S(1)} %stack.15.routed_ref), channel_id=1, source_target_pairs={{0,16},{16,0},{1,17},{17,1},{2,18},{18,2},{3,19},{19,3},{4,20},{20... | collective-permute-start | bytes 2359304 | tf_op jit(solution)/shard_map/ppermute | solution.py:527
  74.2 22.6 %collective-permute-start.9 = (s16[136,2048]{1,0:T(8,128)(2,1)S(1)}, s16[136,2048]{1,0:T(8,128)(2,1)S(1)}, u32[]{:S(2)}, u32[]{:S(2)}) collective-permute-start(s16[136,2048]{1,0:T(8,128)(2,1)S(1)} %copy-done.11), channel_id=1, source_target_pairs={{0,1},{1,0},{2,3},{3,2},{4,5},{5,4},{6,7},{7,6},{8,9},{9,8},{10,11... | collective-permute-start | bytes 1671176 | tf_op jit(solution)/shard_map/ppermute | solution.py:524
  77.8 0.8 copy-start.13
  81.0 27.1 %collective-permute-start.10 = (s16[136,2048]{1,0:T(8,128)(2,1)}, s16[136,2048]{1,0:T(8,128)(2,1)S(1)}, u32[]{:S(2)}, u32[]{:S(2)}) collective-permute-start(s16[136,2048]{1,0:T(8,128)(2,1)} %close.1), channel_id=1, source_target_pairs={{0,2},{1,3},{2,0},{3,1},{4,6},{5,7},{6,4},{7,5},{8,10},{9,11},{10,... | collective-permute-start | bytes 1671176 | tf_op jit(solution)/shard_map/ppermute | solution.py:524
  92.5 0.9 copy-start.10
  96.8 11.2 %copy-start.12 = (s16[136,2048]{1,0:T(8,128)(2,1)}, s16[136,2048]{1,0:T(8,128)(2,1)S(1)}, u32[]{:S(2)}) copy-start(s16[136,2048]{1,0:T(8,128)(2,1)S(1)} %collective-permute-done.9.refs_0_) | copy-start | bytes 1671172
  108.0 0.8 copy-start.14

commit v3 on v2

--- a/solution.py
+++ b/solution.py
@@ -27,7 +27,7 @@
 SCALE = 1.0 / math.sqrt(HD)
 EXP2_SCALE = SCALE * math.log2(math.e)
 LANES = 256
-KEYS = 256
+KEYS = 512
 DEPTH = 512
 TAIL = 8
 CONTRACT_FIRST = (((0,), (0,)), ((), ()))
@@ -192,7 +192,7 @@
             jax.ShapeDtypeStruct((KVH, CTX, HD), jnp.bfloat16),
         ],
         compiler_params=PARAMS,
-        cost_estimate=small_cost(1 << 20),
+        cost_estimate=small_cost(1 << 30),
         name="prepare",
     )(queries, cache, key_scale, *q_tables, *k_tables)
 
@@ -262,13 +262,14 @@
         in_specs=[pl.BlockSpec(memory_space=pltpu.SMEM)] + [vmem] * (2 + len(fresh)),
         out_specs=[vmem] * 2,
         out_shape=[jax.ShapeDtypeStruct((KVH, share, HD), jnp.bfloat16)] * 2,
-        compiler_params=SMALL_PARAMS,
+        compiler_params=PARAMS,
         cost_estimate=small_cost(1 << 18),
         name="gather",
     )(info, *q_tables, *fresh)
 
 
-def attend_kernel(is_open, info, q_ref, k_ref, v_ref, fk_ref, fv_ref, *refs):
+def attend_kernel(is_open, deps, info, q_ref, k_ref, v_ref, fk_ref, fv_ref, *refs):
+    refs = refs[deps:]
     if is_open:
         num_ref, stat_ref, scores = refs
     else:
@@ -333,7 +334,7 @@
     return [pl.BlockSpec((1, HD, cols), place), pl.BlockSpec((1, 8, cols), place)]
 
 
-def attend(info, code, queries, keys, cache, fresh, ranks, is_open):
+def attend(info, code, queries, keys, cache, fresh, earlier, ranks, is_open):
     pieces, heads, cols, share = layout(ranks)
 
     def piece(j, s):
@@ -353,7 +354,7 @@
         out_shape = jax.ShapeDtypeStruct((HD + TAIL, pieces * cols), jnp.int16)
     own_head = lambda j, s: (key_head(j, s), 0, 0)
     return pl.pallas_call(
-        functools.partial(attend_kernel, is_open),
+        functools.partial(attend_kernel, is_open, len(earlier)),
         grid_spec=pltpu.PrefetchScalarGridSpec(
             num_scalar_prefetch=1,
             grid=(pieces,),
@@ -363,19 +364,20 @@
                 pl.BlockSpec((CTX, HD), lambda j, s: (0, KVH + key_head(j, s))),
                 pl.BlockSpec((1, share, HD), own_head),
                 pl.BlockSpec((1, share, HD), own_head),
-            ],
+            ]
+            + [pl.BlockSpec(memory_space=pl.ANY)] * len(earlier),
             out_specs=out_specs,
             scratch_shapes=[pltpu.VMEM((CTX, cols), jnp.float32)],
         ),
         out_shape=out_shape,
         compiler_params=PARAMS,
-        cost_estimate=small_cost(1 << 31),
+        cost_estimate=small_cost(1 << 28),
         name="attend_open" if is_open else "attend",
-    )(info, queries, keys, cache, *fresh)
-
-
-def close_kernel(is_last, num_ref, stat_ref, *refs):
-    in_refs, out_ref = refs[:-1], refs[-1]
+    )(info, queries, keys, cache, *fresh, *earlier)
+
+
+def close_kernel(is_last, count, num_ref, stat_ref, *refs):
+    in_refs, out_ref = refs[:count], refs[-1]
     for b in range(out_ref.shape[1] // LANES):
         lanes = slice(b * LANES, (b + 1) * LANES)
         top, total, numerator = stat_ref[0, 0:1, lanes], stat_ref[0, 1:2, lanes], num_ref[0, :, lanes]
@@ -392,21 +394,22 @@
             )
 
 
-def close(opened, received, ranks, is_last=False):
+def close(opened, received, earlier, ranks, is_last=False):
     pieces, _, cols, _ = layout(ranks)
     rows, kind = (ROWS, jnp.bfloat16) if is_last else (HD + TAIL, jnp.int16)
     place = lambda j: (j, 0, 0)
     return pl.pallas_call(
-        functools.partial(close_kernel, is_last),
+        functools.partial(close_kernel, is_last, len(received)),
         grid=(pieces,),
         in_specs=[pl.BlockSpec((1, HD, cols), place), pl.BlockSpec((1, 8, cols), place)]
-        + [pl.BlockSpec((HD + TAIL, cols), lambda j: (0, j))] * len(received),
+        + [pl.BlockSpec((HD + TAIL, cols), lambda j: (0, j))] * len(received)
+        + [pl.BlockSpec(memory_space=pl.ANY)] * len(earlier),
         out_specs=pl.BlockSpec((rows, cols), lambda j: (0, j)),
         out_shape=jax.ShapeDtypeStruct((rows, pieces * cols), kind),
-        compiler_params=PARAMS,
+        compiler_params=SMALL_PARAMS,
         cost_estimate=small_cost(1 << 18),
         name="finish" if is_last else "close",
-    )(*opened, *received)
+    )(*opened, *received, *earlier)
 
 
 def choose_kernel(sec_ref, *refs):
@@ -440,10 +443,11 @@
     )(sec.reshape(1), *near, there)
 
 
-def stack_kernel(*refs):
-    out_ref, sems = refs[-2:]
+def stack_kernel(count, *refs):
+    out_ref, token_ref, sems = refs[-3:]
+    token_ref[...] = jnp.zeros_like(token_ref)
     copies = [
-        pltpu.make_async_copy(ref, out_ref.at[k], sems.at[k]) for k, ref in enumerate(refs[:-2])
+        pltpu.make_async_copy(ref, out_ref.at[k], sems.at[k]) for k, ref in enumerate(refs[:count])
     ]
     for c in copies:
         c.start()
@@ -451,18 +455,21 @@
         c.wait()
 
 
-def stack(values):
+def stack(values, earlier):
     count = len(values)
     return pl.pallas_call(
-        stack_kernel,
-        in_specs=[pl.BlockSpec(memory_space=pl.ANY)] * count,
-        out_specs=pl.BlockSpec(memory_space=pltpu.VMEM),
-        out_shape=jax.ShapeDtypeStruct((count,) + values[0].shape, values[0].dtype),
+        functools.partial(stack_kernel, count),
+        in_specs=[pl.BlockSpec(memory_space=pl.ANY)] * (count + len(earlier)),
+        out_specs=[pl.BlockSpec(memory_space=pltpu.VMEM)] * 2,
+        out_shape=[
+            jax.ShapeDtypeStruct((count,) + values[0].shape, values[0].dtype),
+            jax.ShapeDtypeStruct((8, 128), jnp.float32),
+        ],
         scratch_shapes=[pltpu.SemaphoreType.DMA((count,))],
         compiler_params=SMALL_PARAMS,
         cost_estimate=small_cost(1 << 32),
         name="stack",
-    )(*values)
+    )(*values, *earlier)
 
 
 def arrange_kernel(place_ref, kept_ref, crossed_ref, routed_ref, out_ref):
@@ -498,7 +505,7 @@
         ],
         out_specs=pl.BlockSpec((slots, PAGE, 2 * KVW), lambda j: (j, 0, 0)),
         out_shape=jax.ShapeDtypeStruct((ranks * slots, PAGE, 2 * KVW), jnp.bfloat16),
-        compiler_params=PARAMS,
+        compiler_params=SMALL_PARAMS,
         cost_estimate=small_cost(1 << 18),
         name="arrange",
     )(place, kept, crossed, routed)
@@ -534,45 +541,45 @@
     q_tables = rope_tables(after(length, part) + jnp.arange(ROWS, dtype=jnp.int32))
     k_tables = rope_tables(after(me, part) * CTX + jnp.arange(CTX, dtype=jnp.int32))
     there = handed_on(there)
-    kept = handed_on(kept)
+    info = jnp.stack([after(length, part), me])
     q_rot, keys = prepare(queries[0], cache, key_scale[None, :], q_tables, k_tables)
     chosen = choose(sec, near, after(there, q_rot))
     arrived = after(fresh, chosen)
-    chosen = after(chosen, arrived)
+    chosen, kept = after((chosen, kept), arrived)
     routed = [shifted(c, k + 1) for k, c in enumerate(chosen)]
-    info = jnp.stack([length, me])
+    kept = handed_on(kept)
     fresh = gather(info, q_tables, arrived)
 
     def attend_to(code, earlier, is_open):
-        return attend(info, code, after(q_rot, earlier), keys, cache, fresh, ranks, is_open)
+        return attend(info, code, q_rot, keys, cache, fresh, earlier, ranks, is_open)
 
     taken = {code: [] for code in range(ranks)}
 
     def send(value, code, bit):
         taken[code ^ bit].append(swapped(value, bit))
 
-    last = chosen
+    last = chosen[:1]
     for code in range(ranks - 1, 1, -2):
-        last = attend_to(code, last, False)
-        send(last, code, 1)
+        last = [attend_to(code, last, False)]
+        send(last[0], code, 1)
     merging = {}
     for code in range(ranks - 2, 0, -2):
-        last = merging[code] = attend_to(code, (last, kept), True)
-    last = attend_to(1, last, False)
-    send(last, 1, 1)
-    both = stack(after(routed, last))
+        merging[code] = attend_to(code, last, True)
+        last = merging[code][1:]
+    direct = attend_to(1, last, False)
+    both, token = stack(routed, [kept, direct])
     bit = 2
     while bit < ranks:
         for code in range(ranks - bit, 0, -2 * bit):
-            last = close(after(merging[code], both), taken[code], ranks)
-            send(last, code, bit)
+            last = [close(merging[code], taken[code], [token], ranks)]
+            send(last[0], code, bit)
         bit *= 2
     crossed = handed_on(both)
     own = attend_to(0, last, True)
-
-    handed = arrange(jnp.stack([sec, me]), kept, crossed, both)[None]
-    attended = close(own, taken[0], ranks, is_last=True)[None]
-    return (attended, handed)
+    handed = arrange(jnp.stack([sec, me]), kept, crossed, both)
+    taken[0].append(swapped(direct, 1))
+    attended = close(own, taken[0], [handed], ranks, is_last=True)[None]
+    return (attended, handed[None])
 
 
 def solution(mesh):

time: 112 us -> 100 us (0.89)
  waiting for transfers between devices: 28.8 us -> 23.4 us
  Pallas kernels: 52.3 us -> 49.5 us
  local copies, waits for them, and re-layouts: 3.84 us -> 1.93 us
  starting transfers between devices: 20.2 us -> 18.7 us
    ppermute x3, waiting for transfers between devices: 15.5 us -> 9.91 us  [handed_on(): lax.ppermute(value, 'sec', [(i, (i + 1) % secs) for i in range(secs)])]
    ppermute x3, starting transfers between devices: 5.75 us -> 2.5 us  [swapped(): return lax.ppermute(value, 'rank', [(i, i ^ bit) for i in range(ranks)])]
    pallas_call x7, Pallas kernels: 33.6 us -> 30.5 us  [the longest x4 28.4 us: attend(): pl.pallas_call(functools.partial(attend_kernel, is_open, len(earlier)), g...]
    unnamed x34 -> x32, local copies, waits for them, and re-layouts: 3.84 us -> 1.93 us
    ppermute x6, starting transfers between devices: 10.8 us -> 12.5 us  [shifted(): lax.ppermute(value, 'rank', [(i, (i + k) % ranks) for i in range(ranks)])]
    pallas_call x1, Pallas kernels: 0.65 us -> 1.99 us  [gather(): pl.pallas_call(functools.partial(gather_kernel, len(fresh)), in_specs=[pl...]
  transfers between devices with their start and end apart: 12 -> 12, of which waited for: 3 -> 5; matrix products, arithmetic and copies ran while one was open for 4% -> 5% of each run, Pallas kernels for 38% -> 41%
where the time goes in v3:
time: 100 us; the launch traced here: 99.7 us
  Pallas kernels  49.5 us (50%)
  waiting for transfers between devices  23.4 us (23%)
  starting transfers between devices  18.7 us (19%)
  other arithmetic  4.78 us (5%)
  local copies, waits for them, and re-layouts  1.93 us (2%)
  between operations  1.5 us (2%)
    pallas_call x4, Pallas kernels, attend(): pl.pallas_call(functools.partial(attend_kernel, is_open, len(earlier)), g...  28.4 us
    ppermute x3, waiting for transfers between devices, swapped(): return lax.ppermute(value, 'rank', [(i, i ^ bit) for i in range(ranks)])  13.4 us
    ppermute x6, starting transfers between devices, shifted(): lax.ppermute(value, 'rank', [(i, (i + k) % ranks) for i in range(ranks)])  12.5 us
    ppermute x3, waiting for transfers between devices, handed_on(): lax.ppermute(value, 'sec', [(i, (i + 1) % secs) for i in range(secs)])  9.91 us
    pallas_call x1, Pallas kernels, prepare(): pl.pallas_call(prepare_kernel, grid=(KVH,), in_specs=[pl.BlockSpec((ROWS,...  7.5 us
    pallas_call x1, Pallas kernels, project(): pl.pallas_call(functools.partial(project_kernel, ranks), in_specs=[smem,...  7.03 us
    mul x2, other arithmetic, rope_tables(): return (jnp.cos(angles), jnp.sin(angles) * sign[None, :])  4.05 us
    ppermute x3, starting transfers between devices, handed_on(): lax.ppermute(value, 'sec', [(i, (i + 1) % secs) for i in range(secs)])  3.64 us
  transfers between devices with their start and end apart: 12, of which 5 were waited for; matrix products, arithmetic and copies ran while one was open for 5% of the time, Pallas kernels for 41%

profile of v3, /device:TPU:0, one launch (start us, length us, event | category | flops | bytes accessed | tf_op | source)
XLA Modules:
  0.0 99.7 jit_solution(17686424801221641542)
XLA Ops:
  0.6 0.0 copy-start.13
  0.6 0.0 copy-start.14
  0.7 7.0 %project.1 = (f32[32,2048]{1,0:T(8,128)}, f32[32,2048]{1,0:T(8,128)}, f32[32,2048]{1,0:T(8,128)}, f32[32,2048]{1,0:T(8,128)}, bf16[8,16,2048]{2,1,0:T(8,128)(2,1...) custom-call(s32[1]{0:T(128)} %bitcast.1.rank_ref, ...), custom_call_target="tpu_custom_call" | custom-call | flops 1048576 | bytes 65536 | tf_op jit(solution)/shard_map/project/pallas_call | solution.py:142
  7.7 3.1 %collective-permute-start = (f32[32,2048]{1,0:T(8,128)}, f32[32,2048]{1,0:T(8,128)S(1)}, u32[]{:S(2)}, u32[]{:S(2)}) collective-permute-start(f32[32,2048]{1,0:T(8,128)} %get-tuple-element.36), channel_id=1, source_target_pairs={{0,1},{1,2},{2,3},{3,0},{4,5},{5,6},{6,7},{7,4},{8,9},{9,10},{10,1... | collective-permute-start | bytes 786440 | tf_op jit(solution)/shard_map/ppermute | solution.py:528
  10.8 2.6 %collective-permute-start.1 = (f32[32,2048]{1,0:T(8,128)}, f32[32,2048]{1,0:T(8,128)S(1)}, u32[]{:S(2)}, u32[]{:S(2)}) collective-permute-start(f32[32,2048]{1,0:T(8,128)} %get-tuple-element.37), channel_id=1, source_target_pairs={{0,2},{1,3},{2,0},{3,1},{4,6},{5,7},{6,4},{7,5},{8,10},{9,11},{10,... | collective-permute-start | bytes 786440 | tf_op jit(solution)/shard_map/ppermute | solution.py:528
  13.4 1.3 %collective-permute-start.2 = (f32[32,2048]{1,0:T(8,128)}, f32[32,2048]{1,0:T(8,128)S(1)}, u32[]{:S(2)}, u32[]{:S(2)}) collective-permute-start(f32[32,2048]{1,0:T(8,128)} %get-tuple-element.38), channel_id=1, source_target_pairs={{0,3},{1,0},{2,1},{3,2},{4,7},{5,4},{6,5},{7,6},{8,11},{9,8},{10,9... | collective-permute-start | bytes 786440 | tf_op jit(solution)/shard_map/ppermute | solution.py:528
  14.7 1.5 %collective-permute-start.3 = (bf16[3,8,16,1024]{3,2,1,0:T(8,128)(2,1)}, bf16[3,8,16,1024]{3,2,1,0:T(8,128)(2,1)S(1)}, u32[]{:S(2)}, u32[]{:S(2)}) collective-permute-start(bf16[3,8,16,1024]{3,2,1,0:T(8,128)(2,1)} %get-tuple-element.46), channel_id=1, source_target_pairs={{0,16},{16,0},{1,17},{17,1},{2,18},{18,2},{3,19},{19,3},{4,20},{20... | collective-permute-start | bytes 2359304 | tf_op jit(solution)/shard_map/ppermute | solution.py:534
  16.9 0.0 copy-done.13
  16.9 0.0 copy-done.14
  16.9 3.1 %fusion = (f32[1024,128]{1,0:T(8,128)}, f32[1024,128]{1,0:T(8,128)}) fusion(f32[128]{0:T(128)S(1)} %copy-done.13, f32[128]{0:T(128)S(1)} %copy-done.14, f32[1024]{0:T(1024)S(1)} %add_convert_fusion), kind=kLoop, calls=%fused_computation.2 | loop fusion | flops 262144 | bytes 1053696 | tf_op jit(solution)/shard_map/mul | solution.py:52
  20.0 1.0 fusion.1
  20.9 0.0 copy-start.6
  21.0 7.5 %prepare.1 = (bf16[8192,128]{1,0:T(8,128)(2,1)}, bf16[8,1024,128]{2,1,0:T(8,128)(2,1)}) custom-call(bf16[128,8192]{1,0:T(8,128)(2,1)} %bitcast.20, bf16[1024,2048]{1,0:T(8,128)(2,1)} %bitcast.15, f32[1,1024]{1,0:T(1,128)} %bitcast.23, f32[128,128]{1,0:T(8,128)} %get-tuple-element.71.qc_ref, f32[128,128]{1,0:T(8,128)} %get-tuple-element.70.qs_ref, ...), custom_call_target="tpu_custom_call" | custom-call | flops 1073741824 | bytes 65536 | tf_op jit(solution)/shard_map/prepare/pallas_call | solution.py:174
  28.5 4.9 %collective-permute-done.3.refs_3_ = bf16[3,8,16,1024]{3,2,1,0:T(8,128)(2,1)S(1)} collective-permute-done((bf16[3,8,16,1024]{3,2,1,0:T(8,128)(2,1)}, bf16[3,8,16,1024]{3,2,1,0:T(8,128)(2,1)S(1)}, u32[]{:S(2)}, u32[]{:S(2)}) %collective-permute-start.3) | collective-permute-done | bytes 786464 | tf_op jit(solution)/shard_map/ppermute | solution.py:534
  33.4 0.0 copy-done.6
  33.4 0.0 copy-done.7
  33.4 0.0 copy-done.8
  33.4 0.1 choose.1
  33.5 0.0 copy-start.5
  33.5 0.0 collective-permute-done.refs_1_
  33.5 0.0 copy-start.10
  33.5 0.0 collective-permute-done.1.refs_2_
  33.5 0.0 copy-start.11
  33.5 0.0 collective-permute-done.2.refs_3_
  33.6 0.0 copy-start.12
  33.6 0.0 copy-done.15
  33.6 1.6 %collective-permute-start.8 = (bf16[8,16,2048]{2,1,0:T(8,128)(2,1)S(1)}, bf16[8,16,2048]{2,1,0:T(8,128)(2,1)S(1)}, u32[]{:S(2)}, u32[]{:S(2)}) collective-permute-start(bf16[8,16,2048]{2,1,0:T(8,128)(2,1)S(1)} %copy-done.15), channel_id=1, source_target_pairs={{0,16},{16,0},{1,17},{17,1},{2,18},{18,2},{3,19},{19,3},{4,20},{20... | collective-permute-start | bytes 1572872 | tf_op jit(solution)/shard_map/ppermute | solution.py:534
  35.1 2.2 %collective-permute-start.6 = (bf16[8,16,1024]{2,1,0:T(8,128)(2,1)S(1)}, bf16[8,16,1024]{2,1,0:T(8,128)(2,1)S(1)}, u32[]{:S(2)}, u32[]{:S(2)}) collective-permute-start(bf16[8,16,1024]{2,1,0:T(8,128)(2,1)S(1)} %get-tuple-element.61), channel_id=1, source_target_pairs={{0,2},{1,3},{2,0},{3,1},{4,6},{5,7},{6,4},{7,5},{8,10},{9,11},{10,... | collective-permute-start | bytes 786440 | tf_op jit(solution)/shard_map/ppermute | solution.py:528
  37.4 3.3 %collective-permute-start.7 = (bf16[8,16,1024]{2,1,0:T(8,128)(2,1)S(1)}, bf16[8,16,1024]{2,1,0:T(8,128)(2,1)S(1)}, u32[]{:S(2)}, u32[]{:S(2)}) collective-permute-start(bf16[8,16,1024]{2,1,0:T(8,128)(2,1)S(1)} %get-tuple-element.62), channel_id=1, source_target_pairs={{0,3},{1,0},{2,1},{3,2},{4,7},{5,4},{6,5},{7,6},{8,11},{9,8},{10,9... | collective-permute-start | bytes 786440 | tf_op jit(solution)/shard_map/ppermute | solution.py:528
  40.6 0.0 collective-permute-start.5
  40.6 0.6 pad_add_fusion.info
  41.3 0.0 copy-done.10
  41.3 0.0 copy-done.11
  41.3 0.0 copy-done.12
  41.3 2.0 %gather.1 = (bf16[8,32,128]{2,1,0:T(8,128)(2,1)}, bf16[8,32,128]{2,1,0:T(8,128)(2,1)}) custom-call(s32[2]{0:T(128)} %pad_add_fusion.info, f32[128,128]{1,0:T(8,128)} %get-tuple-element.71.qc_ref, f32[128,128]{1,0:T(8,128)} %get-tuple-element.70.qs_ref, f32[32,2048]{1,0:T(8,128)} %get-tuple-element.51.refs_0_, f32[32,2048]{1,0:T(8,128)} %copy-done.10, ...), custom_call_target="tpu_custom_call" | custom-call | flops 262144 | bytes 65536 | tf_op jit(solution)/shard_map/gather/pallas_call | solution.py:260
  43.3 0.0 copy-done.5
  43.3 7.2 %attend.2.refs_0_ = s16[136,2048]{1,0:T(8,128)(2,1)} custom-call(s32[2]{0:T(128)} %pad_add_fusion.info, bf16[8192,128]{1,0:T(8,128)(2,1)} %get-tuple-element.41.q_ref, bf16[8,1024,128]{2,1,0:T(8,128)(2,1)} %get-tuple-element.42.k_ref, bf16[1024,2048]{1,0:T(8,128)(2,1)} %bitcast.16, bf16[8,32,128]{2,1,0:T(8,128)(2,1)} %get-tuple-element.55.fk_ref, ...), custom_call_target="tpu_custom_call" | custom-call | flops 268435456 | bytes 65536 | tf_op jit(solution)/shard_map/attend/pallas_call | solution.py:356
  50.4 1.3 %collective-permute-start.4 = (s16[136,2048]{1,0:T(8,128)(2,1)}, s16[136,2048]{1,0:T(8,128)(2,1)S(1)}, u32[]{:S(2)}, u32[]{:S(2)}) collective-permute-start(s16[136,2048]{1,0:T(8,128)(2,1)} %attend.2.refs_0_), channel_id=1, source_target_pairs={{0,1},{1,0},{2,3},{3,2},{4,5},{5,4},{6,7},{7,6},{8,9},{9,8},{10,11... | collective-permute-start | bytes 1671176 | tf_op jit(solution)/shard_map/ppermute | solution.py:531
  51.8 7.1 %attend_open.2 = (f32[2,128,1024]{2,1,0:T(8,128)}, f32[2,8,1024]{2,1,0:T(8,128)}) custom-call(s32[2]{0:T(128)} %pad_add_fusion.info, bf16[8192,128]{1,0:T(8,128)(2,1)} %get-tuple-element.41.q_ref, bf16[8,1024,128]{2,1,0:T(8,128)(2,1)} %get-tuple-element.42.k_ref, bf16[1024,2048]{1,0:T(8,128)(2,1)} %bitcast.17, bf16[8,32,128]{2,1,0:T(8,128)(2,1)} %get-tuple-element.55.fk_ref, ...), custom_call_target="tpu_custom_call" | custom-call | flops 268435456 | bytes 65536 | tf_op jit(solution)/shard_map/attend_open/pallas_call | solution.py:356
  58.8 7.1 %attend.3.refs_4_ = s16[136,2048]{1,0:T(8,128)(2,1)} custom-call(s32[2]{0:T(128)} %pad_add_fusion.info, bf16[8192,128]{1,0:T(8,128)(2,1)} %get-tuple-element.41.q_ref, bf16[8,1024,128]{2,1,0:T(8,128)(2,1)} %get-tuple-element.42.k_ref, bf16[1024,2048]{1,0:T(8,128)(2,1)} %bitcast.18, bf16[8,32,128]{2,1,0:T(8,128)(2,1)} %get-tuple-element.55.fk_ref, ...), custom_call_target="tpu_custom_call" | custom-call | flops 268435456 | bytes 65536 | tf_op jit(solution)/shard_map/attend/pallas_call | solution.py:356
  66.0 0.0 collective-permute-done.6.refs_1_
  66.0 0.0 collective-permute-done.7.refs_2_
  66.0 0.0 collective-permute-done.5.refs_0_
  66.0 0.0 collective-permute-done.8.refs_3_.kept_ref
  66.0 0.1 stack.16
  66.1 0.6 collective-permute-start.11
  66.7 0.7 collective-permute-start.10
  67.4 2.6 %collective-permute-done.4.refs_0_ = s16[136,2048]{1,0:T(8,128)(2,1)S(1)} collective-permute-done((s16[136,2048]{1,0:T(8,128)(2,1)}, s16[136,2048]{1,0:T(8,128)(2,1)S(1)}, u32[]{:S(2)}, u32[]{:S(2)}) %collective-permute-start.4) | collective-permute-done | bytes 557088 | tf_op jit(solution)/shard_map/ppermute | solution.py:531
  70.0 0.0 copy-done.3
  70.0 0.0 copy-done.4
  70.0 0.6 close.1.refs_0_
  70.6 0.0 copy-start.1
  70.6 0.5 collective-permute-start.9
  71.0 0.1 pad_add_fusion.1.place_ref
  71.1 0.3 copy-done.1
  71.4 7.0 %attend_open.3 = (f32[2,128,1024]{2,1,0:T(8,128)}, f32[2,8,1024]{2,1,0:T(8,128)}) custom-call(s32[2]{0:T(128)} %pad_add_fusion.info, bf16[8192,128]{1,0:T(8,128)(2,1)} %get-tuple-element.41.q_ref, bf16[8,1024,128]{2,1,0:T(8,128)(2,1)} %get-tuple-element.42.k_ref, bf16[1024,2048]{1,0:T(8,128)(2,1)} %bitcast.19, bf16[8,32,128]{2,1,0:T(8,128)(2,1)} %get-tuple-element.55.fk_ref, ...), custom_call_target="tpu_custom_call" | custom-call | flops 268435456 | bytes 65536 | tf_op jit(solution)/shard_map/attend_open/pallas_call | solution.py:356
  78.5 5.0 %collective-permute-done.11.crossed_ref = bf16[3,8,16,1024]{3,2,1,0:T(8,128)(2,1)S(1)} collective-permute-done((bf16[3,8,16,1024]{3,2,1,0:T(8,128)(2,1)S(1)}, bf16[3,8,16,1024]{3,2,1,0:T(8,128)(2,1)S(1)}, u32[]{:S(2)}, u32[]{:S(2)}) %collective-permute-start.11) | collective-permute-done | bytes 786464 | tf_op jit(solution)/shard_map/ppermute | solution.py:534
  83.5 2.4 %arrange.1.refs_2_ = bf16[32,16,2048]{2,1,0:T(8,128)(2,1)} custom-call(s32[2]{0:T(128)S(1)} %pad_add_fusion.1.place_ref, bf16[8,16,2048]{2,1,0:T(8,128)(2,1)S(1)} %collective-permute-done.8.refs_3_.kept_ref, bf16[3,8,16,1024]{3,2,1,0:T(8,128)(2,1)S(1)} %collective-permute-done.11.crossed_ref, bf16[3,8,16,1024]{3,2,1,0:T(8,128)(2,1)S(1)} %get-tuple-element.67.routed_ref), custom_call_target="tpu_custom_call" | custom-call | flops 262144 | bytes 65536 | tf_op jit(solution)/shard_map/arrange/pallas_call | solution.py:497
  85.9 4.9 %collective-permute-done.10.refs_1_ = s16[136,2048]{1,0:T(8,128)(2,1)S(1)} collective-permute-done((s16[136,2048]{1,0:T(8,128)(2,1)}, s16[136,2048]{1,0:T(8,128)(2,1)S(1)}, u32[]{:S(2)}, u32[]{:S(2)}) %collective-permute-start.10) | collective-permute-done | bytes 557088 | tf_op jit(solution)/shard_map/ppermute | solution.py:531
  90.7 6.0 %collective-permute-done.9.refs_0_ = s16[136,2048]{1,0:T(8,128)(2,1)S(1)} collective-permute-done((s16[136,2048]{1,0:T(8,128)(2,1)S(1)}, s16[136,2048]{1,0:T(8,128)(2,1)S(1)}, u32[]{:S(2)}, u32[]{:S(2)}) %collective-permute-start.9) | collective-permute-done | bytes 557088 | tf_op jit(solution)/shard_map/ppermute | solution.py:531
  96.7 0.0 copy-done.2
  96.7 0.0 copy-done.9
  96.7 1.6 %copy-done = bf16[32,16,2048]{2,1,0:T(8,128)(2,1)S(1)} copy-done((bf16[32,16,2048]{2,1,0:T(8,128)(2,1)S(1)}, bf16[32,16,2048]{2,1,0:T(8,128)(2,1)}, u32[]{:S(2)}) %copy-start) | copy-done | bytes 2097176
  98.3 1.4 %finish.1 = bf16[128,2048]{1,0:T(8,128)(2,1)} custom-call(f32[2,128,1024]{2,1,0:T(8,128)S(1)} %copy-done.2, f32[2,8,1024]{2,1,0:T(8,128)S(1)} %copy-done.9, s16[136,2048]{1,0:T(8,128)(2,1)S(1)} %collective-permute-done.9.refs_0_, s16[136,2048]{1,0:T(8,128)(2,1)S(1)} %collective-permute-done.10.refs_1_, bf16[32,16,2048]{2,1,0:T(8,128)(2,1)S(1)} %copy-done), custom_call_target="tpu_custom_call" | custom-call | flops 262144 | bytes 65536 | tf_op jit(solution)/shard_map/finish/pallas_call | solution.py:401
  (10 shorter events, 0.0 us)
Async XLA Ops:
  0.6 16.2 %copy-start.13 = (f32[128]{0:T(128)S(1)}, f32[128]{0:T(128)}, u32[]{:S(2)}) copy-start(f32[128]{0:T(128)} %constant.24) | copy-start | bytes 1540
  0.6 16.2 %copy-start.14 = (f32[128]{0:T(128)S(1)}, f32[128]{0:T(128)}, u32[]{:S(2)}) copy-start(f32[128]{0:T(128)} %constant.16.clone) | copy-start | bytes 1540
  7.7 25.8 %collective-permute-start = (f32[32,2048]{1,0:T(8,128)}, f32[32,2048]{1,0:T(8,128)S(1)}, u32[]{:S(2)}, u32[]{:S(2)}) collective-permute-start(f32[32,2048]{1,0:T(8,128)} %get-tuple-element.36), channel_id=1, source_target_pairs={{0,1},{1,2},{2,3},{3,0},{4,5},{5,6},{6,7},{7,4},{8,9},{9,10},{10,1... | collective-permute-start | bytes 786440 | tf_op jit(solution)/shard_map/ppermute | solution.py:528
  10.8 22.8 %collective-permute-start.1 = (f32[32,2048]{1,0:T(8,128)}, f32[32,2048]{1,0:T(8,128)S(1)}, u32[]{:S(2)}, u32[]{:S(2)}) collective-permute-start(f32[32,2048]{1,0:T(8,128)} %get-tuple-element.37), channel_id=1, source_target_pairs={{0,2},{1,3},{2,0},{3,1},{4,6},{5,7},{6,4},{7,5},{8,10},{9,11},{10,... | collective-permute-start | bytes 786440 | tf_op jit(solution)/shard_map/ppermute | solution.py:528
  13.4 20.2 %collective-permute-start.2 = (f32[32,2048]{1,0:T(8,128)}, f32[32,2048]{1,0:T(8,128)S(1)}, u32[]{:S(2)}, u32[]{:S(2)}) collective-permute-start(f32[32,2048]{1,0:T(8,128)} %get-tuple-element.38), channel_id=1, source_target_pairs={{0,3},{1,0},{2,1},{3,2},{4,7},{5,4},{6,5},{7,6},{8,11},{9,8},{10,9... | collective-permute-start | bytes 786440 | tf_op jit(solution)/shard_map/ppermute | solution.py:528
  14.7 18.7 %collective-permute-start.3 = (bf16[3,8,16,1024]{3,2,1,0:T(8,128)(2,1)}, bf16[3,8,16,1024]{3,2,1,0:T(8,128)(2,1)S(1)}, u32[]{:S(2)}, u32[]{:S(2)}) collective-permute-start(bf16[3,8,16,1024]{3,2,1,0:T(8,128)(2,1)} %get-tuple-element.46), channel_id=1, source_target_pairs={{0,16},{16,0},{1,17},{17,1},{2,18},{18,2},{3,19},{19,3},{4,20},{20... | collective-permute-start | bytes 2359304 | tf_op jit(solution)/shard_map/ppermute | solution.py:534
  20.9 12.4 %copy-start.6 = (bf16[8,16,1024]{2,1,0:T(8,128)(2,1)S(1)}, bf16[8,16,1024]{2,1,0:T(8,128)(2,1)}, u32[]{:S(2)}) copy-start(bf16[8,16,1024]{2,1,0:T(8,128)(2,1)} %get-tuple-element.43.refs_0_) | copy-start | bytes 786436
  21.0 12.4 %copy-start.7 = (bf16[8,16,1024]{2,1,0:T(8,128)(2,1)S(1)}, bf16[8,16,1024]{2,1,0:T(8,128)(2,1)}, u32[]{:S(2)}) copy-start(bf16[8,16,1024]{2,1,0:T(8,128)(2,1)} %get-tuple-element.44.refs_1_) | copy-start | bytes 786436
  21.0 12.4 %copy-start.8 = (bf16[8,16,1024]{2,1,0:T(8,128)(2,1)S(1)}, bf16[8,16,1024]{2,1,0:T(8,128)(2,1)}, u32[]{:S(2)}) copy-start(bf16[8,16,1024]{2,1,0:T(8,128)(2,1)} %get-tuple-element.45.refs_2_) | copy-start | bytes 786436
  21.0 12.6 %copy-start.15 = (bf16[8,16,2048]{2,1,0:T(8,128)(2,1)S(1)}, bf16[8,16,2048]{2,1,0:T(8,128)(2,1)}, u32[]{:S(2)}) copy-start(bf16[8,16,2048]{2,1,0:T(8,128)(2,1)} %get-tuple-element.63) | copy-start | bytes 1572868
  33.5 9.8 %copy-start.5 = (bf16[8,16,1024]{2,1,0:T(8,128)(2,1)}, bf16[8,16,1024]{2,1,0:T(8,128)(2,1)S(1)}, u32[]{:S(2)}) copy-start(bf16[8,16,1024]{2,1,0:T(8,128)(2,1)S(1)} %get-tuple-element.58.refs_0_) | copy-start | bytes 786436
  33.5 7.8 %copy-start.10 = (f32[32,2048]{1,0:T(8,128)}, f32[32,2048]{1,0:T(8,128)S(1)}, u32[]{:S(2)}) copy-start(f32[32,2048]{1,0:T(8,128)S(1)} %collective-permute-done.refs_1_) | copy-start | bytes 786436
  33.5 7.7 %copy-start.11 = (f32[32,2048]{1,0:T(8,128)}, f32[32,2048]{1,0:T(8,128)S(1)}, u32[]{:S(2)}) copy-start(f32[32,2048]{1,0:T(8,128)S(1)} %collective-permute-done.1.refs_2_) | copy-start | bytes 786436
  33.6 7.7 %copy-start.12 = (f32[32,2048]{1,0:T(8,128)}, f32[32,2048]{1,0:T(8,128)S(1)}, u32[]{:S(2)}) copy-start(f32[32,2048]{1,0:T(8,128)S(1)} %collective-permute-done.2.refs_3_) | copy-start | bytes 786436
  33.6 32.4 %collective-permute-start.8 = (bf16[8,16,2048]{2,1,0:T(8,128)(2,1)S(1)}, bf16[8,16,2048]{2,1,0:T(8,128)(2,1)S(1)}, u32[]{:S(2)}, u32[]{:S(2)}) collective-permute-start(bf16[8,16,2048]{2,1,0:T(8,128)(2,1)S(1)} %copy-done.15), channel_id=1, source_target_pairs={{0,16},{16,0},{1,17},{17,1},{2,18},{18,2},{3,19},{19,3},{4,20},{20... | collective-permute-start | bytes 1572872 | tf_op jit(solution)/shard_map/ppermute | solution.py:534
  35.1 30.8 %collective-permute-start.6 = (bf16[8,16,1024]{2,1,0:T(8,128)(2,1)S(1)}, bf16[8,16,1024]{2,1,0:T(8,128)(2,1)S(1)}, u32[]{:S(2)}, u32[]{:S(2)}) collective-permute-start(bf16[8,16,1024]{2,1,0:T(8,128)(2,1)S(1)} %get-tuple-element.61), channel_id=1, source_target_pairs={{0,2},{1,3},{2,0},{3,1},{4,6},{5,7},{6,4},{7,5},{8,10},{9,11},{10,... | collective-permute-start | bytes 786440 | tf_op jit(solution)/shard_map/ppermute | solution.py:528
  37.4 28.6 %collective-permute-start.7 = (bf16[8,16,1024]{2,1,0:T(8,128)(2,1)S(1)}, bf16[8,16,1024]{2,1,0:T(8,128)(2,1)S(1)}, u32[]{:S(2)}, u32[]{:S(2)}) collective-permute-start(bf16[8,16,1024]{2,1,0:T(8,128)(2,1)S(1)} %get-tuple-element.62), channel_id=1, source_target_pairs={{0,3},{1,0},{2,1},{3,2},{4,7},{5,4},{6,5},{7,6},{8,11},{9,8},{10,9... | collective-permute-start | bytes 786440 | tf_op jit(solution)/shard_map/ppermute | solution.py:528
  40.6 25.4 %collective-permute-start.5 = (bf16[8,16,1024]{2,1,0:T(8,128)(2,1)S(1)}, bf16[8,16,1024]{2,1,0:T(8,128)(2,1)S(1)}, u32[]{:S(2)}, u32[]{:S(2)}) collective-permute-start(bf16[8,16,1024]{2,1,0:T(8,128)(2,1)S(1)} %get-tuple-element.58.refs_0_), channel_id=1, source_target_pairs={{0,1},{1,2},{2,3},{3,0},{4,5},{5,6},{6,7},{7,4},{8,9},{9,10},{10,1... | collective-permute-start | bytes 786440 | tf_op jit(solution)/shard_map/ppermute | solution.py:528
  50.4 19.5 %collective-permute-start.4 = (s16[136,2048]{1,0:T(8,128)(2,1)}, s16[136,2048]{1,0:T(8,128)(2,1)S(1)}, u32[]{:S(2)}, u32[]{:S(2)}) collective-permute-start(s16[136,2048]{1,0:T(8,128)(2,1)} %attend.2.refs_0_), channel_id=1, source_target_pairs={{0,1},{1,0},{2,3},{3,2},{4,5},{5,4},{6,7},{7,6},{8,9},{9,8},{10,11... | collective-permute-start | bytes 1671176 | tf_op jit(solution)/shard_map/ppermute | solution.py:531
  66.0 4.0 %copy-start.3 = (f32[2,128,1024]{2,1,0:T(8,128)S(1)}, f32[2,128,1024]{2,1,0:T(8,128)}, u32[]{:S(2)}) copy-start(f32[2,128,1024]{2,1,0:T(8,128)} %get-tuple-element.59.num_ref) | copy-start | bytes 3145732
  66.0 4.0 %copy-start.4 = (f32[2,8,1024]{2,1,0:T(8,128)S(1)}, f32[2,8,1024]{2,1,0:T(8,128)}, u32[]{:S(2)}) copy-start(f32[2,8,1024]{2,1,0:T(8,128)} %get-tuple-element.60.refs_0_.stat_ref) | copy-start | bytes 196612
  66.1 17.4 %collective-permute-start.11 = (bf16[3,8,16,1024]{3,2,1,0:T(8,128)(2,1)S(1)}, bf16[3,8,16,1024]{3,2,1,0:T(8,128)(2,1)S(1)}, u32[]{:S(2)}, u32[]{:S(2)}) collective-permute-start(bf16[3,8,16,1024]{3,2,1,0:T(8,128)(2,1)S(1)} %get-tuple-element.67.routed_ref), channel_id=1, source_target_pairs={{0,16},{16,0},{1,17},{17,1},{2,18},{18,2},{3,19},{19,3},{4,20},{20... | collective-permute-start | bytes 2359304 | tf_op jit(solution)/shard_map/ppermute | solution.py:534
  66.7 24.0 %collective-permute-start.10 = (s16[136,2048]{1,0:T(8,128)(2,1)}, s16[136,2048]{1,0:T(8,128)(2,1)S(1)}, u32[]{:S(2)}, u32[]{:S(2)}) collective-permute-start(s16[136,2048]{1,0:T(8,128)(2,1)} %attend.3.refs_4_), channel_id=1, source_target_pairs={{0,1},{1,0},{2,3},{3,2},{4,5},{5,4},{6,7},{7,6},{8,9},{9,8},{10,11... | collective-permute-start | bytes 1671176 | tf_op jit(solution)/shard_map/ppermute | solution.py:531
  70.6 0.8 copy-start.1
  70.6 26.1 %collective-permute-start.9 = (s16[136,2048]{1,0:T(8,128)(2,1)S(1)}, s16[136,2048]{1,0:T(8,128)(2,1)S(1)}, u32[]{:S(2)}, u32[]{:S(2)}) collective-permute-start(s16[136,2048]{1,0:T(8,128)(2,1)S(1)} %close.1.refs_0_), channel_id=1, source_target_pairs={{0,2},{1,3},{2,0},{3,1},{4,6},{5,7},{6,4},{7,5},{8,10},{9,11},{10,... | collective-permute-start | bytes 1671176 | tf_op jit(solution)/shard_map/ppermute | solution.py:531
  78.4 18.3 %copy-start.2 = (f32[2,128,1024]{2,1,0:T(8,128)S(1)}, f32[2,128,1024]{2,1,0:T(8,128)}, u32[]{:S(2)}) copy-start(f32[2,128,1024]{2,1,0:T(8,128)} %get-tuple-element.65.num_ref) | copy-start | bytes 3145732
  78.5 18.3 %copy-start.9 = (f32[2,8,1024]{2,1,0:T(8,128)S(1)}, f32[2,8,1024]{2,1,0:T(8,128)}, u32[]{:S(2)}) copy-start(f32[2,8,1024]{2,1,0:T(8,128)} %get-tuple-element.66.stat_ref) | copy-start | bytes 196612
  96.7 1.6 %copy-start = (bf16[32,16,2048]{2,1,0:T(8,128)(2,1)S(1)}, bf16[32,16,2048]{2,1,0:T(8,128)(2,1)}, u32[]{:S(2)}) copy-start(bf16[32,16,2048]{2,1,0:T(8,128)(2,1)} %arrange.1.refs_2_) | copy-start | bytes 6291460

commit v4 on v3

--- a/solution.py
+++ b/solution.py
@@ -33,6 +33,7 @@
 CONTRACT_FIRST = (((0,), (0,)), ((), ()))
 CONTRACT_LAST = (((1,), (1,)), ((), ()))
 PARAMS = pltpu.CompilerParams(vmem_limit_bytes=60 << 20)
+ATTEND_PARAMS = pltpu.CompilerParams(vmem_limit_bytes=32 << 20)
 SMALL_PARAMS = pltpu.CompilerParams(vmem_limit_bytes=40 << 20)
 
 
@@ -191,7 +192,7 @@
             jax.ShapeDtypeStruct((HEADS * ROWS, HD), jnp.bfloat16),
             jax.ShapeDtypeStruct((KVH, CTX, HD), jnp.bfloat16),
         ],
-        compiler_params=PARAMS,
+        compiler_params=ATTEND_PARAMS,
         cost_estimate=small_cost(1 << 30),
         name="prepare",
     )(queries, cache, key_scale, *q_tables, *k_tables)
@@ -240,10 +241,10 @@
     return combine(values.reshape(rows // 8, 8, cols), axis=0)
 
 
-def gather_kernel(ranks, info, qc_ref, qs_ref, *refs):
+def gather_kernel(ranks, rank_ref, qc_ref, qs_ref, *refs):
     key_out, value_out = refs[ranks:]
     share = refs[0].shape[0]
-    mine = pl.ds(pl.multiple_of(info[1] * share, share), share)
+    mine = pl.ds(pl.multiple_of(rank_ref[0] * share, share), share)
     cosine, signed_sine = qc_ref[mine, :], qs_ref[mine, :]
     for h in range(KVH):
         columns = slice(h * HD, (h + 1) * HD)
@@ -254,7 +255,7 @@
         value_out[h] = sum(ref[:, columns] for ref in refs[:ranks]).astype(jnp.bfloat16)
 
 
-def gather(info, q_tables, fresh):
+def gather(me, q_tables, fresh):
     share = fresh[0].shape[0]
     vmem = pl.BlockSpec(memory_space=pltpu.VMEM)
     return pl.pallas_call(
@@ -262,21 +263,21 @@
         in_specs=[pl.BlockSpec(memory_space=pltpu.SMEM)] + [vmem] * (2 + len(fresh)),
         out_specs=[vmem] * 2,
         out_shape=[jax.ShapeDtypeStruct((KVH, share, HD), jnp.bfloat16)] * 2,
-        compiler_params=PARAMS,
+        compiler_params=ATTEND_PARAMS,
         cost_estimate=small_cost(1 << 18),
         name="gather",
-    )(info, *q_tables, *fresh)
-
-
-def attend_kernel(is_open, deps, info, q_ref, k_ref, v_ref, fk_ref, fv_ref, *refs):
+    )(me.reshape(1), *q_tables, *fresh)
+
+
+def attend_kernel(is_open, deps, length_ref, rank_ref, q_ref, k_ref, v_ref, fk_ref, fv_ref, *refs):
     refs = refs[deps:]
     if is_open:
         num_ref, stat_ref, scores = refs
     else:
         out_ref, scores = refs
-    rank = info[1]
+    rank = rank_ref[0]
     share = fk_ref.shape[1]
-    valid = info[0] - rank * CTX
+    valid = length_ref[0] - rank * CTX
     first = rank * share
     fresh_key, fresh_value = fk_ref[0], fv_ref[0]
     cols = q_ref.shape[0]
@@ -330,18 +331,18 @@
 
 
 def opened_specs(cols):
-    place = lambda j, s: (j, 0, 0)
+    place = lambda j, n, r: (j, 0, 0)
     return [pl.BlockSpec((1, HD, cols), place), pl.BlockSpec((1, 8, cols), place)]
 
 
-def attend(info, code, queries, keys, cache, fresh, earlier, ranks, is_open):
+def attend(length, me, code, queries, keys, cache, fresh, earlier, ranks, is_open):
     pieces, heads, cols, share = layout(ranks)
 
-    def piece(j, s):
-        return (s[1] ^ code) * pieces + j
-
-    def key_head(j, s):
-        return piece(j, s) * heads // GQ
+    def piece(j, rank_ref):
+        return (rank_ref[0] ^ code) * pieces + j
+
+    def key_head(j, rank_ref):
+        return piece(j, rank_ref) * heads // GQ
 
     if is_open:
         out_specs = opened_specs(cols)
@@ -350,18 +351,18 @@
             jax.ShapeDtypeStruct((pieces, 8, cols), jnp.float32),
         ]
     else:
-        out_specs = pl.BlockSpec((HD + TAIL, cols), lambda j, s: (0, j))
+        out_specs = pl.BlockSpec((HD + TAIL, cols), lambda j, n, r: (0, j))
         out_shape = jax.ShapeDtypeStruct((HD + TAIL, pieces * cols), jnp.int16)
-    own_head = lambda j, s: (key_head(j, s), 0, 0)
+    own_head = lambda j, n, r: (key_head(j, r), 0, 0)
     return pl.pallas_call(
         functools.partial(attend_kernel, is_open, len(earlier)),
         grid_spec=pltpu.PrefetchScalarGridSpec(
-            num_scalar_prefetch=1,
+            num_scalar_prefetch=2,
             grid=(pieces,),
             in_specs=[
-                pl.BlockSpec((cols, HD), lambda j, s: (piece(j, s), 0)),
+                pl.BlockSpec((cols, HD), lambda j, n, r: (piece(j, r), 0)),
                 pl.BlockSpec((1, CTX, HD), own_head),
-                pl.BlockSpec((CTX, HD), lambda j, s: (0, KVH + key_head(j, s))),
+                pl.BlockSpec((CTX, HD), lambda j, n, r: (0, KVH + key_head(j, r))),
                 pl.BlockSpec((1, share, HD), own_head),
                 pl.BlockSpec((1, share, HD), own_head),
             ]
@@ -370,10 +371,10 @@
             scratch_shapes=[pltpu.VMEM((CTX, cols), jnp.float32)],
         ),
         out_shape=out_shape,
-        compiler_params=PARAMS,
+        compiler_params=ATTEND_PARAMS,
         cost_estimate=small_cost(1 << 28),
         name="attend_open" if is_open else "attend",
-    )(info, queries, keys, cache, *fresh, *earlier)
+    )(length, me, queries, keys, cache, *fresh, *earlier)
 
 
 def close_kernel(is_last, count, num_ref, stat_ref, *refs):
@@ -472,10 +473,11 @@
     )(*values, *earlier)
 
 
-def arrange_kernel(place_ref, kept_ref, crossed_ref, routed_ref, out_ref):
+def arrange_kernel(sec_ref, rank_ref, kept_ref, crossed_ref, routed_ref, out_ref, token_ref):
+    token_ref[...] = jnp.zeros_like(token_ref)
     count = crossed_ref.shape[0]
-    shift = lax.rem(place_ref[1] - pl.program_id(0) + count + 1, count + 1)
-    second = place_ref[0] > 0
+    shift = lax.rem(rank_ref[0] - pl.program_id(0) + count + 1, count + 1)
+    second = sec_ref[0] > 0
 
     @pl.when(jnp.logical_not(second))
     def _():
@@ -491,7 +493,7 @@
         out_ref[:, :, KVW:] = routed_ref[shift - 1]
 
 
-def arrange(place, kept, crossed, routed):
+def arrange(sec, me, kept, crossed, routed):
     ranks = crossed.shape[0] + 1
     slots = kept.shape[0]
     return pl.pallas_call(
@@ -499,16 +501,23 @@
         grid=(ranks,),
         in_specs=[
             pl.BlockSpec(memory_space=pltpu.SMEM),
+            pl.BlockSpec(memory_space=pltpu.SMEM),
             pl.BlockSpec(kept.shape, lambda j: (0, 0, 0)),
             pl.BlockSpec(crossed.shape, lambda j: (0, 0, 0, 0)),
             pl.BlockSpec(routed.shape, lambda j: (0, 0, 0, 0)),
         ],
-        out_specs=pl.BlockSpec((slots, PAGE, 2 * KVW), lambda j: (j, 0, 0)),
-        out_shape=jax.ShapeDtypeStruct((ranks * slots, PAGE, 2 * KVW), jnp.bfloat16),
-        compiler_params=SMALL_PARAMS,
+        out_specs=[
+            pl.BlockSpec((slots, PAGE, 2 * KVW), lambda j: (j, 0, 0)),
+            pl.BlockSpec((8, 128), lambda j: (0, 0)),
+        ],
+        out_shape=[
+            jax.ShapeDtypeStruct((ranks * slots, PAGE, 2 * KVW), jnp.bfloat16),
+            jax.ShapeDtypeStruct((8, 128), jnp.float32),
+        ],
+        compiler_params=PARAMS,
         cost_estimate=small_cost(1 << 18),
         name="arrange",
-    )(place, kept, crossed, routed)
+    )(sec.reshape(1), me.reshape(1), kept, crossed, routed)
 
 
 def after(value, earlier):
@@ -541,17 +550,18 @@
     q_tables = rope_tables(after(length, part) + jnp.arange(ROWS, dtype=jnp.int32))
     k_tables = rope_tables(after(me, part) * CTX + jnp.arange(CTX, dtype=jnp.int32))
     there = handed_on(there)
-    info = jnp.stack([after(length, part), me])
     q_rot, keys = prepare(queries[0], cache, key_scale[None, :], q_tables, k_tables)
     chosen = choose(sec, near, after(there, q_rot))
     arrived = after(fresh, chosen)
-    chosen, kept = after((chosen, kept), arrived)
+    chosen = after(chosen, arrived)
     routed = [shifted(c, k + 1) for k, c in enumerate(chosen)]
-    kept = handed_on(kept)
-    fresh = gather(info, q_tables, arrived)
+    fresh = gather(me, q_tables, arrived)
+    kept = handed_on(after(kept, fresh))
 
     def attend_to(code, earlier, is_open):
-        return attend(info, code, q_rot, keys, cache, fresh, earlier, ranks, is_open)
+        return attend(
+            lengths[0], me.reshape(1), code, q_rot, keys, cache, fresh, earlier, ranks, is_open
+        )
 
     taken = {code: [] for code in range(ranks)}
 
@@ -576,9 +586,9 @@
         bit *= 2
     crossed = handed_on(both)
     own = attend_to(0, last, True)
-    handed = arrange(jnp.stack([sec, me]), kept, crossed, both)
+    handed, token = arrange(sec, me, kept, crossed, both)
     taken[0].append(swapped(direct, 1))
-    attended = close(own, taken[0], [handed], ranks, is_last=True)[None]
+    attended = close(own, taken[0], [token], ranks, is_last=True)[None]
     return (attended, handed[None])
 
 

time: 100 us -> 98.6 us (0.986)
  Pallas kernels: 49.5 us -> 35.8 us
  waiting for transfers between devices: 23.4 us -> 31.5 us
  starting transfers between devices: 18.7 us -> 23.6 us
  other arithmetic: 4.78 us -> 2.22 us
  local copies, waits for them, and re-layouts: 1.93 us -> 3.61 us
    pallas_call x4, Pallas kernels: 28.4 us -> 19.1 us  [attend(): pl.pallas_call(functools.partial(attend_kernel, is_open, len(earlier)), g...]
    ppermute x3, waiting for transfers between devices: 13.4 us -> 19.5 us  [swapped(): return lax.ppermute(value, 'rank', [(i, i ^ bit) for i in range(ranks)])]
    ppermute x3, starting transfers between devices: 2.5 us -> 7.25 us  [swapped(): return lax.ppermute(value, 'rank', [(i, i ^ bit) for i in range(ranks)])]
    pallas_call x1, Pallas kernels: 7.5 us -> 2.9 us  [prepare(): pl.pallas_call(prepare_kernel, grid=(KVH,), in_specs=[pl.BlockSpec((ROWS,...]
    ppermute x6, waiting for transfers between devices: 0.02 us -> 2.74 us  [shifted(): lax.ppermute(value, 'rank', [(i, (i + k) % ranks) for i in range(ranks)])]
    mul x2, other arithmetic: 4.05 us -> 2.21 us  [rope_tables(): return (jnp.cos(angles), jnp.sin(angles) * sign[None, :])]
    unnamed x32 -> x28, local copies, waits for them, and re-layouts: 1.93 us -> 3.61 us
  transfers between devices with their start and end apart: 12 -> 12, of which waited for: 5 -> 6; matrix products, arithmetic and copies ran while one was open for 5% -> 2% of each run, Pallas kernels for 41% -> 27%
where the time goes in v4:
time: 98.6 us; the launch traced here: 98.3 us
  Pallas kernels  35.8 us (36%)
  waiting for transfers between devices  31.5 us (32%)
  starting transfers between devices  23.6 us (24%)
  local copies, waits for them, and re-layouts  3.61 us (4%)
  other arithmetic  2.22 us (2%)
  between operations  1.56 us (2%)
    ppermute x3, waiting for transfers between devices, swapped(): return lax.ppermute(value, 'rank', [(i, i ^ bit) for i in range(ranks)])  19.5 us
    pallas_call x4, Pallas kernels, attend(): pl.pallas_call(functools.partial(attend_kernel, is_open, len(earlier)), g...  19.1 us
    ppermute x6, starting transfers between devices, shifted(): lax.ppermute(value, 'rank', [(i, (i + k) % ranks) for i in range(ranks)])  12.7 us
    ppermute x3, waiting for transfers between devices, handed_on(): lax.ppermute(value, 'sec', [(i, (i + 1) % secs) for i in range(secs)])  9.32 us
    ppermute x3, starting transfers between devices, swapped(): return lax.ppermute(value, 'rank', [(i, i ^ bit) for i in range(ranks)])  7.25 us
    pallas_call x1, Pallas kernels, project(): pl.pallas_call(functools.partial(project_kernel, ranks), in_specs=[smem,...  7.13 us
    unnamed x28, local copies, waits for them, and re-layouts  3.61 us
    ppermute x3, starting transfers between devices, handed_on(): lax.ppermute(value, 'sec', [(i, (i + 1) % secs) for i in range(secs)])  3.59 us
  transfers between devices with their start and end apart: 12, of which 6 were waited for; matrix products, arithmetic and copies ran while one was open for 2% of the time, Pallas kernels for 27%

profile of v4, /device:TPU:0, one launch (start us, length us, event | category | flops | bytes accessed | tf_op | source)
XLA Modules:
  0.0 98.3 jit_solution(3846409233349942013)
XLA Ops:
  0.6 0.0 copy-start.11
  0.6 0.0 copy-start.12
  0.7 0.0 copy-start.2
  0.7 0.0 copy-start.9
  0.7 7.1 %project.1 = (f32[32,2048]{1,0:T(8,128)}, f32[32,2048]{1,0:T(8,128)}, f32[32,2048]{1,0:T(8,128)}, f32[32,2048]{1,0:T(8,128)}, bf16[8,16,2048]{2,1,0:T(8,128)(2,1...) custom-call(s32[1]{0:T(128)} %bitcast.1.rank_ref, ...), custom_call_target="tpu_custom_call" | custom-call | flops 1048576 | bytes 65536 | tf_op jit(solution)/shard_map/project/pallas_call | solution.py:143
  7.8 3.1 %collective-permute-start = (f32[32,2048]{1,0:T(8,128)}, f32[32,2048]{1,0:T(8,128)S(1)}, u32[]{:S(2)}, u32[]{:S(2)}) collective-permute-start(f32[32,2048]{1,0:T(8,128)} %get-tuple-element.38), channel_id=1, source_target_pairs={{0,1},{1,2},{2,3},{3,0},{4,5},{5,6},{6,7},{7,4},{8,9},{9,10},{10,1... | collective-permute-start | bytes 786440 | tf_op jit(solution)/shard_map/ppermute | solution.py:537
  10.9 2.6 %collective-permute-start.1 = (f32[32,2048]{1,0:T(8,128)}, f32[32,2048]{1,0:T(8,128)S(1)}, u32[]{:S(2)}, u32[]{:S(2)}) collective-permute-start(f32[32,2048]{1,0:T(8,128)} %get-tuple-element.39), channel_id=1, source_target_pairs={{0,2},{1,3},{2,0},{3,1},{4,6},{5,7},{6,4},{7,5},{8,10},{9,11},{10,... | collective-permute-start | bytes 786440 | tf_op jit(solution)/shard_map/ppermute | solution.py:537
  13.5 1.3 %collective-permute-start.2 = (f32[32,2048]{1,0:T(8,128)}, f32[32,2048]{1,0:T(8,128)}, u32[]{:S(2)}, u32[]{:S(2)}) collective-permute-start(f32[32,2048]{1,0:T(8,128)} %get-tuple-element.40), channel_id=1, source_target_pairs={{0,3},{1,0},{2,1},{3,2},{4,7},{5,4},{6,5},{7,6},{8,11},{9,8},{10,9... | collective-permute-start | bytes 786440 | tf_op jit(solution)/shard_map/ppermute | solution.py:537
  14.8 1.5 %collective-permute-start.3 = (bf16[3,8,16,1024]{3,2,1,0:T(8,128)(2,1)}, bf16[3,8,16,1024]{3,2,1,0:T(8,128)(2,1)S(1)}, u32[]{:S(2)}, u32[]{:S(2)}) collective-permute-start(bf16[3,8,16,1024]{3,2,1,0:T(8,128)(2,1)} %get-tuple-element.48), channel_id=1, source_target_pairs={{0,16},{16,0},{1,17},{17,1},{2,18},{18,2},{3,19},{19,3},{4,20},{20... | collective-permute-start | bytes 2359304 | tf_op jit(solution)/shard_map/ppermute | solution.py:543
  17.0 0.0 copy-done.11
  17.0 0.0 copy-done.12
  17.0 1.9 %fusion = (f32[1024,128]{1,0:T(8,128)S(1)}, f32[1024,128]{1,0:T(8,128)S(1)}) fusion(f32[128]{0:T(128)S(1)} %copy-done.11, f32[128]{0:T(128)S(1)} %copy-done.12, f32[1024]{0:T(1024)S(1)} %add_convert_fusion), kind=kLoop, calls=%fused_computation.2 | loop fusion | flops 262144 | bytes 1053696 | tf_op jit(solution)/shard_map/mul | solution.py:53
  18.9 0.3 fusion.1
  19.2 0.0 copy-done.2
  19.3 0.0 copy-done.9
  19.3 0.0 copy-start
  19.3 2.2 %copy-done = bf16[1,1024,2048]{2,1,0:T(8,128)(2,1)S(1)} copy-done((bf16[1,1024,2048]{2,1,0:T(8,128)(2,1)S(1)}, bf16[1,1024,2048]{2,1,0:T(8,128)(2,1)}, u32[]{:S(2)}) %copy-start) | copy-done | bytes 4194328
  21.5 0.0 copy-start.6
  21.5 0.0 copy-start.7
  21.5 0.0 copy-start.5
  21.5 0.0 copy-start.1
  21.5 2.9 %prepare.1 = (bf16[8192,128]{1,0:T(8,128)(2,1)S(1)}, bf16[8,1024,128]{2,1,0:T(8,128)(2,1)S(1)}) custom-call(bf16[128,8192]{1,0:T(8,128)(2,1)S(1)} %bitcast.22, bf16[1024,2048]{1,0:T(8,128)(2,1)S(1)} %bitcast.17, f32[1,1024]{1,0:T(1,128)S(1)} %bitcast.23, f32[128,128]{1,0:T(8,128)S(1)} %get-tuple-element.75.qc_ref, f32[128,128]{1,0:T(8,128)S(1)} %get-tuple-element.74.qs_ref, ...), custom_call_target="tpu_custom_call" | custom-call | flops 1073741824 | bytes 65536 | tf_op jit(solution)/shard_map/prepare/pallas_call | solution.py:175
  24.4 0.0 copy-start.13
  24.4 9.1 %collective-permute-done.3.refs_3_ = bf16[3,8,16,1024]{3,2,1,0:T(8,128)(2,1)S(1)} collective-permute-done((bf16[3,8,16,1024]{3,2,1,0:T(8,128)(2,1)}, bf16[3,8,16,1024]{3,2,1,0:T(8,128)(2,1)S(1)}, u32[]{:S(2)}, u32[]{:S(2)}) %collective-permute-start.3) | collective-permute-done | bytes 786464 | tf_op jit(solution)/shard_map/ppermute | solution.py:543
  33.5 0.0 copy-done.6
  33.5 0.0 copy-done.7
  33.5 0.0 copy-done.8
  33.5 0.1 choose.1
  33.6 0.0 collective-permute-done.refs_1_
  33.6 0.0 collective-permute-done.1.refs_2_
  33.6 0.0 collective-permute-done.2.refs_3_
  33.6 0.0 copy-done.5
  33.7 1.1 %gather.1 = (bf16[8,32,128]{2,1,0:T(8,128)(2,1)S(1)}, bf16[8,32,128]{2,1,0:T(8,128)(2,1)S(1)}) custom-call(s32[1]{0:T(128)} %bitcast.1.rank_ref, f32[128,128]{1,0:T(8,128)S(1)} %get-tuple-element.75.qc_ref, f32[128,128]{1,0:T(8,128)S(1)} %get-tuple-element.74.qs_ref, f32[32,2048]{1,0:T(8,128)S(1)} %copy-done.5, f32[32,2048]{1,0:T(8,128)S(1)} %collective-permute-done.refs_1_, ...), custom_call_target="tpu_custom_call" | custom-call | flops 262144 | bytes 65536 | tf_op jit(solution)/shard_map/gather/pallas_call | solution.py:261
  34.7 0.0 copy-done.13
  34.8 1.6 %collective-permute-start.8 = (bf16[8,16,2048]{2,1,0:T(8,128)(2,1)S(1)}, bf16[8,16,2048]{2,1,0:T(8,128)(2,1)S(1)}, u32[]{:S(2)}, u32[]{:S(2)}) collective-permute-start(bf16[8,16,2048]{2,1,0:T(8,128)(2,1)S(1)} %copy-done.13), channel_id=1, source_target_pairs={{0,16},{16,0},{1,17},{17,1},{2,18},{18,2},{3,19},{19,3},{4,20},{20... | collective-permute-start | bytes 1572872 | tf_op jit(solution)/shard_map/ppermute | solution.py:543
  36.3 2.3 %collective-permute-start.6 = (bf16[8,16,1024]{2,1,0:T(8,128)(2,1)S(1)}, bf16[8,16,1024]{2,1,0:T(8,128)(2,1)S(1)}, u32[]{:S(2)}, u32[]{:S(2)}) collective-permute-start(bf16[8,16,1024]{2,1,0:T(8,128)(2,1)S(1)} %get-tuple-element.62), channel_id=1, source_target_pairs={{0,2},{1,3},{2,0},{3,1},{4,6},{5,7},{6,4},{7,5},{8,10},{9,11},{10,... | collective-permute-start | bytes 786440 | tf_op jit(solution)/shard_map/ppermute | solution.py:537
  38.6 3.4 %collective-permute-start.7 = (bf16[8,16,1024]{2,1,0:T(8,128)(2,1)S(1)}, bf16[8,16,1024]{2,1,0:T(8,128)(2,1)S(1)}, u32[]{:S(2)}, u32[]{:S(2)}) collective-permute-start(bf16[8,16,1024]{2,1,0:T(8,128)(2,1)S(1)} %get-tuple-element.63), channel_id=1, source_target_pairs={{0,3},{1,0},{2,1},{3,2},{4,7},{5,4},{6,5},{7,6},{8,11},{9,8},{10,9... | collective-permute-start | bytes 786440 | tf_op jit(solution)/shard_map/ppermute | solution.py:537
  42.0 0.0 collective-permute-start.5
  42.0 0.0 copy-done.1
  42.0 4.9 %attend.2.refs_0_ = s16[136,2048]{1,0:T(8,128)(2,1)S(1)} custom-call(s32[1]{0:T(128)} %bitcast.12.length_ref, s32[1]{0:T(128)} %bitcast.1.rank_ref, bf16[8192,128]{1,0:T(8,128)(2,1)S(1)} %get-tuple-element.43.q_ref, bf16[8,1024,128]{2,1,0:T(8,128)(2,1)S(1)} %get-tuple-element.44.k_ref, bf16[1024,2048]{1,0:T(8,128)(2,1)S(1)} %bitcast.18, ...), custom_call_target="tpu_custom_call" | custom-call | flops 268435456 | bytes 65536 | tf_op jit(solution)/shard_map/attend/pallas_call | solution.py:357
  46.9 1.2 %collective-permute-start.4 = (s16[136,2048]{1,0:T(8,128)(2,1)S(1)}, s16[136,2048]{1,0:T(8,128)(2,1)S(1)}, u32[]{:S(2)}, u32[]{:S(2)}) collective-permute-start(s16[136,2048]{1,0:T(8,128)(2,1)S(1)} %attend.2.refs_0_), channel_id=1, source_target_pairs={{0,1},{1,0},{2,3},{3,2},{4,5},{5,4},{6,7},{7,6},{8,9},{9,8},{10,11... | collective-permute-start | bytes 1671176 | tf_op jit(solution)/shard_map/ppermute | solution.py:540
  48.1 4.6 %attend_open.2 = (f32[2,128,1024]{2,1,0:T(8,128)S(1)}, f32[2,8,1024]{2,1,0:T(8,128)S(1)}) custom-call(s32[1]{0:T(128)} %bitcast.13.length_ref, s32[1]{0:T(128)} %bitcast.1.rank_ref, bf16[8192,128]{1,0:T(8,128)(2,1)S(1)} %get-tuple-element.43.q_ref, bf16[8,1024,128]{2,1,0:T(8,128)(2,1)S(1)} %get-tuple-element.44.k_ref, bf16[1024,2048]{1,0:T(8,128)(2,1)S(1)} %bitcast.19, ...), custom_call_target="tpu_custom_call" | custom-call | flops 268435456 | bytes 65536 | tf_op jit(solution)/shard_map/attend_open/pallas_call | solution.py:357
  52.8 4.9 %attend.3.refs_4_ = s16[136,2048]{1,0:T(8,128)(2,1)S(1)} custom-call(s32[1]{0:T(128)} %bitcast.14.length_ref, s32[1]{0:T(128)} %bitcast.1.rank_ref, bf16[8192,128]{1,0:T(8,128)(2,1)S(1)} %get-tuple-element.43.q_ref, bf16[8,1024,128]{2,1,0:T(8,128)(2,1)S(1)} %get-tuple-element.44.k_ref, bf16[1024,2048]{1,0:T(8,128)(2,1)S(1)} %bitcast.20, ...), custom_call_target="tpu_custom_call" | custom-call | flops 268435456 | bytes 65536 | tf_op jit(solution)/shard_map/attend/pallas_call | solution.py:357
  57.7 0.0 collective-permute-done.6.refs_1_
  57.7 0.0 collective-permute-done.7.refs_2_
  57.8 2.7 %collective-permute-done.5.refs_0_ = bf16[8,16,1024]{2,1,0:T(8,128)(2,1)S(1)} collective-permute-done((bf16[8,16,1024]{2,1,0:T(8,128)(2,1)S(1)}, bf16[8,16,1024]{2,1,0:T(8,128)(2,1)S(1)}, u32[]{:S(2)}, u32[]{:S(2)}) %collective-permute-start.5) | collective-permute-done | bytes 262176 | tf_op jit(solution)/shard_map/ppermute | solution.py:537
  60.5 0.0 collective-permute-done.8.refs_3_.kept_ref
  60.5 0.0 copy-start.4
  60.5 0.1 stack.1
  60.6 0.7 copy-done.4
  61.3 0.0 copy-start.3
  61.3 0.5 collective-permute-start.11
  61.8 2.0 %collective-permute-start.10 = (s16[136,2048]{1,0:T(8,128)(2,1)S(1)}, s16[136,2048]{1,0:T(8,128)(2,1)S(1)}, u32[]{:S(2)}, u32[]{:S(2)}) collective-permute-start(s16[136,2048]{1,0:T(8,128)(2,1)S(1)} %attend.3.refs_4_), channel_id=1, source_target_pairs={{0,1},{1,0},{2,3},{3,2},{4,5},{5,4},{6,7},{7,6},{8,9},{9,8},{10,11... | collective-permute-start | bytes 1671176 | tf_op jit(solution)/shard_map/ppermute | solution.py:540
  63.8 5.2 %collective-permute-done.4.refs_0_ = s16[136,2048]{1,0:T(8,128)(2,1)S(1)} collective-permute-done((s16[136,2048]{1,0:T(8,128)(2,1)S(1)}, s16[136,2048]{1,0:T(8,128)(2,1)S(1)}, u32[]{:S(2)}, u32[]{:S(2)}) %collective-permute-start.4) | collective-permute-done | bytes 557088 | tf_op jit(solution)/shard_map/ppermute | solution.py:540
  69.0 0.6 close.1.refs_0_
  69.5 4.1 %collective-permute-start.9 = (s16[136,2048]{1,0:T(8,128)(2,1)S(1)}, s16[136,2048]{1,0:T(8,128)(2,1)S(1)}, u32[]{:S(2)}, u32[]{:S(2)}) collective-permute-start(s16[136,2048]{1,0:T(8,128)(2,1)S(1)} %close.1.refs_0_), channel_id=1, source_target_pairs={{0,2},{1,3},{2,0},{3,1},{4,6},{5,7},{6,4},{7,5},{8,10},{9,11},{10,... | collective-permute-start | bytes 1671176 | tf_op jit(solution)/shard_map/ppermute | solution.py:540
  73.6 4.6 %attend_open.3 = (f32[2,128,1024]{2,1,0:T(8,128)S(1)}, f32[2,8,1024]{2,1,0:T(8,128)S(1)}) custom-call(s32[1]{0:T(128)} %bitcast.15.length_ref, s32[1]{0:T(128)} %bitcast.1.rank_ref, bf16[8192,128]{1,0:T(8,128)(2,1)S(1)} %get-tuple-element.43.q_ref, bf16[8,1024,128]{2,1,0:T(8,128)(2,1)S(1)} %get-tuple-element.44.k_ref, bf16[1024,2048]{1,0:T(8,128)(2,1)S(1)} %bitcast.21, ...), custom_call_target="tpu_custom_call" | custom-call | flops 268435456 | bytes 65536 | tf_op jit(solution)/shard_map/attend_open/pallas_call | solution.py:357
  78.3 0.0 copy-done.3
  78.3 0.2 collective-permute-done.11.crossed_ref
  78.5 3.4 %arrange.1 = (bf16[32,16,2048]{2,1,0:T(8,128)(2,1)}, f32[8,128]{1,0:T(8,128)}) custom-call(s32[1]{0:T(128)} %bitcast.8.sec_ref, s32[1]{0:T(128)} %bitcast.1.rank_ref, bf16[8,16,2048]{2,1,0:T(8,128)(2,1)} %copy-done.4, bf16[3,8,16,1024]{3,2,1,0:T(8,128)(2,1)} %collective-permute-done.11.crossed_ref, bf16[3,8,16,1024]{3,2,1,0:T(8,128)(2,1)} %copy-done.3), custom_call_target="tpu_custom_call" | custom-call | flops 262144 | bytes 65536 | tf_op jit(solution)/shard_map/arrange/pallas_call | solution.py:499
  81.9 9.0 %collective-permute-done.10.refs_1_ = s16[136,2048]{1,0:T(8,128)(2,1)S(1)} collective-permute-done((s16[136,2048]{1,0:T(8,128)(2,1)S(1)}, s16[136,2048]{1,0:T(8,128)(2,1)S(1)}, u32[]{:S(2)}, u32[]{:S(2)}) %collective-permute-start.10) | collective-permute-done | bytes 557088 | tf_op jit(solution)/shard_map/ppermute | solution.py:540
  90.9 5.3 %collective-permute-done.9.refs_0_ = s16[136,2048]{1,0:T(8,128)(2,1)S(1)} collective-permute-done((s16[136,2048]{1,0:T(8,128)(2,1)S(1)}, s16[136,2048]{1,0:T(8,128)(2,1)S(1)}, u32[]{:S(2)}, u32[]{:S(2)}) %collective-permute-start.9) | collective-permute-done | bytes 557088 | tf_op jit(solution)/shard_map/ppermute | solution.py:540
  96.2 0.7 copy-done.10
  96.9 1.4 %finish.1 = bf16[128,2048]{1,0:T(8,128)(2,1)} custom-call(f32[2,128,1024]{2,1,0:T(8,128)S(1)} %get-tuple-element.67.num_ref, f32[2,8,1024]{2,1,0:T(8,128)S(1)} %get-tuple-element.68.stat_ref, s16[136,2048]{1,0:T(8,128)(2,1)S(1)} %collective-permute-done.9.refs_0_, s16[136,2048]{1,0:T(8,128)(2,1)S(1)} %collective-permute-done.10.refs_1_, f32[8,128]{1,0:T(8,128)S(1)} %copy-done.10), custom_call_target="tpu_custom_call" | custom-call | flops 262144 | bytes 65536 | tf_op jit(solution)/shard_map/finish/pallas_call | solution.py:402
  (4 shorter events, 0.0 us)
Async XLA Ops:
  0.6 16.4 %copy-start.11 = (f32[128]{0:T(128)S(1)}, f32[128]{0:T(128)}, u32[]{:S(2)}) copy-start(f32[128]{0:T(128)} %constant.24) | copy-start | bytes 1540
  0.6 16.4 %copy-start.12 = (f32[128]{0:T(128)S(1)}, f32[128]{0:T(128)}, u32[]{:S(2)}) copy-start(f32[128]{0:T(128)} %constant.16.clone) | copy-start | bytes 1540
  0.7 18.6 %copy-start.2 = (bf16[1,128,8192]{2,1,0:T(8,128)(2,1)S(1)}, bf16[1,128,8192]{2,1,0:T(8,128)(2,1)}, u32[]{:S(2)}) copy-start(bf16[1,128,8192]{2,1,0:T(8,128)(2,1)} %param.12) | copy-start | bytes 6291460
  0.7 18.6 %copy-start.9 = (f32[1024]{0:T(1024)S(1)}, f32[1024]{0:T(1024)}, u32[]{:S(2)}) copy-start(f32[1024]{0:T(1024)} %param.14) | copy-start | bytes 12292
  7.8 25.8 %collective-permute-start = (f32[32,2048]{1,0:T(8,128)}, f32[32,2048]{1,0:T(8,128)S(1)}, u32[]{:S(2)}, u32[]{:S(2)}) collective-permute-start(f32[32,2048]{1,0:T(8,128)} %get-tuple-element.38), channel_id=1, source_target_pairs={{0,1},{1,2},{2,3},{3,0},{4,5},{5,6},{6,7},{7,4},{8,9},{9,10},{10,1... | collective-permute-start | bytes 786440 | tf_op jit(solution)/shard_map/ppermute | solution.py:537
  10.9 22.7 %collective-permute-start.1 = (f32[32,2048]{1,0:T(8,128)}, f32[32,2048]{1,0:T(8,128)S(1)}, u32[]{:S(2)}, u32[]{:S(2)}) collective-permute-start(f32[32,2048]{1,0:T(8,128)} %get-tuple-element.39), channel_id=1, source_target_pairs={{0,2},{1,3},{2,0},{3,1},{4,6},{5,7},{6,4},{7,5},{8,10},{9,11},{10,... | collective-permute-start | bytes 786440 | tf_op jit(solution)/shard_map/ppermute | solution.py:537
  13.5 20.1 %collective-permute-start.2 = (f32[32,2048]{1,0:T(8,128)}, f32[32,2048]{1,0:T(8,128)}, u32[]{:S(2)}, u32[]{:S(2)}) collective-permute-start(f32[32,2048]{1,0:T(8,128)} %get-tuple-element.40), channel_id=1, source_target_pairs={{0,3},{1,0},{2,1},{3,2},{4,7},{5,4},{6,5},{7,6},{8,11},{9,8},{10,9... | collective-permute-start | bytes 786440 | tf_op jit(solution)/shard_map/ppermute | solution.py:537
  14.8 18.6 %collective-permute-start.3 = (bf16[3,8,16,1024]{3,2,1,0:T(8,128)(2,1)}, bf16[3,8,16,1024]{3,2,1,0:T(8,128)(2,1)S(1)}, u32[]{:S(2)}, u32[]{:S(2)}) collective-permute-start(bf16[3,8,16,1024]{3,2,1,0:T(8,128)(2,1)} %get-tuple-element.48), channel_id=1, source_target_pairs={{0,16},{16,0},{1,17},{17,1},{2,18},{18,2},{3,19},{19,3},{4,20},{20... | collective-permute-start | bytes 2359304 | tf_op jit(solution)/shard_map/ppermute | solution.py:543
  19.3 2.2 %copy-start = (bf16[1,1024,2048]{2,1,0:T(8,128)(2,1)S(1)}, bf16[1,1024,2048]{2,1,0:T(8,128)(2,1)}, u32[]{:S(2)}) copy-start(bf16[1,1024,2048]{2,1,0:T(8,128)(2,1)} %param.13) | copy-start | bytes 12582916
  21.5 12.0 %copy-start.6 = (bf16[8,16,1024]{2,1,0:T(8,128)(2,1)S(1)}, bf16[8,16,1024]{2,1,0:T(8,128)(2,1)}, u32[]{:S(2)}) copy-start(bf16[8,16,1024]{2,1,0:T(8,128)(2,1)} %get-tuple-element.45.refs_0_) | copy-start | bytes 786436
  21.5 12.0 %copy-start.7 = (bf16[8,16,1024]{2,1,0:T(8,128)(2,1)S(1)}, bf16[8,16,1024]{2,1,0:T(8,128)(2,1)}, u32[]{:S(2)}) copy-start(bf16[8,16,1024]{2,1,0:T(8,128)(2,1)} %get-tuple-element.46.refs_1_) | copy-start | bytes 786436
  21.5 12.0 %copy-start.8 = (bf16[8,16,1024]{2,1,0:T(8,128)(2,1)S(1)}, bf16[8,16,1024]{2,1,0:T(8,128)(2,1)}, u32[]{:S(2)}) copy-start(bf16[8,16,1024]{2,1,0:T(8,128)(2,1)} %get-tuple-element.47.refs_2_) | copy-start | bytes 786436
  21.5 12.2 %copy-start.5 = (f32[32,2048]{1,0:T(8,128)S(1)}, f32[32,2048]{1,0:T(8,128)}, u32[]{:S(2)}) copy-start(f32[32,2048]{1,0:T(8,128)} %get-tuple-element.53.refs_0_) | copy-start | bytes 786436
  21.5 20.6 %copy-start.1 = (bf16[1,1024,2048]{2,1,0:T(8,128)(2,1)S(1)}, bf16[1,1024,2048]{2,1,0:T(8,128)(2,1)}, u32[]{:S(2)}) copy-start(bf16[1,1024,2048]{2,1,0:T(8,128)(2,1)} %param.13) | copy-start | bytes 12582916
  24.4 10.4 %copy-start.13 = (bf16[8,16,2048]{2,1,0:T(8,128)(2,1)S(1)}, bf16[8,16,2048]{2,1,0:T(8,128)(2,1)}, u32[]{:S(2)}) copy-start(bf16[8,16,2048]{2,1,0:T(8,128)(2,1)} %get-tuple-element.65) | copy-start | bytes 1572868
  34.8 25.7 %collective-permute-start.8 = (bf16[8,16,2048]{2,1,0:T(8,128)(2,1)S(1)}, bf16[8,16,2048]{2,1,0:T(8,128)(2,1)S(1)}, u32[]{:S(2)}, u32[]{:S(2)}) collective-permute-start(bf16[8,16,2048]{2,1,0:T(8,128)(2,1)S(1)} %copy-done.13), channel_id=1, source_target_pairs={{0,16},{16,0},{1,17},{17,1},{2,18},{18,2},{3,19},{19,3},{4,20},{20... | collective-permute-start | bytes 1572872 | tf_op jit(solution)/shard_map/ppermute | solution.py:543
  36.3 21.4 %collective-permute-start.6 = (bf16[8,16,1024]{2,1,0:T(8,128)(2,1)S(1)}, bf16[8,16,1024]{2,1,0:T(8,128)(2,1)S(1)}, u32[]{:S(2)}, u32[]{:S(2)}) collective-permute-start(bf16[8,16,1024]{2,1,0:T(8,128)(2,1)S(1)} %get-tuple-element.62), channel_id=1, source_target_pairs={{0,2},{1,3},{2,0},{3,1},{4,6},{5,7},{6,4},{7,5},{8,10},{9,11},{10,... | collective-permute-start | bytes 786440 | tf_op jit(solution)/shard_map/ppermute | solution.py:537
  38.6 19.1 %collective-permute-start.7 = (bf16[8,16,1024]{2,1,0:T(8,128)(2,1)S(1)}, bf16[8,16,1024]{2,1,0:T(8,128)(2,1)S(1)}, u32[]{:S(2)}, u32[]{:S(2)}) collective-permute-start(bf16[8,16,1024]{2,1,0:T(8,128)(2,1)S(1)} %get-tuple-element.63), channel_id=1, source_target_pairs={{0,3},{1,0},{2,1},{3,2},{4,7},{5,4},{6,5},{7,6},{8,11},{9,8},{10,9... | collective-permute-start | bytes 786440 | tf_op jit(solution)/shard_map/ppermute | solution.py:537
  42.0 18.5 %collective-permute-start.5 = (bf16[8,16,1024]{2,1,0:T(8,128)(2,1)S(1)}, bf16[8,16,1024]{2,1,0:T(8,128)(2,1)S(1)}, u32[]{:S(2)}, u32[]{:S(2)}) collective-permute-start(bf16[8,16,1024]{2,1,0:T(8,128)(2,1)S(1)} %get-tuple-element.59.refs_0_), channel_id=1, source_target_pairs={{0,1},{1,2},{2,3},{3,0},{4,5},{5,6},{6,7},{7,4},{8,9},{9,10},{10,1... | collective-permute-start | bytes 786440 | tf_op jit(solution)/shard_map/ppermute | solution.py:537
  46.9 22.0 %collective-permute-start.4 = (s16[136,2048]{1,0:T(8,128)(2,1)S(1)}, s16[136,2048]{1,0:T(8,128)(2,1)S(1)}, u32[]{:S(2)}, u32[]{:S(2)}) collective-permute-start(s16[136,2048]{1,0:T(8,128)(2,1)S(1)} %attend.2.refs_0_), channel_id=1, source_target_pairs={{0,1},{1,0},{2,3},{3,2},{4,5},{5,4},{6,7},{7,6},{8,9},{9,8},{10,11... | collective-permute-start | bytes 1671176 | tf_op jit(solution)/shard_map/ppermute | solution.py:540
  60.5 0.8 copy-start.4
  61.3 17.0 %copy-start.3 = (bf16[3,8,16,1024]{3,2,1,0:T(8,128)(2,1)}, bf16[3,8,16,1024]{3,2,1,0:T(8,128)(2,1)S(1)}, u32[]{:S(2)}) copy-start(bf16[3,8,16,1024]{3,2,1,0:T(8,128)(2,1)S(1)} %get-tuple-element.69.routed_ref) | copy-start | bytes 2359300
  61.3 17.2 %collective-permute-start.11 = (bf16[3,8,16,1024]{3,2,1,0:T(8,128)(2,1)S(1)}, bf16[3,8,16,1024]{3,2,1,0:T(8,128)(2,1)}, u32[]{:S(2)}, u32[]{:S(2)}) collective-permute-start(bf16[3,8,16,1024]{3,2,1,0:T(8,128)(2,1)S(1)} %get-tuple-element.69.routed_ref), channel_id=1, source_target_pairs={{0,16},{16,0},{1,17},{17,1},{2,18},{18,2},{3,19},{19,3},{4,20},{20... | collective-permute-start | bytes 2359304 | tf_op jit(solution)/shard_map/ppermute | solution.py:543
  61.8 29.0 %collective-permute-start.10 = (s16[136,2048]{1,0:T(8,128)(2,1)S(1)}, s16[136,2048]{1,0:T(8,128)(2,1)S(1)}, u32[]{:S(2)}, u32[]{:S(2)}) collective-permute-start(s16[136,2048]{1,0:T(8,128)(2,1)S(1)} %attend.3.refs_4_), channel_id=1, source_target_pairs={{0,1},{1,0},{2,3},{3,2},{4,5},{5,4},{6,7},{7,6},{8,9},{9,8},{10,11... | collective-permute-start | bytes 1671176 | tf_op jit(solution)/shard_map/ppermute | solution.py:540
  69.5 26.7 %collective-permute-start.9 = (s16[136,2048]{1,0:T(8,128)(2,1)S(1)}, s16[136,2048]{1,0:T(8,128)(2,1)S(1)}, u32[]{:S(2)}, u32[]{:S(2)}) collective-permute-start(s16[136,2048]{1,0:T(8,128)(2,1)S(1)} %close.1.refs_0_), channel_id=1, source_target_pairs={{0,2},{1,3},{2,0},{3,1},{4,6},{5,7},{6,4},{7,5},{8,10},{9,11},{10,... | collective-permute-start | bytes 1671176 | tf_op jit(solution)/shard_map/ppermute | solution.py:540
  96.2 0.7 copy-start.10

commit v5 on v4

--- a/solution.py
+++ b/solution.py
@@ -473,8 +473,7 @@
     )(*values, *earlier)
 
 
-def arrange_kernel(sec_ref, rank_ref, kept_ref, crossed_ref, routed_ref, out_ref, token_ref):
-    token_ref[...] = jnp.zeros_like(token_ref)
+def arrange_kernel(sec_ref, rank_ref, kept_ref, crossed_ref, routed_ref, out_ref):
     count = crossed_ref.shape[0]
     shift = lax.rem(rank_ref[0] - pl.program_id(0) + count + 1, count + 1)
     second = sec_ref[0] > 0
@@ -506,15 +505,9 @@
             pl.BlockSpec(crossed.shape, lambda j: (0, 0, 0, 0)),
             pl.BlockSpec(routed.shape, lambda j: (0, 0, 0, 0)),
         ],
-        out_specs=[
-            pl.BlockSpec((slots, PAGE, 2 * KVW), lambda j: (j, 0, 0)),
-            pl.BlockSpec((8, 128), lambda j: (0, 0)),
-        ],
-        out_shape=[
-            jax.ShapeDtypeStruct((ranks * slots, PAGE, 2 * KVW), jnp.bfloat16),
-            jax.ShapeDtypeStruct((8, 128), jnp.float32),
-        ],
-        compiler_params=PARAMS,
+        out_specs=pl.BlockSpec((slots, PAGE, 2 * KVW), lambda j: (j, 0, 0)),
+        out_shape=jax.ShapeDtypeStruct((ranks * slots, PAGE, 2 * KVW), jnp.bfloat16),
+        compiler_params=SMALL_PARAMS,
         cost_estimate=small_cost(1 << 18),
         name="arrange",
     )(sec.reshape(1), me.reshape(1), kept, crossed, routed)
@@ -576,19 +569,20 @@
     for code in range(ranks - 2, 0, -2):
         merging[code] = attend_to(code, last, True)
         last = merging[code][1:]
-    direct = attend_to(1, last, False)
-    both, token = stack(routed, [kept, direct])
+    waiting = attend_to(1, last, True)
+    both, token = stack(routed, [kept, waiting[1]])
     bit = 2
     while bit < ranks:
         for code in range(ranks - bit, 0, -2 * bit):
             last = [close(merging[code], taken[code], [token], ranks)]
             send(last[0], code, bit)
         bit *= 2
+    direct = close(waiting, [], last, ranks)
     crossed = handed_on(both)
-    own = attend_to(0, last, True)
-    handed, token = arrange(sec, me, kept, crossed, both)
-    taken[0].append(swapped(direct, 1))
-    attended = close(own, taken[0], [token], ranks, is_last=True)[None]
+    own = attend_to(0, [direct], True)
+    handed = arrange(sec, me, kept, crossed, both)
+    taken[0].insert(0, swapped(direct, 1))
+    attended = close(after(own, handed), taken[0], [], ranks, is_last=True)[None]
     return (attended, handed[None])
 
 

time: 98.6 us -> 99.5 us (level)
  waiting for transfers between devices: 31.5 us -> 36 us
  Pallas kernels: 35.8 us -> 34.4 us
  local copies, waits for them, and re-layouts: 3.61 us -> 2.23 us
    ppermute x3, waiting for transfers between devices: 19.5 us -> 23.9 us  [swapped(): return lax.ppermute(value, 'rank', [(i, i ^ bit) for i in range(ranks)])]
    pallas_call x1, Pallas kernels: 3.37 us -> 1.88 us  [arrange(): pl.pallas_call(arrange_kernel, grid=(ranks,), in_specs=[pl.BlockSpec(memo...]
    unnamed x28 -> x22, local copies, waits for them, and re-layouts: 3.61 us -> 2.23 us
    pallas_call x2 -> x3, Pallas kernels: 1.98 us -> 2.37 us  [close(): pl.pallas_call(functools.partial(close_kernel, is_last, len(received)), g...]
  transfers between devices with their start and end apart: 12 -> 12, of which waited for: 6 -> 5; matrix products, arithmetic and copies ran while one was open for 2% -> 2% of each run, Pallas kernels for 27% -> 25%
where the time goes in v5:
time: 99.5 us; the launch traced here: 99.3 us
  waiting for transfers between devices  36 us (36%)
  Pallas kernels  34.4 us (35%)
  starting transfers between devices  22.9 us (23%)
  local copies, waits for them, and re-layouts  2.23 us (2%)
  other arithmetic  2.22 us (2%)
  between operations  1.57 us (2%)
    ppermute x3, waiting for transfers between devices, swapped(): return lax.ppermute(value, 'rank', [(i, i ^ bit) for i in range(ranks)])  23.9 us
    pallas_call x4, Pallas kernels, attend(): pl.pallas_call(functools.partial(attend_kernel, is_open, len(earlier)), g...  18.8 us
    ppermute x6, starting transfers between devices, shifted(): lax.ppermute(value, 'rank', [(i, (i + k) % ranks) for i in range(ranks)])  12.7 us
    ppermute x3, waiting for transfers between devices, handed_on(): lax.ppermute(value, 'sec', [(i, (i + 1) % secs) for i in range(secs)])  9.09 us
    pallas_call x1, Pallas kernels, project(): pl.pallas_call(functools.partial(project_kernel, ranks), in_specs=[smem,...  7.13 us
    ppermute x3, starting transfers between devices, swapped(): return lax.ppermute(value, 'rank', [(i, i ^ bit) for i in range(ranks)])  6.56 us
    ppermute x3, starting transfers between devices, handed_on(): lax.ppermute(value, 'sec', [(i, (i + 1) % secs) for i in range(secs)])  3.65 us
    ppermute x6, waiting for transfers between devices, shifted(): lax.ppermute(value, 'rank', [(i, (i + k) % ranks) for i in range(ranks)])  3.01 us
  transfers between devices with their start and end apart: 12, of which 5 were waited for; matrix products, arithmetic and copies ran while one was open for 2% of the time, Pallas kernels for 25%

profile of v5, /device:TPU:0, one launch (start us, length us, event | category | flops | bytes accessed | tf_op | source)
XLA Modules:
  0.0 99.3 jit_solution(16106649134025781365)
XLA Ops:
  0.6 0.0 copy-start.8
  0.6 0.0 copy-start.9
  0.7 0.0 copy-start.2
  0.7 0.0 copy-start.7
  0.7 7.1 %project.1 = (f32[32,2048]{1,0:T(8,128)}, f32[32,2048]{1,0:T(8,128)}, f32[32,2048]{1,0:T(8,128)}, f32[32,2048]{1,0:T(8,128)}, bf16[8,16,2048]{2,1,0:T(8,128)(2,1...) custom-call(s32[1]{0:T(128)} %bitcast.1.rank_ref, ...), custom_call_target="tpu_custom_call" | custom-call | flops 1048576 | bytes 65536 | tf_op jit(solution)/shard_map/project/pallas_call | solution.py:143
  7.8 3.1 %collective-permute-start = (f32[32,2048]{1,0:T(8,128)}, f32[32,2048]{1,0:T(8,128)S(1)}, u32[]{:S(2)}, u32[]{:S(2)}) collective-permute-start(f32[32,2048]{1,0:T(8,128)} %get-tuple-element.40), channel_id=1, source_target_pairs={{0,1},{1,2},{2,3},{3,0},{4,5},{5,6},{6,7},{7,4},{8,9},{9,10},{10,1... | collective-permute-start | bytes 786440 | tf_op jit(solution)/shard_map/ppermute | solution.py:530
  10.9 2.6 %collective-permute-start.1 = (f32[32,2048]{1,0:T(8,128)}, f32[32,2048]{1,0:T(8,128)S(1)}, u32[]{:S(2)}, u32[]{:S(2)}) collective-permute-start(f32[32,2048]{1,0:T(8,128)} %get-tuple-element.41), channel_id=1, source_target_pairs={{0,2},{1,3},{2,0},{3,1},{4,6},{5,7},{6,4},{7,5},{8,10},{9,11},{10,... | collective-permute-start | bytes 786440 | tf_op jit(solution)/shard_map/ppermute | solution.py:530
  13.5 1.3 %collective-permute-start.2 = (f32[32,2048]{1,0:T(8,128)}, f32[32,2048]{1,0:T(8,128)}, u32[]{:S(2)}, u32[]{:S(2)}) collective-permute-start(f32[32,2048]{1,0:T(8,128)} %get-tuple-element.42), channel_id=1, source_target_pairs={{0,3},{1,0},{2,1},{3,2},{4,7},{5,4},{6,5},{7,6},{8,11},{9,8},{10,9... | collective-permute-start | bytes 786440 | tf_op jit(solution)/shard_map/ppermute | solution.py:530
  14.8 1.5 %collective-permute-start.3 = (bf16[3,8,16,1024]{3,2,1,0:T(8,128)(2,1)}, bf16[3,8,16,1024]{3,2,1,0:T(8,128)(2,1)S(1)}, u32[]{:S(2)}, u32[]{:S(2)}) collective-permute-start(bf16[3,8,16,1024]{3,2,1,0:T(8,128)(2,1)} %get-tuple-element.50), channel_id=1, source_target_pairs={{0,16},{16,0},{1,17},{17,1},{2,18},{18,2},{3,19},{19,3},{4,20},{20... | collective-permute-start | bytes 2359304 | tf_op jit(solution)/shard_map/ppermute | solution.py:536
  17.0 0.0 copy-done.8
  17.0 0.0 copy-done.9
  17.0 1.9 %fusion = (f32[1024,128]{1,0:T(8,128)S(1)}, f32[1024,128]{1,0:T(8,128)S(1)}) fusion(f32[128]{0:T(128)S(1)} %copy-done.8, f32[128]{0:T(128)S(1)} %copy-done.9, f32[1024]{0:T(1024)S(1)} %add_convert_fusion), kind=kLoop, calls=%fused_computation.2 | loop fusion | flops 262144 | bytes 1053696 | tf_op jit(solution)/shard_map/mul | solution.py:53
  18.9 0.3 fusion.1
  19.2 0.0 copy-done.2
  19.3 0.0 copy-done.7
  19.3 0.0 copy-start
  19.3 2.2 %copy-done = bf16[1,1024,2048]{2,1,0:T(8,128)(2,1)S(1)} copy-done((bf16[1,1024,2048]{2,1,0:T(8,128)(2,1)S(1)}, bf16[1,1024,2048]{2,1,0:T(8,128)(2,1)}, u32[]{:S(2)}) %copy-start) | copy-done | bytes 4194328
  21.5 0.0 copy-start.4
  21.5 0.0 copy-start.5
  21.5 0.0 copy-start.6
  21.5 0.0 copy-start.3
  21.5 0.0 copy-start.1
  21.5 2.9 %prepare.1 = (bf16[8192,128]{1,0:T(8,128)(2,1)S(1)}, bf16[8,1024,128]{2,1,0:T(8,128)(2,1)S(1)}) custom-call(bf16[128,8192]{1,0:T(8,128)(2,1)S(1)} %bitcast.22, bf16[1024,2048]{1,0:T(8,128)(2,1)S(1)} %bitcast.17, f32[1,1024]{1,0:T(1,128)S(1)} %bitcast.23, f32[128,128]{1,0:T(8,128)S(1)} %get-tuple-element.79.qc_ref, f32[128,128]{1,0:T(8,128)S(1)} %get-tuple-element.78.qs_ref, ...), custom_call_target="tpu_custom_call" | custom-call | flops 1073741824 | bytes 65536 | tf_op jit(solution)/shard_map/prepare/pallas_call | solution.py:175
  24.4 0.0 copy-start.10
  24.4 9.1 %collective-permute-done.3.refs_3_ = bf16[3,8,16,1024]{3,2,1,0:T(8,128)(2,1)S(1)} collective-permute-done((bf16[3,8,16,1024]{3,2,1,0:T(8,128)(2,1)}, bf16[3,8,16,1024]{3,2,1,0:T(8,128)(2,1)S(1)}, u32[]{:S(2)}, u32[]{:S(2)}) %collective-permute-start.3) | collective-permute-done | bytes 786464 | tf_op jit(solution)/shard_map/ppermute | solution.py:536
  33.5 0.0 copy-done.4
  33.5 0.0 copy-done.5
  33.5 0.0 copy-done.6
  33.5 0.1 choose.1
  33.6 0.0 collective-permute-done.refs_1_
  33.6 0.0 collective-permute-done.1.refs_2_
  33.6 0.0 collective-permute-done.2.refs_3_
  33.6 0.0 copy-done.3
  33.7 1.1 %gather.1 = (bf16[8,32,128]{2,1,0:T(8,128)(2,1)S(1)}, bf16[8,32,128]{2,1,0:T(8,128)(2,1)S(1)}) custom-call(s32[1]{0:T(128)} %bitcast.1.rank_ref, f32[128,128]{1,0:T(8,128)S(1)} %get-tuple-element.79.qc_ref, f32[128,128]{1,0:T(8,128)S(1)} %get-tuple-element.78.qs_ref, f32[32,2048]{1,0:T(8,128)S(1)} %copy-done.3, f32[32,2048]{1,0:T(8,128)S(1)} %collective-permute-done.refs_1_, ...), custom_call_target="tpu_custom_call" | custom-call | flops 262144 | bytes 65536 | tf_op jit(solution)/shard_map/gather/pallas_call | solution.py:261
  34.7 0.0 copy-done.10
  34.8 1.6 %collective-permute-start.8 = (bf16[8,16,2048]{2,1,0:T(8,128)(2,1)S(1)}, bf16[8,16,2048]{2,1,0:T(8,128)(2,1)S(1)}, u32[]{:S(2)}, u32[]{:S(2)}) collective-permute-start(bf16[8,16,2048]{2,1,0:T(8,128)(2,1)S(1)} %copy-done.10), channel_id=1, source_target_pairs={{0,16},{16,0},{1,17},{17,1},{2,18},{18,2},{3,19},{19,3},{4,20},{20... | collective-permute-start | bytes 1572872 | tf_op jit(solution)/shard_map/ppermute | solution.py:536
  36.3 2.3 %collective-permute-start.6 = (bf16[8,16,1024]{2,1,0:T(8,128)(2,1)S(1)}, bf16[8,16,1024]{2,1,0:T(8,128)(2,1)S(1)}, u32[]{:S(2)}, u32[]{:S(2)}) collective-permute-start(bf16[8,16,1024]{2,1,0:T(8,128)(2,1)S(1)} %get-tuple-element.66), channel_id=1, source_target_pairs={{0,2},{1,3},{2,0},{3,1},{4,6},{5,7},{6,4},{7,5},{8,10},{9,11},{10,... | collective-permute-start | bytes 786440 | tf_op jit(solution)/shard_map/ppermute | solution.py:530
  38.6 3.4 %collective-permute-start.7 = (bf16[8,16,1024]{2,1,0:T(8,128)(2,1)S(1)}, bf16[8,16,1024]{2,1,0:T(8,128)(2,1)S(1)}, u32[]{:S(2)}, u32[]{:S(2)}) collective-permute-start(bf16[8,16,1024]{2,1,0:T(8,128)(2,1)S(1)} %get-tuple-element.67), channel_id=1, source_target_pairs={{0,3},{1,0},{2,1},{3,2},{4,7},{5,4},{6,5},{7,6},{8,11},{9,8},{10,9... | collective-permute-start | bytes 786440 | tf_op jit(solution)/shard_map/ppermute | solution.py:530
  42.0 0.0 collective-permute-start.5
  42.0 0.0 copy-done.1
  42.0 4.9 %attend.1.refs_0_ = s16[136,2048]{1,0:T(8,128)(2,1)S(1)} custom-call(s32[1]{0:T(128)} %bitcast.12.length_ref, s32[1]{0:T(128)} %bitcast.1.rank_ref, bf16[8192,128]{1,0:T(8,128)(2,1)S(1)} %get-tuple-element.45.q_ref, bf16[8,1024,128]{2,1,0:T(8,128)(2,1)S(1)} %get-tuple-element.46.k_ref, bf16[1024,2048]{1,0:T(8,128)(2,1)S(1)} %bitcast.18, ...), custom_call_target="tpu_custom_call" | custom-call | flops 268435456 | bytes 65536 | tf_op jit(solution)/shard_map/attend/pallas_call | solution.py:357
  46.9 1.2 %collective-permute-start.4 = (s16[136,2048]{1,0:T(8,128)(2,1)S(1)}, s16[136,2048]{1,0:T(8,128)(2,1)S(1)}, u32[]{:S(2)}, u32[]{:S(2)}) collective-permute-start(s16[136,2048]{1,0:T(8,128)(2,1)S(1)} %attend.1.refs_0_), channel_id=1, source_target_pairs={{0,1},{1,0},{2,3},{3,2},{4,5},{5,4},{6,7},{7,6},{8,9},{9,8},{10,11... | collective-permute-start | bytes 1671176 | tf_op jit(solution)/shard_map/ppermute | solution.py:533
  48.1 4.6 %attend_open.3 = (f32[2,128,1024]{2,1,0:T(8,128)S(1)}, f32[2,8,1024]{2,1,0:T(8,128)S(1)}) custom-call(s32[1]{0:T(128)} %bitcast.13.length_ref, s32[1]{0:T(128)} %bitcast.1.rank_ref, bf16[8192,128]{1,0:T(8,128)(2,1)S(1)} %get-tuple-element.45.q_ref, bf16[8,1024,128]{2,1,0:T(8,128)(2,1)S(1)} %get-tuple-element.46.k_ref, bf16[1024,2048]{1,0:T(8,128)(2,1)S(1)} %bitcast.19, ...), custom_call_target="tpu_custom_call" | custom-call | flops 268435456 | bytes 65536 | tf_op jit(solution)/shard_map/attend_open/pallas_call | solution.py:357
  52.8 4.7 %attend_open.4 = (f32[2,128,1024]{2,1,0:T(8,128)S(1)}, f32[2,8,1024]{2,1,0:T(8,128)S(1)}) custom-call(s32[1]{0:T(128)} %bitcast.14.length_ref, s32[1]{0:T(128)} %bitcast.1.rank_ref, bf16[8192,128]{1,0:T(8,128)(2,1)S(1)} %get-tuple-element.45.q_ref, bf16[8,1024,128]{2,1,0:T(8,128)(2,1)S(1)} %get-tuple-element.46.k_ref, bf16[1024,2048]{1,0:T(8,128)(2,1)S(1)} %bitcast.20, ...), custom_call_target="tpu_custom_call" | custom-call | flops 268435456 | bytes 65536 | tf_op jit(solution)/shard_map/attend_open/pallas_call | solution.py:357
  57.5 0.0 collective-permute-done.6.refs_1_
  57.5 0.0 collective-permute-done.7.refs_2_
  57.5 3.0 %collective-permute-done.5.refs_0_ = bf16[8,16,1024]{2,1,0:T(8,128)(2,1)S(1)} collective-permute-done((bf16[8,16,1024]{2,1,0:T(8,128)(2,1)S(1)}, bf16[8,16,1024]{2,1,0:T(8,128)(2,1)S(1)}, u32[]{:S(2)}, u32[]{:S(2)}) %collective-permute-start.5) | collective-permute-done | bytes 262176 | tf_op jit(solution)/shard_map/ppermute | solution.py:530
  60.5 0.0 collective-permute-done.8.refs_3_.kept_ref
  60.5 0.1 stack.1
  60.6 0.6 collective-permute-start.9
  61.2 6.8 %collective-permute-done.4.refs_0_ = s16[136,2048]{1,0:T(8,128)(2,1)S(1)} collective-permute-done((s16[136,2048]{1,0:T(8,128)(2,1)S(1)}, s16[136,2048]{1,0:T(8,128)(2,1)S(1)}, u32[]{:S(2)}, u32[]{:S(2)}) %collective-permute-start.4) | collective-permute-done | bytes 557088 | tf_op jit(solution)/shard_map/ppermute | solution.py:533
  68.0 0.6 close.2.refs_0_
  68.6 0.4 close.3.refs_0_
  69.0 1.9 %collective-permute-start.10 = (s16[136,2048]{1,0:T(8,128)(2,1)S(1)}, s16[136,2048]{1,0:T(8,128)(2,1)S(1)}, u32[]{:S(2)}, u32[]{:S(2)}) collective-permute-start(s16[136,2048]{1,0:T(8,128)(2,1)S(1)} %close.3.refs_0_), channel_id=1, source_target_pairs={{0,1},{1,0},{2,3},{3,2},{4,5},{5,4},{6,7},{7,6},{8,9},{9,8},{10,11... | collective-permute-start | bytes 1671176 | tf_op jit(solution)/shard_map/ppermute | solution.py:533
  70.9 3.5 %collective-permute-start.11 = (s16[136,2048]{1,0:T(8,128)(2,1)S(1)}, s16[136,2048]{1,0:T(8,128)(2,1)S(1)}, u32[]{:S(2)}, u32[]{:S(2)}) collective-permute-start(s16[136,2048]{1,0:T(8,128)(2,1)S(1)} %close.2.refs_0_), channel_id=1, source_target_pairs={{0,2},{1,3},{2,0},{3,1},{4,6},{5,7},{6,4},{7,5},{8,10},{9,11},{10,... | collective-permute-start | bytes 1671176 | tf_op jit(solution)/shard_map/ppermute | solution.py:533
  74.4 4.6 %attend_open.5 = (f32[2,128,1024]{2,1,0:T(8,128)S(1)}, f32[2,8,1024]{2,1,0:T(8,128)S(1)}) custom-call(s32[1]{0:T(128)} %bitcast.15.length_ref, s32[1]{0:T(128)} %bitcast.1.rank_ref, bf16[8192,128]{1,0:T(8,128)(2,1)S(1)} %get-tuple-element.45.q_ref, bf16[8,1024,128]{2,1,0:T(8,128)(2,1)S(1)} %get-tuple-element.46.k_ref, bf16[1024,2048]{1,0:T(8,128)(2,1)S(1)} %bitcast.21, ...), custom_call_target="tpu_custom_call" | custom-call | flops 268435456 | bytes 65536 | tf_op jit(solution)/shard_map/attend_open/pallas_call | solution.py:357
  79.0 0.0 collective-permute-done.9.crossed_ref
  79.0 1.9 %arrange.1 = bf16[32,16,2048]{2,1,0:T(8,128)(2,1)} custom-call(s32[1]{0:T(128)} %bitcast.8.sec_ref, s32[1]{0:T(128)} %bitcast.1.rank_ref, bf16[8,16,2048]{2,1,0:T(8,128)(2,1)S(1)} %collective-permute-done.8.refs_3_.kept_ref, bf16[3,8,16,1024]{3,2,1,0:T(8,128)(2,1)S(1)} %collective-permute-done.9.crossed_ref, ...), custom_call_target="tpu_custom_call" | custom-call | flops 262144 | bytes 65536 | tf_op jit(solution)/shard_map/arrange/pallas_call | solution.py:498
  80.9 13.6 %collective-permute-done.10.refs_0_ = s16[136,2048]{1,0:T(8,128)(2,1)S(1)} collective-permute-done((s16[136,2048]{1,0:T(8,128)(2,1)S(1)}, s16[136,2048]{1,0:T(8,128)(2,1)S(1)}, u32[]{:S(2)}, u32[]{:S(2)}) %collective-permute-start.10) | collective-permute-done | bytes 557088 | tf_op jit(solution)/shard_map/ppermute | solution.py:533
  94.5 3.4 %collective-permute-done.11.refs_1_ = s16[136,2048]{1,0:T(8,128)(2,1)S(1)} collective-permute-done((s16[136,2048]{1,0:T(8,128)(2,1)S(1)}, s16[136,2048]{1,0:T(8,128)(2,1)S(1)}, u32[]{:S(2)}, u32[]{:S(2)}) %collective-permute-start.11) | collective-permute-done | bytes 557088 | tf_op jit(solution)/shard_map/ppermute | solution.py:533
  97.9 1.4 %finish.1 = bf16[128,2048]{1,0:T(8,128)(2,1)} custom-call(f32[2,128,1024]{2,1,0:T(8,128)S(1)} %get-tuple-element.74.num_ref, f32[2,8,1024]{2,1,0:T(8,128)S(1)} %get-tuple-element.75.stat_ref, s16[136,2048]{1,0:T(8,128)(2,1)S(1)} %collective-permute-done.10.refs_0_, s16[136,2048]{1,0:T(8,128)(2,1)S(1)} %collective-permute-done.11.refs_1_), custom_call_target="tpu_custom_call" | custom-call | flops 262144 | bytes 65536 | tf_op jit(solution)/shard_map/finish/pallas_call | solution.py:402
  (2 shorter events, 0.0 us)
Async XLA Ops:
  0.6 16.4 %copy-start.8 = (f32[128]{0:T(128)S(1)}, f32[128]{0:T(128)}, u32[]{:S(2)}) copy-start(f32[128]{0:T(128)} %constant.24) | copy-start | bytes 1540
  0.6 16.4 %copy-start.9 = (f32[128]{0:T(128)S(1)}, f32[128]{0:T(128)}, u32[]{:S(2)}) copy-start(f32[128]{0:T(128)} %constant.16.clone) | copy-start | bytes 1540
  0.7 18.6 %copy-start.2 = (bf16[1,128,8192]{2,1,0:T(8,128)(2,1)S(1)}, bf16[1,128,8192]{2,1,0:T(8,128)(2,1)}, u32[]{:S(2)}) copy-start(bf16[1,128,8192]{2,1,0:T(8,128)(2,1)} %param.12) | copy-start | bytes 6291460
  0.7 18.6 %copy-start.7 = (f32[1024]{0:T(1024)S(1)}, f32[1024]{0:T(1024)}, u32[]{:S(2)}) copy-start(f32[1024]{0:T(1024)} %param.14) | copy-start | bytes 12292
  7.8 25.8 %collective-permute-start = (f32[32,2048]{1,0:T(8,128)}, f32[32,2048]{1,0:T(8,128)S(1)}, u32[]{:S(2)}, u32[]{:S(2)}) collective-permute-start(f32[32,2048]{1,0:T(8,128)} %get-tuple-element.40), channel_id=1, source_target_pairs={{0,1},{1,2},{2,3},{3,0},{4,5},{5,6},{6,7},{7,4},{8,9},{9,10},{10,1... | collective-permute-start | bytes 786440 | tf_op jit(solution)/shard_map/ppermute | solution.py:530
  10.9 22.7 %collective-permute-start.1 = (f32[32,2048]{1,0:T(8,128)}, f32[32,2048]{1,0:T(8,128)S(1)}, u32[]{:S(2)}, u32[]{:S(2)}) collective-permute-start(f32[32,2048]{1,0:T(8,128)} %get-tuple-element.41), channel_id=1, source_target_pairs={{0,2},{1,3},{2,0},{3,1},{4,6},{5,7},{6,4},{7,5},{8,10},{9,11},{10,... | collective-permute-start | bytes 786440 | tf_op jit(solution)/shard_map/ppermute | solution.py:530
  13.5 20.1 %collective-permute-start.2 = (f32[32,2048]{1,0:T(8,128)}, f32[32,2048]{1,0:T(8,128)}, u32[]{:S(2)}, u32[]{:S(2)}) collective-permute-start(f32[32,2048]{1,0:T(8,128)} %get-tuple-element.42), channel_id=1, source_target_pairs={{0,3},{1,0},{2,1},{3,2},{4,7},{5,4},{6,5},{7,6},{8,11},{9,8},{10,9... | collective-permute-start | bytes 786440 | tf_op jit(solution)/shard_map/ppermute | solution.py:530
  14.8 18.6 %collective-permute-start.3 = (bf16[3,8,16,1024]{3,2,1,0:T(8,128)(2,1)}, bf16[3,8,16,1024]{3,2,1,0:T(8,128)(2,1)S(1)}, u32[]{:S(2)}, u32[]{:S(2)}) collective-permute-start(bf16[3,8,16,1024]{3,2,1,0:T(8,128)(2,1)} %get-tuple-element.50), channel_id=1, source_target_pairs={{0,16},{16,0},{1,17},{17,1},{2,18},{18,2},{3,19},{19,3},{4,20},{20... | collective-permute-start | bytes 2359304 | tf_op jit(solution)/shard_map/ppermute | solution.py:536
  19.3 2.2 %copy-start = (bf16[1,1024,2048]{2,1,0:T(8,128)(2,1)S(1)}, bf16[1,1024,2048]{2,1,0:T(8,128)(2,1)}, u32[]{:S(2)}) copy-start(bf16[1,1024,2048]{2,1,0:T(8,128)(2,1)} %param.13) | copy-start | bytes 12582916
  21.5 12.0 %copy-start.4 = (bf16[8,16,1024]{2,1,0:T(8,128)(2,1)S(1)}, bf16[8,16,1024]{2,1,0:T(8,128)(2,1)}, u32[]{:S(2)}) copy-start(bf16[8,16,1024]{2,1,0:T(8,128)(2,1)} %get-tuple-element.47.refs_0_) | copy-start | bytes 786436
  21.5 12.0 %copy-start.5 = (bf16[8,16,1024]{2,1,0:T(8,128)(2,1)S(1)}, bf16[8,16,1024]{2,1,0:T(8,128)(2,1)}, u32[]{:S(2)}) copy-start(bf16[8,16,1024]{2,1,0:T(8,128)(2,1)} %get-tuple-element.48.refs_1_) | copy-start | bytes 786436
  21.5 12.0 %copy-start.6 = (bf16[8,16,1024]{2,1,0:T(8,128)(2,1)S(1)}, bf16[8,16,1024]{2,1,0:T(8,128)(2,1)}, u32[]{:S(2)}) copy-start(bf16[8,16,1024]{2,1,0:T(8,128)(2,1)} %get-tuple-element.49.refs_2_) | copy-start | bytes 786436
  21.5 12.2 %copy-start.3 = (f32[32,2048]{1,0:T(8,128)S(1)}, f32[32,2048]{1,0:T(8,128)}, u32[]{:S(2)}) copy-start(f32[32,2048]{1,0:T(8,128)} %get-tuple-element.55.refs_0_) | copy-start | bytes 786436
  21.5 20.6 %copy-start.1 = (bf16[1,1024,2048]{2,1,0:T(8,128)(2,1)S(1)}, bf16[1,1024,2048]{2,1,0:T(8,128)(2,1)}, u32[]{:S(2)}) copy-start(bf16[1,1024,2048]{2,1,0:T(8,128)(2,1)} %param.13) | copy-start | bytes 12582916
  24.4 10.4 %copy-start.10 = (bf16[8,16,2048]{2,1,0:T(8,128)(2,1)S(1)}, bf16[8,16,2048]{2,1,0:T(8,128)(2,1)}, u32[]{:S(2)}) copy-start(bf16[8,16,2048]{2,1,0:T(8,128)(2,1)} %get-tuple-element.69) | copy-start | bytes 1572868
  34.8 25.7 %collective-permute-start.8 = (bf16[8,16,2048]{2,1,0:T(8,128)(2,1)S(1)}, bf16[8,16,2048]{2,1,0:T(8,128)(2,1)S(1)}, u32[]{:S(2)}, u32[]{:S(2)}) collective-permute-start(bf16[8,16,2048]{2,1,0:T(8,128)(2,1)S(1)} %copy-done.10), channel_id=1, source_target_pairs={{0,16},{16,0},{1,17},{17,1},{2,18},{18,2},{3,19},{19,3},{4,20},{20... | collective-permute-start | bytes 1572872 | tf_op jit(solution)/shard_map/ppermute | solution.py:536
  36.3 21.2 %collective-permute-start.6 = (bf16[8,16,1024]{2,1,0:T(8,128)(2,1)S(1)}, bf16[8,16,1024]{2,1,0:T(8,128)(2,1)S(1)}, u32[]{:S(2)}, u32[]{:S(2)}) collective-permute-start(bf16[8,16,1024]{2,1,0:T(8,128)(2,1)S(1)} %get-tuple-element.66), channel_id=1, source_target_pairs={{0,2},{1,3},{2,0},{3,1},{4,6},{5,7},{6,4},{7,5},{8,10},{9,11},{10,... | collective-permute-start | bytes 786440 | tf_op jit(solution)/shard_map/ppermute | solution.py:530
  38.6 18.8 %collective-permute-start.7 = (bf16[8,16,1024]{2,1,0:T(8,128)(2,1)S(1)}, bf16[8,16,1024]{2,1,0:T(8,128)(2,1)S(1)}, u32[]{:S(2)}, u32[]{:S(2)}) collective-permute-start(bf16[8,16,1024]{2,1,0:T(8,128)(2,1)S(1)} %get-tuple-element.67), channel_id=1, source_target_pairs={{0,3},{1,0},{2,1},{3,2},{4,7},{5,4},{6,5},{7,6},{8,11},{9,8},{10,9... | collective-permute-start | bytes 786440 | tf_op jit(solution)/shard_map/ppermute | solution.py:530
  42.0 18.5 %collective-permute-start.5 = (bf16[8,16,1024]{2,1,0:T(8,128)(2,1)S(1)}, bf16[8,16,1024]{2,1,0:T(8,128)(2,1)S(1)}, u32[]{:S(2)}, u32[]{:S(2)}) collective-permute-start(bf16[8,16,1024]{2,1,0:T(8,128)(2,1)S(1)} %get-tuple-element.61.refs_0_), channel_id=1, source_target_pairs={{0,1},{1,2},{2,3},{3,0},{4,5},{5,6},{6,7},{7,4},{8,9},{9,10},{10,1... | collective-permute-start | bytes 786440 | tf_op jit(solution)/shard_map/ppermute | solution.py:530
  46.9 21.1 %collective-permute-start.4 = (s16[136,2048]{1,0:T(8,128)(2,1)S(1)}, s16[136,2048]{1,0:T(8,128)(2,1)S(1)}, u32[]{:S(2)}, u32[]{:S(2)}) collective-permute-start(s16[136,2048]{1,0:T(8,128)(2,1)S(1)} %attend.1.refs_0_), channel_id=1, source_target_pairs={{0,1},{1,0},{2,3},{3,2},{4,5},{5,4},{6,7},{7,6},{8,9},{9,8},{10,11... | collective-permute-start | bytes 1671176 | tf_op jit(solution)/shard_map/ppermute | solution.py:533
  60.6 18.4 %collective-permute-start.9 = (bf16[3,8,16,1024]{3,2,1,0:T(8,128)(2,1)S(1)}, bf16[3,8,16,1024]{3,2,1,0:T(8,128)(2,1)S(1)}, u32[]{:S(2)}, u32[]{:S(2)}) collective-permute-start(bf16[3,8,16,1024]{3,2,1,0:T(8,128)(2,1)S(1)} %get-tuple-element.73.routed_ref), channel_id=1, source_target_pairs={{0,16},{16,0},{1,17},{17,1},{2,18},{18,2},{3,19},{19,3},{4,20},{20... | collective-permute-start | bytes 2359304 | tf_op jit(solution)/shard_map/ppermute | solution.py:536
  69.0 25.5 %collective-permute-start.10 = (s16[136,2048]{1,0:T(8,128)(2,1)S(1)}, s16[136,2048]{1,0:T(8,128)(2,1)S(1)}, u32[]{:S(2)}, u32[]{:S(2)}) collective-permute-start(s16[136,2048]{1,0:T(8,128)(2,1)S(1)} %close.3.refs_0_), channel_id=1, source_target_pairs={{0,1},{1,0},{2,3},{3,2},{4,5},{5,4},{6,7},{7,6},{8,9},{9,8},{10,11... | collective-permute-start | bytes 1671176 | tf_op jit(solution)/shard_map/ppermute | solution.py:533
  70.9 27.0 %collective-permute-start.11 = (s16[136,2048]{1,0:T(8,128)(2,1)S(1)}, s16[136,2048]{1,0:T(8,128)(2,1)S(1)}, u32[]{:S(2)}, u32[]{:S(2)}) collective-permute-start(s16[136,2048]{1,0:T(8,128)(2,1)S(1)} %close.2.refs_0_), channel_id=1, source_target_pairs={{0,2},{1,3},{2,0},{3,1},{4,6},{5,7},{6,4},{7,5},{8,10},{9,11},{10,... | collective-permute-start | bytes 1671176 | tf_op jit(solution)/shard_map/ppermute | solution.py:533

commit v6 on v5

--- a/solution.py
+++ b/solution.py
@@ -335,7 +335,7 @@
     return [pl.BlockSpec((1, HD, cols), place), pl.BlockSpec((1, 8, cols), place)]
 
 
-def attend(length, me, code, queries, keys, cache, fresh, earlier, ranks, is_open):
+def attend(length, me, code, queries, keys, cache, fresh, earlier, ranks, is_open, cost):
     pieces, heads, cols, share = layout(ranks)
 
     def piece(j, rank_ref):
@@ -372,7 +372,7 @@
         ),
         out_shape=out_shape,
         compiler_params=ATTEND_PARAMS,
-        cost_estimate=small_cost(1 << 28),
+        cost_estimate=small_cost(cost),
         name="attend_open" if is_open else "attend",
     )(length, me, queries, keys, cache, *fresh, *earlier)
 
@@ -444,37 +444,9 @@
     )(sec.reshape(1), *near, there)
 
 
-def stack_kernel(count, *refs):
-    out_ref, token_ref, sems = refs[-3:]
-    token_ref[...] = jnp.zeros_like(token_ref)
-    copies = [
-        pltpu.make_async_copy(ref, out_ref.at[k], sems.at[k]) for k, ref in enumerate(refs[:count])
-    ]
-    for c in copies:
-        c.start()
-    for c in copies:
-        c.wait()
-
-
-def stack(values, earlier):
-    count = len(values)
-    return pl.pallas_call(
-        functools.partial(stack_kernel, count),
-        in_specs=[pl.BlockSpec(memory_space=pl.ANY)] * (count + len(earlier)),
-        out_specs=[pl.BlockSpec(memory_space=pltpu.VMEM)] * 2,
-        out_shape=[
-            jax.ShapeDtypeStruct((count,) + values[0].shape, values[0].dtype),
-            jax.ShapeDtypeStruct((8, 128), jnp.float32),
-        ],
-        scratch_shapes=[pltpu.SemaphoreType.DMA((count,))],
-        compiler_params=SMALL_PARAMS,
-        cost_estimate=small_cost(1 << 32),
-        name="stack",
-    )(*values, *earlier)
-
-
-def arrange_kernel(sec_ref, rank_ref, kept_ref, crossed_ref, routed_ref, out_ref):
-    count = crossed_ref.shape[0]
+def arrange_kernel(sec_ref, rank_ref, kept_ref, *refs):
+    count = (len(refs) - 2) // 2
+    crossed, routed, out_ref = refs[:count], refs[count:2 * count], refs[-1]
     shift = lax.rem(rank_ref[0] - pl.program_id(0) + count + 1, count + 1)
     second = sec_ref[0] > 0
 
@@ -486,31 +458,29 @@
     def _():
         out_ref[...] = kept_ref[...]
 
-    @pl.when(jnp.logical_and(second, shift > 0))
-    def _():
-        out_ref[:, :, :KVW] = crossed_ref[shift - 1]
-        out_ref[:, :, KVW:] = routed_ref[shift - 1]
-
-
-def arrange(sec, me, kept, crossed, routed):
-    ranks = crossed.shape[0] + 1
+    for k in range(count):
+        @pl.when(jnp.logical_and(second, shift == k + 1))
+        def _():
+            out_ref[:, :, :KVW] = crossed[k][...]
+            out_ref[:, :, KVW:] = routed[k][...]
+
+
+def arrange(sec, me, kept, crossed, routed, earlier):
+    ranks = len(crossed) + 1
     slots = kept.shape[0]
+    smem = pl.BlockSpec(memory_space=pltpu.SMEM)
     return pl.pallas_call(
         arrange_kernel,
         grid=(ranks,),
-        in_specs=[
-            pl.BlockSpec(memory_space=pltpu.SMEM),
-            pl.BlockSpec(memory_space=pltpu.SMEM),
-            pl.BlockSpec(kept.shape, lambda j: (0, 0, 0)),
-            pl.BlockSpec(crossed.shape, lambda j: (0, 0, 0, 0)),
-            pl.BlockSpec(routed.shape, lambda j: (0, 0, 0, 0)),
-        ],
+        in_specs=[smem, smem]
+        + [pl.BlockSpec(v.shape, lambda j: (0, 0, 0)) for v in [kept, *crossed, *routed]]
+        + [pl.BlockSpec(memory_space=pl.ANY)],
         out_specs=pl.BlockSpec((slots, PAGE, 2 * KVW), lambda j: (j, 0, 0)),
         out_shape=jax.ShapeDtypeStruct((ranks * slots, PAGE, 2 * KVW), jnp.bfloat16),
         compiler_params=SMALL_PARAMS,
         cost_estimate=small_cost(1 << 18),
         name="arrange",
-    )(sec.reshape(1), me.reshape(1), kept, crossed, routed)
+    )(sec.reshape(1), me.reshape(1), kept, *crossed, *routed, earlier)
 
 
 def after(value, earlier):
@@ -551,9 +521,9 @@
     fresh = gather(me, q_tables, arrived)
     kept = handed_on(after(kept, fresh))
 
-    def attend_to(code, earlier, is_open):
+    def attend_to(code, earlier, is_open, cost=1 << 28):
         return attend(
-            lengths[0], me.reshape(1), code, q_rot, keys, cache, fresh, earlier, ranks, is_open
+            lengths[0], me.reshape(1), code, q_rot, keys, cache, fresh, earlier, ranks, is_open, cost
         )
 
     taken = {code: [] for code in range(ranks)}
@@ -569,18 +539,17 @@
     for code in range(ranks - 2, 0, -2):
         merging[code] = attend_to(code, last, True)
         last = merging[code][1:]
-    waiting = attend_to(1, last, True)
-    both, token = stack(routed, [kept, waiting[1]])
+    waiting = attend_to(1, [*routed[::2], *last], True, 1 << 32)
+    last = waiting[1:]
     bit = 2
     while bit < ranks:
         for code in range(ranks - bit, 0, -2 * bit):
-            last = [close(merging[code], taken[code], [token], ranks)]
+            last = [close(merging[code], taken[code], last, ranks)]
             send(last[0], code, bit)
         bit *= 2
-    direct = close(waiting, [], last, ranks)
-    crossed = handed_on(both)
+    direct = close(waiting, [], [*last, *routed[1::2]], ranks)
     own = attend_to(0, [direct], True)
-    handed = arrange(sec, me, kept, crossed, both)
+    handed = arrange(sec, me, kept, [handed_on(r) for r in routed], routed, own[1])
     taken[0].insert(0, swapped(direct, 1))
     attended = close(after(own, handed), taken[0], [], ranks, is_last=True)[None]
     return (attended, handed[None])

time: 99.5 us -> 97.9 us (0.984)
  waiting for transfers between devices: 36 us -> 32 us
  starting transfers between devices: 22.9 us -> 25.4 us
    ppermute x3, waiting for transfers between devices: 23.9 us -> 10.9 us  [swapped(): return lax.ppermute(value, 'rank', [(i, i ^ bit) for i in range(ranks)])]
    ppermute x3 -> x5, waiting for transfers between devices: 9.09 us -> 15.2 us  [handed_on(): lax.ppermute(value, 'sec', [(i, (i + 1) % secs) for i in range(secs)])]
    ppermute x6, waiting for transfers between devices: 3.01 us -> 5.92 us  [shifted(): lax.ppermute(value, 'rank', [(i, (i + k) % ranks) for i in range(ranks)])]
    ppermute x3 -> x5, starting transfers between devices: 3.65 us -> 6.1 us  [handed_on(): lax.ppermute(value, 'sec', [(i, (i + 1) % secs) for i in range(secs)])]
    ppermute x3, starting transfers between devices: 6.56 us -> 5.15 us  [swapped(): return lax.ppermute(value, 'rank', [(i, i ^ bit) for i in range(ranks)])]
    ppermute x6, starting transfers between devices: 12.7 us -> 14.1 us  [shifted(): lax.ppermute(value, 'rank', [(i, (i + k) % ranks) for i in range(ranks)])]
  transfers between devices with their start and end apart: 12 -> 14, of which waited for: 5 -> 9; matrix products, arithmetic and copies ran while one was open for 2% -> 2% of each run, Pallas kernels for 25% -> 26%
where the time goes in v6:
time: 97.9 us; the launch traced here: 97.7 us
  Pallas kernels  34.3 us (35%)
  waiting for transfers between devices  32 us (33%)
  starting transfers between devices  25.4 us (26%)
  local copies, waits for them, and re-layouts  2.23 us (2%)
  other arithmetic  2.22 us (2%)
  between operations  1.54 us (2%)
    pallas_call x4, Pallas kernels, attend(): pl.pallas_call(functools.partial(attend_kernel, is_open, len(earlier)), g...  18.8 us
    ppermute x5, waiting for transfers between devices, handed_on(): lax.ppermute(value, 'sec', [(i, (i + 1) % secs) for i in range(secs)])  15.2 us
    ppermute x6, starting transfers between devices, shifted(): lax.ppermute(value, 'rank', [(i, (i + k) % ranks) for i in range(ranks)])  14.1 us
    ppermute x3, waiting for transfers between devices, swapped(): return lax.ppermute(value, 'rank', [(i, i ^ bit) for i in range(ranks)])  10.9 us
    pallas_call x1, Pallas kernels, project(): pl.pallas_call(functools.partial(project_kernel, ranks), in_specs=[smem,...  7.13 us
    ppermute x5, starting transfers between devices, handed_on(): lax.ppermute(value, 'sec', [(i, (i + 1) % secs) for i in range(secs)])  6.1 us
    ppermute x6, waiting for transfers between devices, shifted(): lax.ppermute(value, 'rank', [(i, (i + k) % ranks) for i in range(ranks)])  5.92 us
    ppermute x3, starting transfers between devices, swapped(): return lax.ppermute(value, 'rank', [(i, i ^ bit) for i in range(ranks)])  5.15 us
  transfers between devices with their start and end apart: 14, of which 9 were waited for; matrix products, arithmetic and copies ran while one was open for 2% of the time, Pallas kernels for 26%

profile of v6, /device:TPU:0, one launch (start us, length us, event | category | flops | bytes accessed | tf_op | source)
XLA Modules:
  0.0 97.7 jit_solution(17104365565145368352)
XLA Ops:
  0.6 0.0 copy-start.8
  0.6 0.0 copy-start.9
  0.7 0.0 copy-start.2
  0.7 0.0 copy-start.7
  0.7 7.1 %project.1 = (f32[32,2048]{1,0:T(8,128)}, f32[32,2048]{1,0:T(8,128)}, f32[32,2048]{1,0:T(8,128)}, f32[32,2048]{1,0:T(8,128)}, bf16[8,16,2048]{2,1,0:T(8,128)(2,1...) custom-call(s32[1]{0:T(128)} %bitcast.1.rank_ref, ...), custom_call_target="tpu_custom_call" | custom-call | flops 1048576 | bytes 65536 | tf_op jit(solution)/shard_map/project/pallas_call | solution.py:143
  7.8 3.0 %collective-permute-start.3 = (bf16[3,8,16,1024]{3,2,1,0:T(8,128)(2,1)}, bf16[3,8,16,1024]{3,2,1,0:T(8,128)(2,1)S(1)}, u32[]{:S(2)}, u32[]{:S(2)}) collective-permute-start(bf16[3,8,16,1024]{3,2,1,0:T(8,128)(2,1)} %get-tuple-element.48), channel_id=1, source_target_pairs={{0,16},{16,0},{1,17},{17,1},{2,18},{18,2},{3,19},{19,3},{4,20},{20... | collective-permute-start | bytes 2359304 | tf_op jit(solution)/shard_map/ppermute | solution.py:506
  10.8 1.6 %collective-permute-start = (f32[32,2048]{1,0:T(8,128)}, f32[32,2048]{1,0:T(8,128)S(1)}, u32[]{:S(2)}, u32[]{:S(2)}) collective-permute-start(f32[32,2048]{1,0:T(8,128)} %get-tuple-element.38), channel_id=1, source_target_pairs={{0,1},{1,2},{2,3},{3,0},{4,5},{5,6},{6,7},{7,4},{8,9},{9,10},{10,1... | collective-permute-start | bytes 786440 | tf_op jit(solution)/shard_map/ppermute | solution.py:500
  12.4 2.6 %collective-permute-start.1 = (f32[32,2048]{1,0:T(8,128)}, f32[32,2048]{1,0:T(8,128)S(1)}, u32[]{:S(2)}, u32[]{:S(2)}) collective-permute-start(f32[32,2048]{1,0:T(8,128)} %get-tuple-element.39), channel_id=1, source_target_pairs={{0,2},{1,3},{2,0},{3,1},{4,6},{5,7},{6,4},{7,5},{8,10},{9,11},{10,... | collective-permute-start | bytes 786440 | tf_op jit(solution)/shard_map/ppermute | solution.py:500
  15.0 1.3 %collective-permute-start.2 = (f32[32,2048]{1,0:T(8,128)}, f32[32,2048]{1,0:T(8,128)}, u32[]{:S(2)}, u32[]{:S(2)}) collective-permute-start(f32[32,2048]{1,0:T(8,128)} %get-tuple-element.40), channel_id=1, source_target_pairs={{0,3},{1,0},{2,1},{3,2},{4,7},{5,4},{6,5},{7,6},{8,11},{9,8},{10,9... | collective-permute-start | bytes 786440 | tf_op jit(solution)/shard_map/ppermute | solution.py:500
  17.0 0.0 copy-done.8
  17.0 0.0 copy-done.9
  17.0 1.9 %fusion = (f32[1024,128]{1,0:T(8,128)S(1)}, f32[1024,128]{1,0:T(8,128)S(1)}) fusion(f32[128]{0:T(128)S(1)} %copy-done.9, f32[128]{0:T(128)S(1)} %copy-done.8, f32[1024]{0:T(1024)S(1)} %add_convert_fusion), kind=kLoop, calls=%fused_computation.2 | loop fusion | flops 262144 | bytes 1053696 | tf_op jit(solution)/shard_map/mul | solution.py:53
  18.9 0.3 fusion.1
  19.3 0.0 copy-done.2
  19.3 0.0 copy-done.7
  19.3 0.0 copy-start
  19.3 2.2 %copy-done = bf16[1,1024,2048]{2,1,0:T(8,128)(2,1)S(1)} copy-done((bf16[1,1024,2048]{2,1,0:T(8,128)(2,1)S(1)}, bf16[1,1024,2048]{2,1,0:T(8,128)(2,1)}, u32[]{:S(2)}) %copy-start) | copy-done | bytes 4194328
  21.5 0.0 copy-start.4
  21.5 0.0 copy-start.5
  21.5 0.0 copy-start.6
  21.5 0.0 copy-start.3
  21.5 0.0 copy-start.1
  21.5 2.9 %prepare.1 = (bf16[8192,128]{1,0:T(8,128)(2,1)S(1)}, bf16[8,1024,128]{2,1,0:T(8,128)(2,1)S(1)}) custom-call(bf16[128,8192]{1,0:T(8,128)(2,1)S(1)} %bitcast.22, bf16[1024,2048]{1,0:T(8,128)(2,1)S(1)} %bitcast.17, f32[1,1024]{1,0:T(1,128)S(1)} %bitcast.23, f32[128,128]{1,0:T(8,128)S(1)} %get-tuple-element.75.qc_ref, f32[128,128]{1,0:T(8,128)S(1)} %get-tuple-element.74.qs_ref, ...), custom_call_target="tpu_custom_call" | custom-call | flops 1073741824 | bytes 65536 | tf_op jit(solution)/shard_map/prepare/pallas_call | solution.py:175
  24.4 4.2 %collective-permute-done.3.refs_3_ = bf16[3,8,16,1024]{3,2,1,0:T(8,128)(2,1)S(1)} collective-permute-done((bf16[3,8,16,1024]{3,2,1,0:T(8,128)(2,1)}, bf16[3,8,16,1024]{3,2,1,0:T(8,128)(2,1)S(1)}, u32[]{:S(2)}, u32[]{:S(2)}) %collective-permute-start.3) | collective-permute-done | bytes 786464 | tf_op jit(solution)/shard_map/ppermute | solution.py:506
  28.6 0.0 copy-done.4
  28.6 0.0 copy-done.5
  28.6 0.0 copy-done.6
  28.6 0.1 choose.1
  28.7 0.0 collective-permute-done.refs_1_
  28.7 3.3 %collective-permute-done.1.refs_2_ = f32[32,2048]{1,0:T(8,128)S(1)} collective-permute-done((f32[32,2048]{1,0:T(8,128)}, f32[32,2048]{1,0:T(8,128)S(1)}, u32[]{:S(2)}, u32[]{:S(2)}) %collective-permute-start.1) | collective-permute-done | bytes 262176 | tf_op jit(solution)/shard_map/ppermute | solution.py:500
  32.0 0.0 collective-permute-done.2.refs_3_
  32.0 6.2 %collective-permute-start.4 = (bf16[8,16,1024]{2,1,0:T(8,128)(2,1)S(1)}, bf16[8,16,1024]{2,1,0:T(8,128)(2,1)S(1)}, u32[]{:S(2)}, u32[]{:S(2)}) collective-permute-start(bf16[8,16,1024]{2,1,0:T(8,128)(2,1)S(1)} %get-tuple-element.59.refs_0_), channel_id=1, source_target_pairs={{0,1},{1,2},{2,3},{3,0},{4,5},{5,6},{6,7},{7,4},{8,9},{9,10},{10,1... | collective-permute-start | bytes 786440 | tf_op jit(solution)/shard_map/ppermute | solution.py:500
  38.2 0.9 collective-permute-start.5
  39.2 0.0 copy-done.3
  39.2 1.1 %gather.1 = (bf16[8,32,128]{2,1,0:T(8,128)(2,1)S(1)}, bf16[8,32,128]{2,1,0:T(8,128)(2,1)S(1)}) custom-call(s32[1]{0:T(128)} %bitcast.1.rank_ref, f32[128,128]{1,0:T(8,128)S(1)} %get-tuple-element.75.qc_ref, f32[128,128]{1,0:T(8,128)S(1)} %get-tuple-element.74.qs_ref, f32[32,2048]{1,0:T(8,128)S(1)} %copy-done.3, f32[32,2048]{1,0:T(8,128)S(1)} %collective-permute-done.refs_1_, ...), custom_call_target="tpu_custom_call" | custom-call | flops 262144 | bytes 65536 | tf_op jit(solution)/shard_map/gather/pallas_call | solution.py:261
  40.2 0.0 copy-done.1
  40.2 0.0 copy-start.10
  40.3 4.9 %attend.1.refs_0_ = s16[136,2048]{1,0:T(8,128)(2,1)S(1)} custom-call(s32[1]{0:T(128)} %bitcast.12.length_ref, s32[1]{0:T(128)} %bitcast.1.rank_ref, bf16[8192,128]{1,0:T(8,128)(2,1)S(1)} %get-tuple-element.43.q_ref, bf16[8,1024,128]{2,1,0:T(8,128)(2,1)S(1)} %get-tuple-element.44.k_ref, bf16[1024,2048]{1,0:T(8,128)(2,1)S(1)} %bitcast.18, ...), custom_call_target="tpu_custom_call" | custom-call | flops 268435456 | bytes 65536 | tf_op jit(solution)/shard_map/attend/pallas_call | solution.py:357
  45.2 1.2 %collective-permute-start.6 = (s16[136,2048]{1,0:T(8,128)(2,1)S(1)}, s16[136,2048]{1,0:T(8,128)(2,1)S(1)}, u32[]{:S(2)}, u32[]{:S(2)}) collective-permute-start(s16[136,2048]{1,0:T(8,128)(2,1)S(1)} %attend.1.refs_0_), channel_id=1, source_target_pairs={{0,1},{1,0},{2,3},{3,2},{4,5},{5,4},{6,7},{7,6},{8,9},{9,8},{10,11... | collective-permute-start | bytes 1671176 | tf_op jit(solution)/shard_map/ppermute | solution.py:503
  46.4 0.0 copy-done.10
  46.4 0.5 collective-permute-start.8
  46.9 1.5 %collective-permute-start.7 = (bf16[8,16,1024]{2,1,0:T(8,128)(2,1)S(1)}, bf16[8,16,1024]{2,1,0:T(8,128)(2,1)S(1)}, u32[]{:S(2)}, u32[]{:S(2)}) collective-permute-start(bf16[8,16,1024]{2,1,0:T(8,128)(2,1)S(1)} %get-tuple-element.65), channel_id=1, source_target_pairs={{0,2},{1,3},{2,0},{3,1},{4,6},{5,7},{6,4},{7,5},{8,10},{9,11},{10,... | collective-permute-start | bytes 786440 | tf_op jit(solution)/shard_map/ppermute | solution.py:500
  48.4 4.6 %attend_open.3 = (f32[2,128,1024]{2,1,0:T(8,128)S(1)}, f32[2,8,1024]{2,1,0:T(8,128)S(1)}) custom-call(s32[1]{0:T(128)} %bitcast.13.length_ref, s32[1]{0:T(128)} %bitcast.1.rank_ref, bf16[8192,128]{1,0:T(8,128)(2,1)S(1)} %get-tuple-element.43.q_ref, bf16[8,1024,128]{2,1,0:T(8,128)(2,1)S(1)} %get-tuple-element.44.k_ref, bf16[1024,2048]{1,0:T(8,128)(2,1)S(1)} %bitcast.19, ...), custom_call_target="tpu_custom_call" | custom-call | flops 268435456 | bytes 65536 | tf_op jit(solution)/shard_map/attend_open/pallas_call | solution.py:357
  53.0 0.0 collective-permute-done.4.refs_0_.refs_3_
  53.1 2.6 %collective-permute-done.5.refs_1_.refs_5_ = bf16[8,16,1024]{2,1,0:T(8,128)(2,1)S(1)} collective-permute-done((bf16[8,16,1024]{2,1,0:T(8,128)(2,1)S(1)}, bf16[8,16,1024]{2,1,0:T(8,128)(2,1)S(1)}, u32[]{:S(2)}, u32[]{:S(2)}) %collective-permute-start.5) | collective-permute-done | bytes 262176 | tf_op jit(solution)/shard_map/ppermute | solution.py:500
  55.6 4.6 %attend_open.4 = (f32[2,128,1024]{2,1,0:T(8,128)S(1)}, f32[2,8,1024]{2,1,0:T(8,128)S(1)}) custom-call(s32[1]{0:T(128)} %bitcast.14.length_ref, s32[1]{0:T(128)} %bitcast.1.rank_ref, bf16[8192,128]{1,0:T(8,128)(2,1)S(1)} %get-tuple-element.43.q_ref, bf16[8,1024,128]{2,1,0:T(8,128)(2,1)S(1)} %get-tuple-element.44.k_ref, bf16[1024,2048]{1,0:T(8,128)(2,1)S(1)} %bitcast.20, ...), custom_call_target="tpu_custom_call" | custom-call | flops 4294967296 | bytes 65536 | tf_op jit(solution)/shard_map/attend_open/pallas_call | solution.py:357
  60.3 7.2 %collective-permute-done.6.refs_0_ = s16[136,2048]{1,0:T(8,128)(2,1)S(1)} collective-permute-done((s16[136,2048]{1,0:T(8,128)(2,1)S(1)}, s16[136,2048]{1,0:T(8,128)(2,1)S(1)}, u32[]{:S(2)}, u32[]{:S(2)}) %collective-permute-start.6) | collective-permute-done | bytes 557088 | tf_op jit(solution)/shard_map/ppermute | solution.py:503
  67.5 0.6 close.2.refs_0_
  68.1 0.0 collective-permute-done.7.refs_1_.refs_4_
  68.1 0.4 close.3.refs_0_
  68.5 0.1 collective-permute-start.12
  68.5 3.9 %collective-permute-start.13 = (s16[136,2048]{1,0:T(8,128)(2,1)S(1)}, s16[136,2048]{1,0:T(8,128)(2,1)S(1)}, u32[]{:S(2)}, u32[]{:S(2)}) collective-permute-start(s16[136,2048]{1,0:T(8,128)(2,1)S(1)} %close.2.refs_0_), channel_id=1, source_target_pairs={{0,2},{1,3},{2,0},{3,1},{4,6},{5,7},{6,4},{7,5},{8,10},{9,11},{10,... | collective-permute-start | bytes 1671176 | tf_op jit(solution)/shard_map/ppermute | solution.py:503
  72.4 0.5 collective-permute-start.10
  73.0 1.5 %collective-permute-start.11 = (bf16[8,16,1024]{2,1,0:T(8,128)(2,1)S(1)}, bf16[8,16,1024]{2,1,0:T(8,128)(2,1)S(1)}, u32[]{:S(2)}, u32[]{:S(2)}) collective-permute-start(bf16[8,16,1024]{2,1,0:T(8,128)(2,1)S(1)} %collective-permute-done.5.refs_1_.refs_5_), channel_id=1, source_target_pairs={{0,16},{16,0},{1,17},{17,1},{2,18},{18,2},{3,19},{19,3},{4,20},{20... | collective-permute-start | bytes 786440 | tf_op jit(solution)/shard_map/ppermute | solution.py:506
  74.5 0.0 collective-permute-done.8.kept_ref
  74.5 0.5 collective-permute-start.9
  75.0 4.6 %attend_open.5 = (f32[2,128,1024]{2,1,0:T(8,128)S(1)}, f32[2,8,1024]{2,1,0:T(8,128)S(1)}) custom-call(s32[1]{0:T(128)} %bitcast.15.length_ref, s32[1]{0:T(128)} %bitcast.1.rank_ref, bf16[8192,128]{1,0:T(8,128)(2,1)S(1)} %get-tuple-element.43.q_ref, bf16[8,1024,128]{2,1,0:T(8,128)(2,1)S(1)} %get-tuple-element.44.k_ref, bf16[1024,2048]{1,0:T(8,128)(2,1)S(1)} %bitcast.21, ...), custom_call_target="tpu_custom_call" | custom-call | flops 268435456 | bytes 65536 | tf_op jit(solution)/shard_map/attend_open/pallas_call | solution.py:357
  79.6 2.0 %collective-permute-done.10.refs_1_ = bf16[8,16,1024]{2,1,0:T(8,128)(2,1)S(1)} collective-permute-done((bf16[8,16,1024]{2,1,0:T(8,128)(2,1)S(1)}, bf16[8,16,1024]{2,1,0:T(8,128)(2,1)S(1)}, u32[]{:S(2)}, u32[]{:S(2)}) %collective-permute-start.10) | collective-permute-done | bytes 262176 | tf_op jit(solution)/shard_map/ppermute | solution.py:506
  81.7 5.6 %collective-permute-done.11.refs_2_ = bf16[8,16,1024]{2,1,0:T(8,128)(2,1)S(1)} collective-permute-done((bf16[8,16,1024]{2,1,0:T(8,128)(2,1)S(1)}, bf16[8,16,1024]{2,1,0:T(8,128)(2,1)S(1)}, u32[]{:S(2)}, u32[]{:S(2)}) %collective-permute-start.11) | collective-permute-done | bytes 262176 | tf_op jit(solution)/shard_map/ppermute | solution.py:506
  87.3 3.4 %collective-permute-done.9.refs_0_ = bf16[8,16,1024]{2,1,0:T(8,128)(2,1)S(1)} collective-permute-done((bf16[8,16,1024]{2,1,0:T(8,128)(2,1)S(1)}, bf16[8,16,1024]{2,1,0:T(8,128)(2,1)S(1)}, u32[]{:S(2)}, u32[]{:S(2)}) %collective-permute-start.9) | collective-permute-done | bytes 262176 | tf_op jit(solution)/shard_map/ppermute | solution.py:506
  90.7 1.9 %arrange.1 = bf16[32,16,2048]{2,1,0:T(8,128)(2,1)} custom-call(s32[1]{0:T(128)} %bitcast.8.sec_ref, s32[1]{0:T(128)} %bitcast.1.rank_ref, bf16[8,16,2048]{2,1,0:T(8,128)(2,1)S(1)} %collective-permute-done.8.kept_ref, bf16[8,16,1024]{2,1,0:T(8,128)(2,1)S(1)} %collective-permute-done.9.refs_0_, bf16[8,16,1024]{2,1,0:T(8,128)(2,1)S(1)} %collective-permute-done.10.refs_1_, ...), custom_call_target="tpu_custom_call" | custom-call | flops 262144 | bytes 65536 | tf_op jit(solution)/shard_map/arrange/pallas_call | solution.py:472
  92.5 2.4 %collective-permute-done.12.refs_0_ = s16[136,2048]{1,0:T(8,128)(2,1)S(1)} collective-permute-done((s16[136,2048]{1,0:T(8,128)(2,1)S(1)}, s16[136,2048]{1,0:T(8,128)(2,1)S(1)}, u32[]{:S(2)}, u32[]{:S(2)}) %collective-permute-start.12) | collective-permute-done | bytes 557088 | tf_op jit(solution)/shard_map/ppermute | solution.py:503
  94.9 1.3 %collective-permute-done.13.refs_1_ = s16[136,2048]{1,0:T(8,128)(2,1)S(1)} collective-permute-done((s16[136,2048]{1,0:T(8,128)(2,1)S(1)}, s16[136,2048]{1,0:T(8,128)(2,1)S(1)}, u32[]{:S(2)}, u32[]{:S(2)}) %collective-permute-start.13) | collective-permute-done | bytes 557088 | tf_op jit(solution)/shard_map/ppermute | solution.py:503
  96.3 1.4 %finish.1 = bf16[128,2048]{1,0:T(8,128)(2,1)} custom-call(f32[2,128,1024]{2,1,0:T(8,128)S(1)} %get-tuple-element.70.num_ref, f32[2,8,1024]{2,1,0:T(8,128)S(1)} %get-tuple-element.71.refs_6_.stat_ref, s16[136,2048]{1,0:T(8,128)(2,1)S(1)} %collective-permute-done.12.refs_0_, s16[136,2048]{1,0:T(8,128)(2,1)S(1)} %collective-permute-done.13.refs_1_), custom_call_target="tpu_custom_call" | custom-call | flops 262144 | bytes 65536 | tf_op jit(solution)/shard_map/finish/pallas_call | solution.py:402
  (2 shorter events, 0.0 us)
Async XLA Ops:
  0.6 16.4 %copy-start.8 = (f32[128]{0:T(128)S(1)}, f32[128]{0:T(128)}, u32[]{:S(2)}) copy-start(f32[128]{0:T(128)} %constant.16.clone) | copy-start | bytes 1540
  0.6 16.4 %copy-start.9 = (f32[128]{0:T(128)S(1)}, f32[128]{0:T(128)}, u32[]{:S(2)}) copy-start(f32[128]{0:T(128)} %constant.24) | copy-start | bytes 1540
  0.7 18.6 %copy-start.2 = (bf16[1,128,8192]{2,1,0:T(8,128)(2,1)S(1)}, bf16[1,128,8192]{2,1,0:T(8,128)(2,1)}, u32[]{:S(2)}) copy-start(bf16[1,128,8192]{2,1,0:T(8,128)(2,1)} %param.12) | copy-start | bytes 6291460
  0.7 18.6 %copy-start.7 = (f32[1024]{0:T(1024)S(1)}, f32[1024]{0:T(1024)}, u32[]{:S(2)}) copy-start(f32[1024]{0:T(1024)} %param.14) | copy-start | bytes 12292
  7.8 20.8 %collective-permute-start.3 = (bf16[3,8,16,1024]{3,2,1,0:T(8,128)(2,1)}, bf16[3,8,16,1024]{3,2,1,0:T(8,128)(2,1)S(1)}, u32[]{:S(2)}, u32[]{:S(2)}) collective-permute-start(bf16[3,8,16,1024]{3,2,1,0:T(8,128)(2,1)} %get-tuple-element.48), channel_id=1, source_target_pairs={{0,16},{16,0},{1,17},{17,1},{2,18},{18,2},{3,19},{19,3},{4,20},{20... | collective-permute-start | bytes 2359304 | tf_op jit(solution)/shard_map/ppermute | solution.py:506
  10.8 17.9 %collective-permute-start = (f32[32,2048]{1,0:T(8,128)}, f32[32,2048]{1,0:T(8,128)S(1)}, u32[]{:S(2)}, u32[]{:S(2)}) collective-permute-start(f32[32,2048]{1,0:T(8,128)} %get-tuple-element.38), channel_id=1, source_target_pairs={{0,1},{1,2},{2,3},{3,0},{4,5},{5,6},{6,7},{7,4},{8,9},{9,10},{10,1... | collective-permute-start | bytes 786440 | tf_op jit(solution)/shard_map/ppermute | solution.py:500
  12.4 19.6 %collective-permute-start.1 = (f32[32,2048]{1,0:T(8,128)}, f32[32,2048]{1,0:T(8,128)S(1)}, u32[]{:S(2)}, u32[]{:S(2)}) collective-permute-start(f32[32,2048]{1,0:T(8,128)} %get-tuple-element.39), channel_id=1, source_target_pairs={{0,2},{1,3},{2,0},{3,1},{4,6},{5,7},{6,4},{7,5},{8,10},{9,11},{10,... | collective-permute-start | bytes 786440 | tf_op jit(solution)/shard_map/ppermute | solution.py:500
  15.0 17.0 %collective-permute-start.2 = (f32[32,2048]{1,0:T(8,128)}, f32[32,2048]{1,0:T(8,128)}, u32[]{:S(2)}, u32[]{:S(2)}) collective-permute-start(f32[32,2048]{1,0:T(8,128)} %get-tuple-element.40), channel_id=1, source_target_pairs={{0,3},{1,0},{2,1},{3,2},{4,7},{5,4},{6,5},{7,6},{8,11},{9,8},{10,9... | collective-permute-start | bytes 786440 | tf_op jit(solution)/shard_map/ppermute | solution.py:500
  19.3 2.2 %copy-start = (bf16[1,1024,2048]{2,1,0:T(8,128)(2,1)S(1)}, bf16[1,1024,2048]{2,1,0:T(8,128)(2,1)}, u32[]{:S(2)}) copy-start(bf16[1,1024,2048]{2,1,0:T(8,128)(2,1)} %param.13) | copy-start | bytes 12582916
  21.5 7.1 %copy-start.4 = (bf16[8,16,1024]{2,1,0:T(8,128)(2,1)S(1)}, bf16[8,16,1024]{2,1,0:T(8,128)(2,1)}, u32[]{:S(2)}) copy-start(bf16[8,16,1024]{2,1,0:T(8,128)(2,1)} %get-tuple-element.45.refs_0_) | copy-start | bytes 786436
  21.5 7.1 %copy-start.5 = (bf16[8,16,1024]{2,1,0:T(8,128)(2,1)S(1)}, bf16[8,16,1024]{2,1,0:T(8,128)(2,1)}, u32[]{:S(2)}) copy-start(bf16[8,16,1024]{2,1,0:T(8,128)(2,1)} %get-tuple-element.46.refs_1_) | copy-start | bytes 786436
  21.5 7.1 %copy-start.6 = (bf16[8,16,1024]{2,1,0:T(8,128)(2,1)S(1)}, bf16[8,16,1024]{2,1,0:T(8,128)(2,1)}, u32[]{:S(2)}) copy-start(bf16[8,16,1024]{2,1,0:T(8,128)(2,1)} %get-tuple-element.47.refs_2_) | copy-start | bytes 786436
  21.5 17.7 %copy-start.3 = (f32[32,2048]{1,0:T(8,128)S(1)}, f32[32,2048]{1,0:T(8,128)}, u32[]{:S(2)}) copy-start(f32[32,2048]{1,0:T(8,128)} %get-tuple-element.53.refs_0_) | copy-start | bytes 786436
  21.5 18.8 %copy-start.1 = (bf16[1,1024,2048]{2,1,0:T(8,128)(2,1)S(1)}, bf16[1,1024,2048]{2,1,0:T(8,128)(2,1)}, u32[]{:S(2)}) copy-start(bf16[1,1024,2048]{2,1,0:T(8,128)(2,1)} %param.13) | copy-start | bytes 12582916
  32.0 21.0 %collective-permute-start.4 = (bf16[8,16,1024]{2,1,0:T(8,128)(2,1)S(1)}, bf16[8,16,1024]{2,1,0:T(8,128)(2,1)S(1)}, u32[]{:S(2)}, u32[]{:S(2)}) collective-permute-start(bf16[8,16,1024]{2,1,0:T(8,128)(2,1)S(1)} %get-tuple-element.59.refs_0_), channel_id=1, source_target_pairs={{0,1},{1,2},{2,3},{3,0},{4,5},{5,6},{6,7},{7,4},{8,9},{9,10},{10,1... | collective-permute-start | bytes 786440 | tf_op jit(solution)/shard_map/ppermute | solution.py:500
  38.2 17.4 %collective-permute-start.5 = (bf16[8,16,1024]{2,1,0:T(8,128)(2,1)S(1)}, bf16[8,16,1024]{2,1,0:T(8,128)(2,1)S(1)}, u32[]{:S(2)}, u32[]{:S(2)}) collective-permute-start(bf16[8,16,1024]{2,1,0:T(8,128)(2,1)S(1)} %get-tuple-element.60), channel_id=1, source_target_pairs={{0,3},{1,0},{2,1},{3,2},{4,7},{5,4},{6,5},{7,6},{8,11},{9,8},{10,9... | collective-permute-start | bytes 786440 | tf_op jit(solution)/shard_map/ppermute | solution.py:500
  40.2 6.1 %copy-start.10 = (bf16[8,16,2048]{2,1,0:T(8,128)(2,1)S(1)}, bf16[8,16,2048]{2,1,0:T(8,128)(2,1)}, u32[]{:S(2)}) copy-start(bf16[8,16,2048]{2,1,0:T(8,128)(2,1)} %get-tuple-element.69) | copy-start | bytes 1572868
  45.2 22.2 %collective-permute-start.6 = (s16[136,2048]{1,0:T(8,128)(2,1)S(1)}, s16[136,2048]{1,0:T(8,128)(2,1)S(1)}, u32[]{:S(2)}, u32[]{:S(2)}) collective-permute-start(s16[136,2048]{1,0:T(8,128)(2,1)S(1)} %attend.1.refs_0_), channel_id=1, source_target_pairs={{0,1},{1,0},{2,3},{3,2},{4,5},{5,4},{6,7},{7,6},{8,9},{9,8},{10,11... | collective-permute-start | bytes 1671176 | tf_op jit(solution)/shard_map/ppermute | solution.py:503
  46.4 28.1 %collective-permute-start.8 = (bf16[8,16,2048]{2,1,0:T(8,128)(2,1)S(1)}, bf16[8,16,2048]{2,1,0:T(8,128)(2,1)S(1)}, u32[]{:S(2)}, u32[]{:S(2)}) collective-permute-start(bf16[8,16,2048]{2,1,0:T(8,128)(2,1)S(1)} %copy-done.10), channel_id=1, source_target_pairs={{0,16},{16,0},{1,17},{17,1},{2,18},{18,2},{3,19},{19,3},{4,20},{20... | collective-permute-start | bytes 1572872 | tf_op jit(solution)/shard_map/ppermute | solution.py:506
  46.9 21.1 %collective-permute-start.7 = (bf16[8,16,1024]{2,1,0:T(8,128)(2,1)S(1)}, bf16[8,16,1024]{2,1,0:T(8,128)(2,1)S(1)}, u32[]{:S(2)}, u32[]{:S(2)}) collective-permute-start(bf16[8,16,1024]{2,1,0:T(8,128)(2,1)S(1)} %get-tuple-element.65), channel_id=1, source_target_pairs={{0,2},{1,3},{2,0},{3,1},{4,6},{5,7},{6,4},{7,5},{8,10},{9,11},{10,... | collective-permute-start | bytes 786440 | tf_op jit(solution)/shard_map/ppermute | solution.py:500
  68.5 26.5 %collective-permute-start.12 = (s16[136,2048]{1,0:T(8,128)(2,1)S(1)}, s16[136,2048]{1,0:T(8,128)(2,1)S(1)}, u32[]{:S(2)}, u32[]{:S(2)}) collective-permute-start(s16[136,2048]{1,0:T(8,128)(2,1)S(1)} %close.3.refs_0_), channel_id=1, source_target_pairs={{0,1},{1,0},{2,3},{3,2},{4,5},{5,4},{6,7},{7,6},{8,9},{9,8},{10,11... | collective-permute-start | bytes 1671176 | tf_op jit(solution)/shard_map/ppermute | solution.py:503
  68.5 27.7 %collective-permute-start.13 = (s16[136,2048]{1,0:T(8,128)(2,1)S(1)}, s16[136,2048]{1,0:T(8,128)(2,1)S(1)}, u32[]{:S(2)}, u32[]{:S(2)}) collective-permute-start(s16[136,2048]{1,0:T(8,128)(2,1)S(1)} %close.2.refs_0_), channel_id=1, source_target_pairs={{0,2},{1,3},{2,0},{3,1},{4,6},{5,7},{6,4},{7,5},{8,10},{9,11},{10,... | collective-permute-start | bytes 1671176 | tf_op jit(solution)/shard_map/ppermute | solution.py:503
  72.4 9.2 %collective-permute-start.10 = (bf16[8,16,1024]{2,1,0:T(8,128)(2,1)S(1)}, bf16[8,16,1024]{2,1,0:T(8,128)(2,1)S(1)}, u32[]{:S(2)}, u32[]{:S(2)}) collective-permute-start(bf16[8,16,1024]{2,1,0:T(8,128)(2,1)S(1)} %collective-permute-done.7.refs_1_.refs_4_), channel_id=1, source_target_pairs={{0,16},{16,0},{1,17},{17,1},{2,18},{18,2},{3,19},{19,3},{4,20},{20... | collective-permute-start | bytes 786440 | tf_op jit(solution)/shard_map/ppermute | solution.py:506
  73.0 14.3 %collective-permute-start.11 = (bf16[8,16,1024]{2,1,0:T(8,128)(2,1)S(1)}, bf16[8,16,1024]{2,1,0:T(8,128)(2,1)S(1)}, u32[]{:S(2)}, u32[]{:S(2)}) collective-permute-start(bf16[8,16,1024]{2,1,0:T(8,128)(2,1)S(1)} %collective-permute-done.5.refs_1_.refs_5_), channel_id=1, source_target_pairs={{0,16},{16,0},{1,17},{17,1},{2,18},{18,2},{3,19},{19,3},{4,20},{20... | collective-permute-start | bytes 786440 | tf_op jit(solution)/shard_map/ppermute | solution.py:506
  74.5 16.2 %collective-permute-start.9 = (bf16[8,16,1024]{2,1,0:T(8,128)(2,1)S(1)}, bf16[8,16,1024]{2,1,0:T(8,128)(2,1)S(1)}, u32[]{:S(2)}, u32[]{:S(2)}) collective-permute-start(bf16[8,16,1024]{2,1,0:T(8,128)(2,1)S(1)} %collective-permute-done.4.refs_0_.refs_3_), channel_id=1, source_target_pairs={{0,16},{16,0},{1,17},{17,1},{2,18},{18,2},{3,19},{19,3},{4,20},{20... | collective-permute-start | bytes 786440 | tf_op jit(solution)/shard_map/ppermute | solution.py:506

commit v7 on v6

--- a/solution.py
+++ b/solution.py
@@ -58,33 +58,37 @@
 
 
 def project_kernel(ranks, rank_ref, x_ref, w_ref, page_ref, owner_ref, cache_ref, *refs):
-    out_refs, page_refs, there_ref = refs[:ranks], refs[ranks:2 * ranks], refs[2 * ranks]
-    weight, total, sems, counts, page_sems = refs[2 * ranks + 1:]
+    out_refs, page_outs = refs[:ranks], refs[ranks:2 * ranks + 1]
+    rows_in, weight, total, kept_pages, near_pages, far_pages, sems, counts, page_sems, out_sems = (
+        refs[2 * ranks + 1:]
+    )
     entries = page_ref.shape[0]
     share = out_refs[0].shape[0]
-    chunks = weight.shape[0]
+    chunks, depth = weight.shape[0], weight.shape[1]
+    rows_copy = pltpu.make_async_copy(x_ref, rows_in, sems.at[chunks])
 
     def weight_copy(j):
-        rows = pl.ds(j * weight.shape[1], weight.shape[1])
-        return pltpu.make_async_copy(w_ref.at[rows, :], weight.at[j], sems.at[j])
+        source = w_ref.at[pl.ds(j * depth, depth), :]
+        return pltpu.make_async_copy(source, weight.at[j], sems.at[j])
 
     def page_rows(e):
         return pl.ds(pl.multiple_of(page_ref[e] * PAGE, PAGE), PAGE)
 
     def kept(e, slot):
-        return pltpu.make_async_copy(cache_ref.at[page_rows(e), :], page_refs[0].at[slot], page_sems.at[e])
+        return pltpu.make_async_copy(cache_ref.at[page_rows(e), :], kept_pages.at[slot], page_sems.at[e])
 
     def near(e, k, slot):
         source = cache_ref.at[page_rows(e), pl.ds(0, KVW)]
-        return pltpu.make_async_copy(source, page_refs[k].at[slot], page_sems.at[e])
+        return pltpu.make_async_copy(source, near_pages.at[k - 1, slot], page_sems.at[e])
 
     def far(e, k, slot):
         source = cache_ref.at[page_rows(e), pl.ds(KVW, KVW)]
-        return pltpu.make_async_copy(source, there_ref.at[k - 1, slot], page_sems.at[e])
-
+        return pltpu.make_async_copy(source, far_pages.at[k - 1, slot], page_sems.at[e])
+
+    rows_copy.start()
     for j in range(chunks):
         weight_copy(j).start()
-    for ref in [*page_refs, there_ref]:
+    for ref in (kept_pages, near_pages, far_pages):
         ref[...] = jnp.zeros_like(ref)
     for r in range(ranks):
         counts[r] = 0
@@ -99,32 +103,41 @@
         def _():
             kept(e, slot).start()
 
-        for k in range(1, ranks):
-            @pl.when(place == k)
-            def _():
-                near(e, k, slot).start()
-                far(e, k, slot).start()
+        @pl.when(place > 0)
+        def _():
+            near(e, place, slot).start()
+            far(e, place, slot).start()
+
         return carry
 
+    def end(e, carry):
+        kept(e, 0).wait()
+        return carry
+
+    sources = [kept_pages, *[near_pages.at[k] for k in range(ranks - 1)], far_pages]
+    page_copies = [
+        pltpu.make_async_copy(source, out, out_sems.at[i])
+        for i, (source, out) in enumerate(zip(sources, page_outs))
+    ]
     lax.fori_loop(0, entries, begin, 0)
+    rows_copy.wait()
     for j in range(chunks):
         weight_copy(j).wait()
-        depth = weight.shape[1]
         part = jnp.dot(
-            x_ref[:, j * depth:(j + 1) * depth], weight[j], preferred_element_type=jnp.float32
+            rows_in[:, j * depth:(j + 1) * depth], weight[j], preferred_element_type=jnp.float32
         )
         if j:
             part = part + total[...]
         total[...] = part
+        if j == min(1, chunks - 1):
+            lax.fori_loop(0, entries, end, 0)
+            for c in page_copies:
+                c.start()
     for k in range(ranks):
         dest = lax.rem(rank_ref[0] + k, ranks)
         out_refs[k][...] = total[pl.ds(pl.multiple_of(dest * share, share), share), :]
-
-    def end(e, carry):
-        kept(e, 0).wait()
-        return carry
-
-    lax.fori_loop(0, entries, end, 0)
+    for c in page_copies:
+        c.wait()
 
 
 def project(me, x, weight, page_list, owner_ids, cache, ranks):
@@ -136,21 +149,25 @@
     smem = pl.BlockSpec(memory_space=pltpu.SMEM)
     vmem = pl.BlockSpec(memory_space=pltpu.VMEM)
     anywhere = pl.BlockSpec(memory_space=pl.ANY)
-    out_shape = [jax.ShapeDtypeStruct((share, 2 * KVW), jnp.float32)] * ranks
-    out_shape += [jax.ShapeDtypeStruct((slots, PAGE, 2 * KVW), jnp.bfloat16)]
-    out_shape += [jax.ShapeDtypeStruct((slots, PAGE, KVW), jnp.bfloat16)] * (ranks - 1)
-    out_shape += [jax.ShapeDtypeStruct((ranks - 1, slots, PAGE, KVW), jnp.bfloat16)]
+    pages = [(slots, PAGE, 2 * KVW)] + [(slots, PAGE, KVW)] * (ranks - 1)
+    pages += [(ranks - 1, slots, PAGE, KVW)]
     out = pl.pallas_call(
         functools.partial(project_kernel, ranks),
-        in_specs=[smem, vmem, anywhere, smem, smem, anywhere],
-        out_specs=[vmem] * len(out_shape),
-        out_shape=out_shape,
+        in_specs=[smem, anywhere, anywhere, smem, smem, anywhere],
+        out_specs=[vmem] * ranks + [anywhere] * len(pages),
+        out_shape=[jax.ShapeDtypeStruct((share, 2 * KVW), jnp.float32)] * ranks
+        + [jax.ShapeDtypeStruct(shape, jnp.bfloat16) for shape in pages],
         scratch_shapes=[
+            pltpu.VMEM((ROWS, depth), jnp.bfloat16),
             pltpu.VMEM((depth // block, block, 2 * KVW), jnp.bfloat16),
             pltpu.VMEM((ROWS, 2 * KVW), jnp.float32),
-            pltpu.SemaphoreType.DMA((depth // block,)),
+            pltpu.VMEM(pages[0], jnp.bfloat16),
+            pltpu.VMEM(pages[-1], jnp.bfloat16),
+            pltpu.VMEM(pages[-1], jnp.bfloat16),
+            pltpu.SemaphoreType.DMA((depth // block + 1,)),
             pltpu.SMEM((ranks,), jnp.int32),
             pltpu.SemaphoreType.DMA((entries,)),
+            pltpu.SemaphoreType.DMA((len(pages),)),
         ],
         compiler_params=PARAMS,
         cost_estimate=small_cost(1 << 20),

time: 97.9 us -> 97.2 us (level)
  no operation moved by 1% of the time
where the time goes in v7:
time: 97.2 us; the launch traced here: 97.7 us
  Pallas kernels  34.3 us (35%)
  waiting for transfers between devices  32.3 us (33%)
  starting transfers between devices  25.2 us (26%)
  local copies, waits for them, and re-layouts  2.23 us (2%)
  other arithmetic  2.22 us (2%)
  between operations  1.54 us (2%)
    pallas_call x4, Pallas kernels, attend(): pl.pallas_call(functools.partial(attend_kernel, is_open, len(earlier)), g...  18.8 us
    ppermute x5, waiting for transfers between devices, handed_on(): lax.ppermute(value, 'sec', [(i, (i + 1) % secs) for i in range(secs)])  15.3 us
    ppermute x6, starting transfers between devices, shifted(): lax.ppermute(value, 'rank', [(i, (i + k) % ranks) for i in range(ranks)])  14.1 us
    ppermute x3, waiting for transfers between devices, swapped(): return lax.ppermute(value, 'rank', [(i, i ^ bit) for i in range(ranks)])  10.9 us
    pallas_call x1, Pallas kernels, project(): pl.pallas_call(functools.partial(project_kernel, ranks), in_specs=[smem,...  7.12 us
    ppermute x5, starting transfers between devices, handed_on(): lax.ppermute(value, 'sec', [(i, (i + 1) % secs) for i in range(secs)])  6.05 us
    ppermute x6, waiting for transfers between devices, shifted(): lax.ppermute(value, 'rank', [(i, (i + k) % ranks) for i in range(ranks)])  6.02 us
    ppermute x3, starting transfers between devices, swapped(): return lax.ppermute(value, 'rank', [(i, i ^ bit) for i in range(ranks)])  5.09 us
  transfers between devices with their start and end apart: 14, of which 9 were waited for; matrix products, arithmetic and copies ran while one was open for 2% of the time, Pallas kernels for 26%

profile of v7, /device:TPU:0, one launch (start us, length us, event | category | flops | bytes accessed | tf_op | source)
XLA Modules:
  0.0 97.7 jit_solution(10395608435597367865)
XLA Ops:
  0.6 0.0 copy-start.8
  0.6 0.0 copy-start.9
  0.7 0.0 copy-start.2
  0.7 0.0 copy-start.7
  0.7 7.1 %project.1 = (f32[32,2048]{1,0:T(8,128)}, f32[32,2048]{1,0:T(8,128)}, f32[32,2048]{1,0:T(8,128)}, f32[32,2048]{1,0:T(8,128)}, bf16[8,16,2048]{2,1,0:T(8,128)(2,1...) custom-call(s32[1]{0:T(128)} %bitcast.1.rank_ref, ...), custom_call_target="tpu_custom_call" | custom-call | flops 1048576 | bytes 65536 | tf_op jit(solution)/shard_map/project/pallas_call | solution.py:154
  7.8 3.0 %collective-permute-start.3 = (bf16[3,8,16,1024]{3,2,1,0:T(8,128)(2,1)}, bf16[3,8,16,1024]{3,2,1,0:T(8,128)(2,1)S(1)}, u32[]{:S(2)}, u32[]{:S(2)}) collective-permute-start(bf16[3,8,16,1024]{3,2,1,0:T(8,128)(2,1)} %get-tuple-element.48), channel_id=1, source_target_pairs={{0,16},{16,0},{1,17},{17,1},{2,18},{18,2},{3,19},{19,3},{4,20},{20... | collective-permute-start | bytes 2359304 | tf_op jit(solution)/shard_map/ppermute | solution.py:523
  10.8 1.6 %collective-permute-start = (f32[32,2048]{1,0:T(8,128)}, f32[32,2048]{1,0:T(8,128)S(1)}, u32[]{:S(2)}, u32[]{:S(2)}) collective-permute-start(f32[32,2048]{1,0:T(8,128)} %get-tuple-element.38), channel_id=1, source_target_pairs={{0,1},{1,2},{2,3},{3,0},{4,5},{5,6},{6,7},{7,4},{8,9},{9,10},{10,1... | collective-permute-start | bytes 786440 | tf_op jit(solution)/shard_map/ppermute | solution.py:517
  12.4 2.6 %collective-permute-start.1 = (f32[32,2048]{1,0:T(8,128)}, f32[32,2048]{1,0:T(8,128)S(1)}, u32[]{:S(2)}, u32[]{:S(2)}) collective-permute-start(f32[32,2048]{1,0:T(8,128)} %get-tuple-element.39), channel_id=1, source_target_pairs={{0,2},{1,3},{2,0},{3,1},{4,6},{5,7},{6,4},{7,5},{8,10},{9,11},{10,... | collective-permute-start | bytes 786440 | tf_op jit(solution)/shard_map/ppermute | solution.py:517
  14.9 1.4 %collective-permute-start.2 = (f32[32,2048]{1,0:T(8,128)}, f32[32,2048]{1,0:T(8,128)}, u32[]{:S(2)}, u32[]{:S(2)}) collective-permute-start(f32[32,2048]{1,0:T(8,128)} %get-tuple-element.40), channel_id=1, source_target_pairs={{0,3},{1,0},{2,1},{3,2},{4,7},{5,4},{6,5},{7,6},{8,11},{9,8},{10,9... | collective-permute-start | bytes 786440 | tf_op jit(solution)/shard_map/ppermute | solution.py:517
  17.0 0.0 copy-done.8
  17.0 0.0 copy-done.9
  17.0 1.9 %fusion = (f32[1024,128]{1,0:T(8,128)S(1)}, f32[1024,128]{1,0:T(8,128)S(1)}) fusion(f32[128]{0:T(128)S(1)} %copy-done.9, f32[128]{0:T(128)S(1)} %copy-done.8, f32[1024]{0:T(1024)S(1)} %add_convert_fusion), kind=kLoop, calls=%fused_computation.2 | loop fusion | flops 262144 | bytes 1053696 | tf_op jit(solution)/shard_map/mul | solution.py:53
  18.9 0.3 fusion.1
  19.2 0.0 copy-done.2
  19.2 0.0 copy-done.7
  19.3 0.0 copy-start
  19.3 2.2 %copy-done = bf16[1,1024,2048]{2,1,0:T(8,128)(2,1)S(1)} copy-done((bf16[1,1024,2048]{2,1,0:T(8,128)(2,1)S(1)}, bf16[1,1024,2048]{2,1,0:T(8,128)(2,1)}, u32[]{:S(2)}) %copy-start) | copy-done | bytes 4194328
  21.4 0.0 copy-start.4
  21.4 0.0 copy-start.5
  21.5 0.0 copy-start.6
  21.5 0.0 copy-start.3
  21.5 0.0 copy-start.1
  21.5 2.9 %prepare.1 = (bf16[8192,128]{1,0:T(8,128)(2,1)S(1)}, bf16[8,1024,128]{2,1,0:T(8,128)(2,1)S(1)}) custom-call(bf16[128,8192]{1,0:T(8,128)(2,1)S(1)} %bitcast.22, bf16[1024,2048]{1,0:T(8,128)(2,1)S(1)} %bitcast.17, f32[1,1024]{1,0:T(1,128)S(1)} %bitcast.23, f32[128,128]{1,0:T(8,128)S(1)} %get-tuple-element.75.qc_ref, f32[128,128]{1,0:T(8,128)S(1)} %get-tuple-element.74.qs_ref, ...), custom_call_target="tpu_custom_call" | custom-call | flops 1073741824 | bytes 65536 | tf_op jit(solution)/shard_map/prepare/pallas_call | solution.py:192
  24.4 4.2 %collective-permute-done.3.refs_3_ = bf16[3,8,16,1024]{3,2,1,0:T(8,128)(2,1)S(1)} collective-permute-done((bf16[3,8,16,1024]{3,2,1,0:T(8,128)(2,1)}, bf16[3,8,16,1024]{3,2,1,0:T(8,128)(2,1)S(1)}, u32[]{:S(2)}, u32[]{:S(2)}) %collective-permute-start.3) | collective-permute-done | bytes 786464 | tf_op jit(solution)/shard_map/ppermute | solution.py:523
  28.6 0.0 copy-done.4
  28.6 0.0 copy-done.5
  28.6 0.0 copy-done.6
  28.6 0.1 choose.1
  28.7 0.0 collective-permute-done.refs_1_
  28.7 3.3 %collective-permute-done.1.refs_2_ = f32[32,2048]{1,0:T(8,128)S(1)} collective-permute-done((f32[32,2048]{1,0:T(8,128)}, f32[32,2048]{1,0:T(8,128)S(1)}, u32[]{:S(2)}, u32[]{:S(2)}) %collective-permute-start.1) | collective-permute-done | bytes 262176 | tf_op jit(solution)/shard_map/ppermute | solution.py:517
  32.0 0.0 collective-permute-done.2.refs_3_
  32.0 6.2 %collective-permute-start.4 = (bf16[8,16,1024]{2,1,0:T(8,128)(2,1)S(1)}, bf16[8,16,1024]{2,1,0:T(8,128)(2,1)S(1)}, u32[]{:S(2)}, u32[]{:S(2)}) collective-permute-start(bf16[8,16,1024]{2,1,0:T(8,128)(2,1)S(1)} %get-tuple-element.59.refs_0_), channel_id=1, source_target_pairs={{0,1},{1,2},{2,3},{3,0},{4,5},{5,6},{6,7},{7,4},{8,9},{9,10},{10,1... | collective-permute-start | bytes 786440 | tf_op jit(solution)/shard_map/ppermute | solution.py:517
  38.2 0.9 collective-permute-start.5
  39.2 0.0 copy-done.3
  39.2 1.1 %gather.1 = (bf16[8,32,128]{2,1,0:T(8,128)(2,1)S(1)}, bf16[8,32,128]{2,1,0:T(8,128)(2,1)S(1)}) custom-call(s32[1]{0:T(128)} %bitcast.1.rank_ref, f32[128,128]{1,0:T(8,128)S(1)} %get-tuple-element.75.qc_ref, f32[128,128]{1,0:T(8,128)S(1)} %get-tuple-element.74.qs_ref, f32[32,2048]{1,0:T(8,128)S(1)} %copy-done.3, f32[32,2048]{1,0:T(8,128)S(1)} %collective-permute-done.refs_1_, ...), custom_call_target="tpu_custom_call" | custom-call | flops 262144 | bytes 65536 | tf_op jit(solution)/shard_map/gather/pallas_call | solution.py:278
  40.3 0.0 copy-done.1
  40.3 0.0 copy-start.10
  40.3 5.0 %attend.1.refs_0_ = s16[136,2048]{1,0:T(8,128)(2,1)S(1)} custom-call(s32[1]{0:T(128)} %bitcast.12.length_ref, s32[1]{0:T(128)} %bitcast.1.rank_ref, bf16[8192,128]{1,0:T(8,128)(2,1)S(1)} %get-tuple-element.43.q_ref, bf16[8,1024,128]{2,1,0:T(8,128)(2,1)S(1)} %get-tuple-element.44.k_ref, bf16[1024,2048]{1,0:T(8,128)(2,1)S(1)} %bitcast.18, ...), custom_call_target="tpu_custom_call" | custom-call | flops 268435456 | bytes 65536 | tf_op jit(solution)/shard_map/attend/pallas_call | solution.py:374
  45.2 1.1 %collective-permute-start.6 = (s16[136,2048]{1,0:T(8,128)(2,1)S(1)}, s16[136,2048]{1,0:T(8,128)(2,1)S(1)}, u32[]{:S(2)}, u32[]{:S(2)}) collective-permute-start(s16[136,2048]{1,0:T(8,128)(2,1)S(1)} %attend.1.refs_0_), channel_id=1, source_target_pairs={{0,1},{1,0},{2,3},{3,2},{4,5},{5,4},{6,7},{7,6},{8,9},{9,8},{10,11... | collective-permute-start | bytes 1671176 | tf_op jit(solution)/shard_map/ppermute | solution.py:520
  46.4 0.0 copy-done.10
  46.4 0.6 collective-permute-start.8
  47.0 1.4 %collective-permute-start.7 = (bf16[8,16,1024]{2,1,0:T(8,128)(2,1)S(1)}, bf16[8,16,1024]{2,1,0:T(8,128)(2,1)S(1)}, u32[]{:S(2)}, u32[]{:S(2)}) collective-permute-start(bf16[8,16,1024]{2,1,0:T(8,128)(2,1)S(1)} %get-tuple-element.65), channel_id=1, source_target_pairs={{0,2},{1,3},{2,0},{3,1},{4,6},{5,7},{6,4},{7,5},{8,10},{9,11},{10,... | collective-permute-start | bytes 786440 | tf_op jit(solution)/shard_map/ppermute | solution.py:517
  48.4 4.6 %attend_open.3 = (f32[2,128,1024]{2,1,0:T(8,128)S(1)}, f32[2,8,1024]{2,1,0:T(8,128)S(1)}) custom-call(s32[1]{0:T(128)} %bitcast.13.length_ref, s32[1]{0:T(128)} %bitcast.1.rank_ref, bf16[8192,128]{1,0:T(8,128)(2,1)S(1)} %get-tuple-element.43.q_ref, bf16[8,1024,128]{2,1,0:T(8,128)(2,1)S(1)} %get-tuple-element.44.k_ref, bf16[1024,2048]{1,0:T(8,128)(2,1)S(1)} %bitcast.19, ...), custom_call_target="tpu_custom_call" | custom-call | flops 268435456 | bytes 65536 | tf_op jit(solution)/shard_map/attend_open/pallas_call | solution.py:374
  53.0 0.0 collective-permute-done.4.refs_0_.refs_3_
  53.0 2.7 %collective-permute-done.5.refs_1_.refs_5_ = bf16[8,16,1024]{2,1,0:T(8,128)(2,1)S(1)} collective-permute-done((bf16[8,16,1024]{2,1,0:T(8,128)(2,1)S(1)}, bf16[8,16,1024]{2,1,0:T(8,128)(2,1)S(1)}, u32[]{:S(2)}, u32[]{:S(2)}) %collective-permute-start.5) | collective-permute-done | bytes 262176 | tf_op jit(solution)/shard_map/ppermute | solution.py:517
  55.7 4.6 %attend_open.4 = (f32[2,128,1024]{2,1,0:T(8,128)S(1)}, f32[2,8,1024]{2,1,0:T(8,128)S(1)}) custom-call(s32[1]{0:T(128)} %bitcast.14.length_ref, s32[1]{0:T(128)} %bitcast.1.rank_ref, bf16[8192,128]{1,0:T(8,128)(2,1)S(1)} %get-tuple-element.43.q_ref, bf16[8,1024,128]{2,1,0:T(8,128)(2,1)S(1)} %get-tuple-element.44.k_ref, bf16[1024,2048]{1,0:T(8,128)(2,1)S(1)} %bitcast.20, ...), custom_call_target="tpu_custom_call" | custom-call | flops 4294967296 | bytes 65536 | tf_op jit(solution)/shard_map/attend_open/pallas_call | solution.py:374
  60.3 7.2 %collective-permute-done.6.refs_0_ = s16[136,2048]{1,0:T(8,128)(2,1)S(1)} collective-permute-done((s16[136,2048]{1,0:T(8,128)(2,1)S(1)}, s16[136,2048]{1,0:T(8,128)(2,1)S(1)}, u32[]{:S(2)}, u32[]{:S(2)}) %collective-permute-start.6) | collective-permute-done | bytes 557088 | tf_op jit(solution)/shard_map/ppermute | solution.py:520
  67.5 0.6 close.2.refs_0_
  68.1 0.0 collective-permute-done.7.refs_1_.refs_4_
  68.1 0.4 close.3.refs_0_
  68.5 0.1 collective-permute-start.12
  68.6 3.9 %collective-permute-start.13 = (s16[136,2048]{1,0:T(8,128)(2,1)S(1)}, s16[136,2048]{1,0:T(8,128)(2,1)S(1)}, u32[]{:S(2)}, u32[]{:S(2)}) collective-permute-start(s16[136,2048]{1,0:T(8,128)(2,1)S(1)} %close.2.refs_0_), channel_id=1, source_target_pairs={{0,2},{1,3},{2,0},{3,1},{4,6},{5,7},{6,4},{7,5},{8,10},{9,11},{10,... | collective-permute-start | bytes 1671176 | tf_op jit(solution)/shard_map/ppermute | solution.py:520
  72.5 0.5 collective-permute-start.10
  73.0 1.5 %collective-permute-start.11 = (bf16[8,16,1024]{2,1,0:T(8,128)(2,1)S(1)}, bf16[8,16,1024]{2,1,0:T(8,128)(2,1)S(1)}, u32[]{:S(2)}, u32[]{:S(2)}) collective-permute-start(bf16[8,16,1024]{2,1,0:T(8,128)(2,1)S(1)} %collective-permute-done.5.refs_1_.refs_5_), channel_id=1, source_target_pairs={{0,16},{16,0},{1,17},{17,1},{2,18},{18,2},{3,19},{19,3},{4,20},{20... | collective-permute-start | bytes 786440 | tf_op jit(solution)/shard_map/ppermute | solution.py:523
  74.5 0.0 collective-permute-done.8.kept_ref
  74.5 0.5 collective-permute-start.9
  75.0 4.6 %attend_open.5 = (f32[2,128,1024]{2,1,0:T(8,128)S(1)}, f32[2,8,1024]{2,1,0:T(8,128)S(1)}) custom-call(s32[1]{0:T(128)} %bitcast.15.length_ref, s32[1]{0:T(128)} %bitcast.1.rank_ref, bf16[8192,128]{1,0:T(8,128)(2,1)S(1)} %get-tuple-element.43.q_ref, bf16[8,1024,128]{2,1,0:T(8,128)(2,1)S(1)} %get-tuple-element.44.k_ref, bf16[1024,2048]{1,0:T(8,128)(2,1)S(1)} %bitcast.21, ...), custom_call_target="tpu_custom_call" | custom-call | flops 268435456 | bytes 65536 | tf_op jit(solution)/shard_map/attend_open/pallas_call | solution.py:374
  79.6 2.1 %collective-permute-done.10.refs_1_ = bf16[8,16,1024]{2,1,0:T(8,128)(2,1)S(1)} collective-permute-done((bf16[8,16,1024]{2,1,0:T(8,128)(2,1)S(1)}, bf16[8,16,1024]{2,1,0:T(8,128)(2,1)S(1)}, u32[]{:S(2)}, u32[]{:S(2)}) %collective-permute-start.10) | collective-permute-done | bytes 262176 | tf_op jit(solution)/shard_map/ppermute | solution.py:523
  81.7 5.6 %collective-permute-done.11.refs_2_ = bf16[8,16,1024]{2,1,0:T(8,128)(2,1)S(1)} collective-permute-done((bf16[8,16,1024]{2,1,0:T(8,128)(2,1)S(1)}, bf16[8,16,1024]{2,1,0:T(8,128)(2,1)S(1)}, u32[]{:S(2)}, u32[]{:S(2)}) %collective-permute-start.11) | collective-permute-done | bytes 262176 | tf_op jit(solution)/shard_map/ppermute | solution.py:523
  87.3 3.4 %collective-permute-done.9.refs_0_ = bf16[8,16,1024]{2,1,0:T(8,128)(2,1)S(1)} collective-permute-done((bf16[8,16,1024]{2,1,0:T(8,128)(2,1)S(1)}, bf16[8,16,1024]{2,1,0:T(8,128)(2,1)S(1)}, u32[]{:S(2)}, u32[]{:S(2)}) %collective-permute-start.9) | collective-permute-done | bytes 262176 | tf_op jit(solution)/shard_map/ppermute | solution.py:523
  90.7 1.9 %arrange.1 = bf16[32,16,2048]{2,1,0:T(8,128)(2,1)} custom-call(s32[1]{0:T(128)} %bitcast.8.sec_ref, s32[1]{0:T(128)} %bitcast.1.rank_ref, bf16[8,16,2048]{2,1,0:T(8,128)(2,1)S(1)} %collective-permute-done.8.kept_ref, bf16[8,16,1024]{2,1,0:T(8,128)(2,1)S(1)} %collective-permute-done.9.refs_0_, bf16[8,16,1024]{2,1,0:T(8,128)(2,1)S(1)} %collective-permute-done.10.refs_1_, ...), custom_call_target="tpu_custom_call" | custom-call | flops 262144 | bytes 65536 | tf_op jit(solution)/shard_map/arrange/pallas_call | solution.py:489
  92.6 2.3 %collective-permute-done.12.refs_0_ = s16[136,2048]{1,0:T(8,128)(2,1)S(1)} collective-permute-done((s16[136,2048]{1,0:T(8,128)(2,1)S(1)}, s16[136,2048]{1,0:T(8,128)(2,1)S(1)}, u32[]{:S(2)}, u32[]{:S(2)}) %collective-permute-start.12) | collective-permute-done | bytes 557088 | tf_op jit(solution)/shard_map/ppermute | solution.py:520
  94.9 1.4 %collective-permute-done.13.refs_1_ = s16[136,2048]{1,0:T(8,128)(2,1)S(1)} collective-permute-done((s16[136,2048]{1,0:T(8,128)(2,1)S(1)}, s16[136,2048]{1,0:T(8,128)(2,1)S(1)}, u32[]{:S(2)}, u32[]{:S(2)}) %collective-permute-start.13) | collective-permute-done | bytes 557088 | tf_op jit(solution)/shard_map/ppermute | solution.py:520
  96.3 1.4 %finish.1 = bf16[128,2048]{1,0:T(8,128)(2,1)} custom-call(f32[2,128,1024]{2,1,0:T(8,128)S(1)} %get-tuple-element.70.num_ref, f32[2,8,1024]{2,1,0:T(8,128)S(1)} %get-tuple-element.71.refs_6_.stat_ref, s16[136,2048]{1,0:T(8,128)(2,1)S(1)} %collective-permute-done.12.refs_0_, s16[136,2048]{1,0:T(8,128)(2,1)S(1)} %collective-permute-done.13.refs_1_), custom_call_target="tpu_custom_call" | custom-call | flops 262144 | bytes 65536 | tf_op jit(solution)/shard_map/finish/pallas_call | solution.py:419
  (2 shorter events, 0.0 us)
Async XLA Ops:
  0.6 16.4 %copy-start.8 = (f32[128]{0:T(128)S(1)}, f32[128]{0:T(128)}, u32[]{:S(2)}) copy-start(f32[128]{0:T(128)} %constant.16.clone) | copy-start | bytes 1540
  0.6 16.4 %copy-start.9 = (f32[128]{0:T(128)S(1)}, f32[128]{0:T(128)}, u32[]{:S(2)}) copy-start(f32[128]{0:T(128)} %constant.24) | copy-start | bytes 1540
  0.7 18.6 %copy-start.2 = (bf16[1,128,8192]{2,1,0:T(8,128)(2,1)S(1)}, bf16[1,128,8192]{2,1,0:T(8,128)(2,1)}, u32[]{:S(2)}) copy-start(bf16[1,128,8192]{2,1,0:T(8,128)(2,1)} %param.12) | copy-start | bytes 6291460
  0.7 18.6 %copy-start.7 = (f32[1024]{0:T(1024)S(1)}, f32[1024]{0:T(1024)}, u32[]{:S(2)}) copy-start(f32[1024]{0:T(1024)} %param.14) | copy-start | bytes 12292
  7.8 20.8 %collective-permute-start.3 = (bf16[3,8,16,1024]{3,2,1,0:T(8,128)(2,1)}, bf16[3,8,16,1024]{3,2,1,0:T(8,128)(2,1)S(1)}, u32[]{:S(2)}, u32[]{:S(2)}) collective-permute-start(bf16[3,8,16,1024]{3,2,1,0:T(8,128)(2,1)} %get-tuple-element.48), channel_id=1, source_target_pairs={{0,16},{16,0},{1,17},{17,1},{2,18},{18,2},{3,19},{19,3},{4,20},{20... | collective-permute-start | bytes 2359304 | tf_op jit(solution)/shard_map/ppermute | solution.py:523
  10.8 17.9 %collective-permute-start = (f32[32,2048]{1,0:T(8,128)}, f32[32,2048]{1,0:T(8,128)S(1)}, u32[]{:S(2)}, u32[]{:S(2)}) collective-permute-start(f32[32,2048]{1,0:T(8,128)} %get-tuple-element.38), channel_id=1, source_target_pairs={{0,1},{1,2},{2,3},{3,0},{4,5},{5,6},{6,7},{7,4},{8,9},{9,10},{10,1... | collective-permute-start | bytes 786440 | tf_op jit(solution)/shard_map/ppermute | solution.py:517
  12.4 19.7 %collective-permute-start.1 = (f32[32,2048]{1,0:T(8,128)}, f32[32,2048]{1,0:T(8,128)S(1)}, u32[]{:S(2)}, u32[]{:S(2)}) collective-permute-start(f32[32,2048]{1,0:T(8,128)} %get-tuple-element.39), channel_id=1, source_target_pairs={{0,2},{1,3},{2,0},{3,1},{4,6},{5,7},{6,4},{7,5},{8,10},{9,11},{10,... | collective-permute-start | bytes 786440 | tf_op jit(solution)/shard_map/ppermute | solution.py:517
  14.9 17.1 %collective-permute-start.2 = (f32[32,2048]{1,0:T(8,128)}, f32[32,2048]{1,0:T(8,128)}, u32[]{:S(2)}, u32[]{:S(2)}) collective-permute-start(f32[32,2048]{1,0:T(8,128)} %get-tuple-element.40), channel_id=1, source_target_pairs={{0,3},{1,0},{2,1},{3,2},{4,7},{5,4},{6,5},{7,6},{8,11},{9,8},{10,9... | collective-permute-start | bytes 786440 | tf_op jit(solution)/shard_map/ppermute | solution.py:517
  19.3 2.2 %copy-start = (bf16[1,1024,2048]{2,1,0:T(8,128)(2,1)S(1)}, bf16[1,1024,2048]{2,1,0:T(8,128)(2,1)}, u32[]{:S(2)}) copy-start(bf16[1,1024,2048]{2,1,0:T(8,128)(2,1)} %param.13) | copy-start | bytes 12582916
  21.4 7.1 %copy-start.4 = (bf16[8,16,1024]{2,1,0:T(8,128)(2,1)S(1)}, bf16[8,16,1024]{2,1,0:T(8,128)(2,1)}, u32[]{:S(2)}) copy-start(bf16[8,16,1024]{2,1,0:T(8,128)(2,1)} %get-tuple-element.45.refs_0_) | copy-start | bytes 786436
  21.4 7.1 %copy-start.5 = (bf16[8,16,1024]{2,1,0:T(8,128)(2,1)S(1)}, bf16[8,16,1024]{2,1,0:T(8,128)(2,1)}, u32[]{:S(2)}) copy-start(bf16[8,16,1024]{2,1,0:T(8,128)(2,1)} %get-tuple-element.46.refs_1_) | copy-start | bytes 786436
  21.5 7.1 %copy-start.6 = (bf16[8,16,1024]{2,1,0:T(8,128)(2,1)S(1)}, bf16[8,16,1024]{2,1,0:T(8,128)(2,1)}, u32[]{:S(2)}) copy-start(bf16[8,16,1024]{2,1,0:T(8,128)(2,1)} %get-tuple-element.47.refs_2_) | copy-start | bytes 786436
  21.5 17.7 %copy-start.3 = (f32[32,2048]{1,0:T(8,128)S(1)}, f32[32,2048]{1,0:T(8,128)}, u32[]{:S(2)}) copy-start(f32[32,2048]{1,0:T(8,128)} %get-tuple-element.53.refs_0_) | copy-start | bytes 786436
  21.5 18.8 %copy-start.1 = (bf16[1,1024,2048]{2,1,0:T(8,128)(2,1)S(1)}, bf16[1,1024,2048]{2,1,0:T(8,128)(2,1)}, u32[]{:S(2)}) copy-start(bf16[1,1024,2048]{2,1,0:T(8,128)(2,1)} %param.13) | copy-start | bytes 12582916
  32.0 21.0 %collective-permute-start.4 = (bf16[8,16,1024]{2,1,0:T(8,128)(2,1)S(1)}, bf16[8,16,1024]{2,1,0:T(8,128)(2,1)S(1)}, u32[]{:S(2)}, u32[]{:S(2)}) collective-permute-start(bf16[8,16,1024]{2,1,0:T(8,128)(2,1)S(1)} %get-tuple-element.59.refs_0_), channel_id=1, source_target_pairs={{0,1},{1,2},{2,3},{3,0},{4,5},{5,6},{6,7},{7,4},{8,9},{9,10},{10,1... | collective-permute-start | bytes 786440 | tf_op jit(solution)/shard_map/ppermute | solution.py:517
  38.2 17.5 %collective-permute-start.5 = (bf16[8,16,1024]{2,1,0:T(8,128)(2,1)S(1)}, bf16[8,16,1024]{2,1,0:T(8,128)(2,1)S(1)}, u32[]{:S(2)}, u32[]{:S(2)}) collective-permute-start(bf16[8,16,1024]{2,1,0:T(8,128)(2,1)S(1)} %get-tuple-element.60), channel_id=1, source_target_pairs={{0,3},{1,0},{2,1},{3,2},{4,7},{5,4},{6,5},{7,6},{8,11},{9,8},{10,9... | collective-permute-start | bytes 786440 | tf_op jit(solution)/shard_map/ppermute | solution.py:517
  40.3 6.1 %copy-start.10 = (bf16[8,16,2048]{2,1,0:T(8,128)(2,1)S(1)}, bf16[8,16,2048]{2,1,0:T(8,128)(2,1)}, u32[]{:S(2)}) copy-start(bf16[8,16,2048]{2,1,0:T(8,128)(2,1)} %get-tuple-element.69) | copy-start | bytes 1572868
  45.2 22.3 %collective-permute-start.6 = (s16[136,2048]{1,0:T(8,128)(2,1)S(1)}, s16[136,2048]{1,0:T(8,128)(2,1)S(1)}, u32[]{:S(2)}, u32[]{:S(2)}) collective-permute-start(s16[136,2048]{1,0:T(8,128)(2,1)S(1)} %attend.1.refs_0_), channel_id=1, source_target_pairs={{0,1},{1,0},{2,3},{3,2},{4,5},{5,4},{6,7},{7,6},{8,9},{9,8},{10,11... | collective-permute-start | bytes 1671176 | tf_op jit(solution)/shard_map/ppermute | solution.py:520
  46.4 28.1 %collective-permute-start.8 = (bf16[8,16,2048]{2,1,0:T(8,128)(2,1)S(1)}, bf16[8,16,2048]{2,1,0:T(8,128)(2,1)S(1)}, u32[]{:S(2)}, u32[]{:S(2)}) collective-permute-start(bf16[8,16,2048]{2,1,0:T(8,128)(2,1)S(1)} %copy-done.10), channel_id=1, source_target_pairs={{0,16},{16,0},{1,17},{17,1},{2,18},{18,2},{3,19},{19,3},{4,20},{20... | collective-permute-start | bytes 1572872 | tf_op jit(solution)/shard_map/ppermute | solution.py:523
  47.0 21.2 %collective-permute-start.7 = (bf16[8,16,1024]{2,1,0:T(8,128)(2,1)S(1)}, bf16[8,16,1024]{2,1,0:T(8,128)(2,1)S(1)}, u32[]{:S(2)}, u32[]{:S(2)}) collective-permute-start(bf16[8,16,1024]{2,1,0:T(8,128)(2,1)S(1)} %get-tuple-element.65), channel_id=1, source_target_pairs={{0,2},{1,3},{2,0},{3,1},{4,6},{5,7},{6,4},{7,5},{8,10},{9,11},{10,... | collective-permute-start | bytes 786440 | tf_op jit(solution)/shard_map/ppermute | solution.py:517
  68.5 26.4 %collective-permute-start.12 = (s16[136,2048]{1,0:T(8,128)(2,1)S(1)}, s16[136,2048]{1,0:T(8,128)(2,1)S(1)}, u32[]{:S(2)}, u32[]{:S(2)}) collective-permute-start(s16[136,2048]{1,0:T(8,128)(2,1)S(1)} %close.3.refs_0_), channel_id=1, source_target_pairs={{0,1},{1,0},{2,3},{3,2},{4,5},{5,4},{6,7},{7,6},{8,9},{9,8},{10,11... | collective-permute-start | bytes 1671176 | tf_op jit(solution)/shard_map/ppermute | solution.py:520
  68.6 27.7 %collective-permute-start.13 = (s16[136,2048]{1,0:T(8,128)(2,1)S(1)}, s16[136,2048]{1,0:T(8,128)(2,1)S(1)}, u32[]{:S(2)}, u32[]{:S(2)}) collective-permute-start(s16[136,2048]{1,0:T(8,128)(2,1)S(1)} %close.2.refs_0_), channel_id=1, source_target_pairs={{0,2},{1,3},{2,0},{3,1},{4,6},{5,7},{6,4},{7,5},{8,10},{9,11},{10,... | collective-permute-start | bytes 1671176 | tf_op jit(solution)/shard_map/ppermute | solution.py:520
  72.5 9.2 %collective-permute-start.10 = (bf16[8,16,1024]{2,1,0:T(8,128)(2,1)S(1)}, bf16[8,16,1024]{2,1,0:T(8,128)(2,1)S(1)}, u32[]{:S(2)}, u32[]{:S(2)}) collective-permute-start(bf16[8,16,1024]{2,1,0:T(8,128)(2,1)S(1)} %collective-permute-done.7.refs_1_.refs_4_), channel_id=1, source_target_pairs={{0,16},{16,0},{1,17},{17,1},{2,18},{18,2},{3,19},{19,3},{4,20},{20... | collective-permute-start | bytes 786440 | tf_op jit(solution)/shard_map/ppermute | solution.py:523
  73.0 14.4 %collective-permute-start.11 = (bf16[8,16,1024]{2,1,0:T(8,128)(2,1)S(1)}, bf16[8,16,1024]{2,1,0:T(8,128)(2,1)S(1)}, u32[]{:S(2)}, u32[]{:S(2)}) collective-permute-start(bf16[8,16,1024]{2,1,0:T(8,128)(2,1)S(1)} %collective-permute-done.5.refs_1_.refs_5_), channel_id=1, source_target_pairs={{0,16},{16,0},{1,17},{17,1},{2,18},{18,2},{3,19},{19,3},{4,20},{20... | collective-permute-start | bytes 786440 | tf_op jit(solution)/shard_map/ppermute | solution.py:523
  74.5 16.2 %collective-permute-start.9 = (bf16[8,16,1024]{2,1,0:T(8,128)(2,1)S(1)}, bf16[8,16,1024]{2,1,0:T(8,128)(2,1)S(1)}, u32[]{:S(2)}, u32[]{:S(2)}) collective-permute-start(bf16[8,16,1024]{2,1,0:T(8,128)(2,1)S(1)} %collective-permute-done.4.refs_0_.refs_3_), channel_id=1, source_target_pairs={{0,16},{16,0},{1,17},{17,1},{2,18},{18,2},{3,19},{19,3},{4,20},{20... | collective-permute-start | bytes 786440 | tf_op jit(solution)/shard_map/ppermute | solution.py:523

commit v8 on v7

--- a/solution.py
+++ b/solution.py
@@ -28,7 +28,7 @@
 EXP2_SCALE = SCALE * math.log2(math.e)
 LANES = 256
 KEYS = 512
-DEPTH = 512
+DEPTH = 1024
 TAIL = 8
 CONTRACT_FIRST = (((0,), (0,)), ((), ()))
 CONTRACT_LAST = (((1,), (1,)), ((), ()))

time: 97.2 us -> 98.5 us (1.013)
  no operation moved by 1% of the time
where the time goes in v8:
time: 98.5 us; the launch traced here: 98.3 us
  Pallas kernels  34.9 us (35%)
  waiting for transfers between devices  32 us (32%)
  starting transfers between devices  25.4 us (26%)
  local copies, waits for them, and re-layouts  2.23 us (2%)
  other arithmetic  2.22 us (2%)
  between operations  1.54 us (2%)
    pallas_call x4, Pallas kernels, attend(): pl.pallas_call(functools.partial(attend_kernel, is_open, len(earlier)), g...  18.8 us
    ppermute x5, waiting for transfers between devices, handed_on(): lax.ppermute(value, 'sec', [(i, (i + 1) % secs) for i in range(secs)])  15.2 us
    ppermute x6, starting transfers between devices, shifted(): lax.ppermute(value, 'rank', [(i, (i + k) % ranks) for i in range(ranks)])  14.1 us
    ppermute x3, waiting for transfers between devices, swapped(): return lax.ppermute(value, 'rank', [(i, i ^ bit) for i in range(ranks)])  10.9 us
    pallas_call x1, Pallas kernels, project(): pl.pallas_call(functools.partial(project_kernel, ranks), in_specs=[smem,...  7.78 us
    ppermute x5, starting transfers between devices, handed_on(): lax.ppermute(value, 'sec', [(i, (i + 1) % secs) for i in range(secs)])  6.09 us
    ppermute x6, waiting for transfers between devices, shifted(): lax.ppermute(value, 'rank', [(i, (i + k) % ranks) for i in range(ranks)])  5.91 us
    ppermute x3, starting transfers between devices, swapped(): return lax.ppermute(value, 'rank', [(i, i ^ bit) for i in range(ranks)])  5.15 us
  transfers between devices with their start and end apart: 14, of which 9 were waited for; matrix products, arithmetic and copies ran while one was open for 2% of the time, Pallas kernels for 26%

profile of v8, /device:TPU:0, one launch (start us, length us, event | category | flops | bytes accessed | tf_op | source)
XLA Modules:
  0.0 98.3 jit_solution(12995667480055097126)
XLA Ops:
  0.6 0.0 copy-start.8
  0.6 0.0 copy-start.9
  0.7 0.0 copy-start.2
  0.7 0.0 copy-start.7
  0.7 7.8 %project.1 = (f32[32,2048]{1,0:T(8,128)}, f32[32,2048]{1,0:T(8,128)}, f32[32,2048]{1,0:T(8,128)}, f32[32,2048]{1,0:T(8,128)}, bf16[8,16,2048]{2,1,0:T(8,128)(2,1...) custom-call(s32[1]{0:T(128)} %bitcast.1.rank_ref, ...), custom_call_target="tpu_custom_call" | custom-call | flops 1048576 | bytes 65536 | tf_op jit(solution)/shard_map/project/pallas_call | solution.py:154
  8.5 3.0 %collective-permute-start.3 = (bf16[3,8,16,1024]{3,2,1,0:T(8,128)(2,1)}, bf16[3,8,16,1024]{3,2,1,0:T(8,128)(2,1)S(1)}, u32[]{:S(2)}, u32[]{:S(2)}) collective-permute-start(bf16[3,8,16,1024]{3,2,1,0:T(8,128)(2,1)} %get-tuple-element.48), channel_id=1, source_target_pairs={{0,16},{16,0},{1,17},{17,1},{2,18},{18,2},{3,19},{19,3},{4,20},{20... | collective-permute-start | bytes 2359304 | tf_op jit(solution)/shard_map/ppermute | solution.py:523
  11.5 1.6 %collective-permute-start = (f32[32,2048]{1,0:T(8,128)}, f32[32,2048]{1,0:T(8,128)S(1)}, u32[]{:S(2)}, u32[]{:S(2)}) collective-permute-start(f32[32,2048]{1,0:T(8,128)} %get-tuple-element.38), channel_id=1, source_target_pairs={{0,1},{1,2},{2,3},{3,0},{4,5},{5,6},{6,7},{7,4},{8,9},{9,10},{10,1... | collective-permute-start | bytes 786440 | tf_op jit(solution)/shard_map/ppermute | solution.py:517
  13.0 2.6 %collective-permute-start.1 = (f32[32,2048]{1,0:T(8,128)}, f32[32,2048]{1,0:T(8,128)S(1)}, u32[]{:S(2)}, u32[]{:S(2)}) collective-permute-start(f32[32,2048]{1,0:T(8,128)} %get-tuple-element.39), channel_id=1, source_target_pairs={{0,2},{1,3},{2,0},{3,1},{4,6},{5,7},{6,4},{7,5},{8,10},{9,11},{10,... | collective-permute-start | bytes 786440 | tf_op jit(solution)/shard_map/ppermute | solution.py:517
  15.6 1.4 %collective-permute-start.2 = (f32[32,2048]{1,0:T(8,128)}, f32[32,2048]{1,0:T(8,128)}, u32[]{:S(2)}, u32[]{:S(2)}) collective-permute-start(f32[32,2048]{1,0:T(8,128)} %get-tuple-element.40), channel_id=1, source_target_pairs={{0,3},{1,0},{2,1},{3,2},{4,7},{5,4},{6,5},{7,6},{8,11},{9,8},{10,9... | collective-permute-start | bytes 786440 | tf_op jit(solution)/shard_map/ppermute | solution.py:517
  17.7 0.0 copy-done.8
  17.7 0.0 copy-done.9
  17.7 1.9 %fusion = (f32[1024,128]{1,0:T(8,128)S(1)}, f32[1024,128]{1,0:T(8,128)S(1)}) fusion(f32[128]{0:T(128)S(1)} %copy-done.9, f32[128]{0:T(128)S(1)} %copy-done.8, f32[1024]{0:T(1024)S(1)} %add_convert_fusion), kind=kLoop, calls=%fused_computation.2 | loop fusion | flops 262144 | bytes 1053696 | tf_op jit(solution)/shard_map/mul | solution.py:53
  19.6 0.3 fusion.1
  19.9 0.0 copy-done.2
  19.9 0.0 copy-done.7
  19.9 0.0 copy-start
  19.9 2.2 %copy-done = bf16[1,1024,2048]{2,1,0:T(8,128)(2,1)S(1)} copy-done((bf16[1,1024,2048]{2,1,0:T(8,128)(2,1)S(1)}, bf16[1,1024,2048]{2,1,0:T(8,128)(2,1)}, u32[]{:S(2)}) %copy-start) | copy-done | bytes 4194328
  22.1 0.0 copy-start.4
  22.1 0.0 copy-start.5
  22.1 0.0 copy-start.6
  22.1 0.0 copy-start.3
  22.1 0.0 copy-start.1
  22.1 2.9 %prepare.1 = (bf16[8192,128]{1,0:T(8,128)(2,1)S(1)}, bf16[8,1024,128]{2,1,0:T(8,128)(2,1)S(1)}) custom-call(bf16[128,8192]{1,0:T(8,128)(2,1)S(1)} %bitcast.22, bf16[1024,2048]{1,0:T(8,128)(2,1)S(1)} %bitcast.17, f32[1,1024]{1,0:T(1,128)S(1)} %bitcast.23, f32[128,128]{1,0:T(8,128)S(1)} %get-tuple-element.75.qc_ref, f32[128,128]{1,0:T(8,128)S(1)} %get-tuple-element.74.qs_ref, ...), custom_call_target="tpu_custom_call" | custom-call | flops 1073741824 | bytes 65536 | tf_op jit(solution)/shard_map/prepare/pallas_call | solution.py:192
  25.1 4.2 %collective-permute-done.3.refs_3_ = bf16[3,8,16,1024]{3,2,1,0:T(8,128)(2,1)S(1)} collective-permute-done((bf16[3,8,16,1024]{3,2,1,0:T(8,128)(2,1)}, bf16[3,8,16,1024]{3,2,1,0:T(8,128)(2,1)S(1)}, u32[]{:S(2)}, u32[]{:S(2)}) %collective-permute-start.3) | collective-permute-done | bytes 786464 | tf_op jit(solution)/shard_map/ppermute | solution.py:523
  29.2 0.0 copy-done.4
  29.2 0.0 copy-done.5
  29.2 0.0 copy-done.6
  29.2 0.1 choose.1
  29.4 0.0 collective-permute-done.refs_1_
  29.4 3.3 %collective-permute-done.1.refs_2_ = f32[32,2048]{1,0:T(8,128)S(1)} collective-permute-done((f32[32,2048]{1,0:T(8,128)}, f32[32,2048]{1,0:T(8,128)S(1)}, u32[]{:S(2)}, u32[]{:S(2)}) %collective-permute-start.1) | collective-permute-done | bytes 262176 | tf_op jit(solution)/shard_map/ppermute | solution.py:517
  32.7 0.0 collective-permute-done.2.refs_3_
  32.7 6.2 %collective-permute-start.4 = (bf16[8,16,1024]{2,1,0:T(8,128)(2,1)S(1)}, bf16[8,16,1024]{2,1,0:T(8,128)(2,1)S(1)}, u32[]{:S(2)}, u32[]{:S(2)}) collective-permute-start(bf16[8,16,1024]{2,1,0:T(8,128)(2,1)S(1)} %get-tuple-element.59.refs_0_), channel_id=1, source_target_pairs={{0,1},{1,2},{2,3},{3,0},{4,5},{5,6},{6,7},{7,4},{8,9},{9,10},{10,1... | collective-permute-start | bytes 786440 | tf_op jit(solution)/shard_map/ppermute | solution.py:517
  38.9 0.9 collective-permute-start.5
  39.8 0.0 copy-done.3
  39.8 1.1 %gather.1 = (bf16[8,32,128]{2,1,0:T(8,128)(2,1)S(1)}, bf16[8,32,128]{2,1,0:T(8,128)(2,1)S(1)}) custom-call(s32[1]{0:T(128)} %bitcast.1.rank_ref, f32[128,128]{1,0:T(8,128)S(1)} %get-tuple-element.75.qc_ref, f32[128,128]{1,0:T(8,128)S(1)} %get-tuple-element.74.qs_ref, f32[32,2048]{1,0:T(8,128)S(1)} %copy-done.3, f32[32,2048]{1,0:T(8,128)S(1)} %collective-permute-done.refs_1_, ...), custom_call_target="tpu_custom_call" | custom-call | flops 262144 | bytes 65536 | tf_op jit(solution)/shard_map/gather/pallas_call | solution.py:278
  40.9 0.0 copy-done.1
  40.9 0.0 copy-start.10
  40.9 4.9 %attend.1.refs_0_ = s16[136,2048]{1,0:T(8,128)(2,1)S(1)} custom-call(s32[1]{0:T(128)} %bitcast.12.length_ref, s32[1]{0:T(128)} %bitcast.1.rank_ref, bf16[8192,128]{1,0:T(8,128)(2,1)S(1)} %get-tuple-element.43.q_ref, bf16[8,1024,128]{2,1,0:T(8,128)(2,1)S(1)} %get-tuple-element.44.k_ref, bf16[1024,2048]{1,0:T(8,128)(2,1)S(1)} %bitcast.18, ...), custom_call_target="tpu_custom_call" | custom-call | flops 268435456 | bytes 65536 | tf_op jit(solution)/shard_map/attend/pallas_call | solution.py:374
  45.9 1.2 %collective-permute-start.6 = (s16[136,2048]{1,0:T(8,128)(2,1)S(1)}, s16[136,2048]{1,0:T(8,128)(2,1)S(1)}, u32[]{:S(2)}, u32[]{:S(2)}) collective-permute-start(s16[136,2048]{1,0:T(8,128)(2,1)S(1)} %attend.1.refs_0_), channel_id=1, source_target_pairs={{0,1},{1,0},{2,3},{3,2},{4,5},{5,4},{6,7},{7,6},{8,9},{9,8},{10,11... | collective-permute-start | bytes 1671176 | tf_op jit(solution)/shard_map/ppermute | solution.py:520
  47.0 0.0 copy-done.10
  47.0 0.5 collective-permute-start.8
  47.6 1.5 %collective-permute-start.7 = (bf16[8,16,1024]{2,1,0:T(8,128)(2,1)S(1)}, bf16[8,16,1024]{2,1,0:T(8,128)(2,1)S(1)}, u32[]{:S(2)}, u32[]{:S(2)}) collective-permute-start(bf16[8,16,1024]{2,1,0:T(8,128)(2,1)S(1)} %get-tuple-element.65), channel_id=1, source_target_pairs={{0,2},{1,3},{2,0},{3,1},{4,6},{5,7},{6,4},{7,5},{8,10},{9,11},{10,... | collective-permute-start | bytes 786440 | tf_op jit(solution)/shard_map/ppermute | solution.py:517
  49.0 4.6 %attend_open.3 = (f32[2,128,1024]{2,1,0:T(8,128)S(1)}, f32[2,8,1024]{2,1,0:T(8,128)S(1)}) custom-call(s32[1]{0:T(128)} %bitcast.13.length_ref, s32[1]{0:T(128)} %bitcast.1.rank_ref, bf16[8192,128]{1,0:T(8,128)(2,1)S(1)} %get-tuple-element.43.q_ref, bf16[8,1024,128]{2,1,0:T(8,128)(2,1)S(1)} %get-tuple-element.44.k_ref, bf16[1024,2048]{1,0:T(8,128)(2,1)S(1)} %bitcast.19, ...), custom_call_target="tpu_custom_call" | custom-call | flops 268435456 | bytes 65536 | tf_op jit(solution)/shard_map/attend_open/pallas_call | solution.py:374
  53.7 0.0 collective-permute-done.4.refs_0_.refs_3_
  53.7 2.6 %collective-permute-done.5.refs_1_.refs_5_ = bf16[8,16,1024]{2,1,0:T(8,128)(2,1)S(1)} collective-permute-done((bf16[8,16,1024]{2,1,0:T(8,128)(2,1)S(1)}, bf16[8,16,1024]{2,1,0:T(8,128)(2,1)S(1)}, u32[]{:S(2)}, u32[]{:S(2)}) %collective-permute-start.5) | collective-permute-done | bytes 262176 | tf_op jit(solution)/shard_map/ppermute | solution.py:517
  56.3 4.6 %attend_open.4 = (f32[2,128,1024]{2,1,0:T(8,128)S(1)}, f32[2,8,1024]{2,1,0:T(8,128)S(1)}) custom-call(s32[1]{0:T(128)} %bitcast.14.length_ref, s32[1]{0:T(128)} %bitcast.1.rank_ref, bf16[8192,128]{1,0:T(8,128)(2,1)S(1)} %get-tuple-element.43.q_ref, bf16[8,1024,128]{2,1,0:T(8,128)(2,1)S(1)} %get-tuple-element.44.k_ref, bf16[1024,2048]{1,0:T(8,128)(2,1)S(1)} %bitcast.20, ...), custom_call_target="tpu_custom_call" | custom-call | flops 4294967296 | bytes 65536 | tf_op jit(solution)/shard_map/attend_open/pallas_call | solution.py:374
  60.9 7.2 %collective-permute-done.6.refs_0_ = s16[136,2048]{1,0:T(8,128)(2,1)S(1)} collective-permute-done((s16[136,2048]{1,0:T(8,128)(2,1)S(1)}, s16[136,2048]{1,0:T(8,128)(2,1)S(1)}, u32[]{:S(2)}, u32[]{:S(2)}) %collective-permute-start.6) | collective-permute-done | bytes 557088 | tf_op jit(solution)/shard_map/ppermute | solution.py:520
  68.1 0.6 close.2.refs_0_
  68.7 0.0 collective-permute-done.7.refs_1_.refs_4_
  68.7 0.4 close.3.refs_0_
  69.1 0.1 collective-permute-start.12
  69.2 3.9 %collective-permute-start.13 = (s16[136,2048]{1,0:T(8,128)(2,1)S(1)}, s16[136,2048]{1,0:T(8,128)(2,1)S(1)}, u32[]{:S(2)}, u32[]{:S(2)}) collective-permute-start(s16[136,2048]{1,0:T(8,128)(2,1)S(1)} %close.2.refs_0_), channel_id=1, source_target_pairs={{0,2},{1,3},{2,0},{3,1},{4,6},{5,7},{6,4},{7,5},{8,10},{9,11},{10,... | collective-permute-start | bytes 1671176 | tf_op jit(solution)/shard_map/ppermute | solution.py:520
  73.1 0.5 collective-permute-start.10
  73.6 1.5 %collective-permute-start.11 = (bf16[8,16,1024]{2,1,0:T(8,128)(2,1)S(1)}, bf16[8,16,1024]{2,1,0:T(8,128)(2,1)S(1)}, u32[]{:S(2)}, u32[]{:S(2)}) collective-permute-start(bf16[8,16,1024]{2,1,0:T(8,128)(2,1)S(1)} %collective-permute-done.5.refs_1_.refs_5_), channel_id=1, source_target_pairs={{0,16},{16,0},{1,17},{17,1},{2,18},{18,2},{3,19},{19,3},{4,20},{20... | collective-permute-start | bytes 786440 | tf_op jit(solution)/shard_map/ppermute | solution.py:523
  75.1 0.0 collective-permute-done.8.kept_ref
  75.1 0.5 collective-permute-start.9
  75.6 4.6 %attend_open.5 = (f32[2,128,1024]{2,1,0:T(8,128)S(1)}, f32[2,8,1024]{2,1,0:T(8,128)S(1)}) custom-call(s32[1]{0:T(128)} %bitcast.15.length_ref, s32[1]{0:T(128)} %bitcast.1.rank_ref, bf16[8192,128]{1,0:T(8,128)(2,1)S(1)} %get-tuple-element.43.q_ref, bf16[8,1024,128]{2,1,0:T(8,128)(2,1)S(1)} %get-tuple-element.44.k_ref, bf16[1024,2048]{1,0:T(8,128)(2,1)S(1)} %bitcast.21, ...), custom_call_target="tpu_custom_call" | custom-call | flops 268435456 | bytes 65536 | tf_op jit(solution)/shard_map/attend_open/pallas_call | solution.py:374
  80.3 2.1 %collective-permute-done.10.refs_1_ = bf16[8,16,1024]{2,1,0:T(8,128)(2,1)S(1)} collective-permute-done((bf16[8,16,1024]{2,1,0:T(8,128)(2,1)S(1)}, bf16[8,16,1024]{2,1,0:T(8,128)(2,1)S(1)}, u32[]{:S(2)}, u32[]{:S(2)}) %collective-permute-start.10) | collective-permute-done | bytes 262176 | tf_op jit(solution)/shard_map/ppermute | solution.py:523
  82.3 5.6 %collective-permute-done.11.refs_2_ = bf16[8,16,1024]{2,1,0:T(8,128)(2,1)S(1)} collective-permute-done((bf16[8,16,1024]{2,1,0:T(8,128)(2,1)S(1)}, bf16[8,16,1024]{2,1,0:T(8,128)(2,1)S(1)}, u32[]{:S(2)}, u32[]{:S(2)}) %collective-permute-start.11) | collective-permute-done | bytes 262176 | tf_op jit(solution)/shard_map/ppermute | solution.py:523
  87.9 3.4 %collective-permute-done.9.refs_0_ = bf16[8,16,1024]{2,1,0:T(8,128)(2,1)S(1)} collective-permute-done((bf16[8,16,1024]{2,1,0:T(8,128)(2,1)S(1)}, bf16[8,16,1024]{2,1,0:T(8,128)(2,1)S(1)}, u32[]{:S(2)}, u32[]{:S(2)}) %collective-permute-start.9) | collective-permute-done | bytes 262176 | tf_op jit(solution)/shard_map/ppermute | solution.py:523
  91.3 1.9 %arrange.1 = bf16[32,16,2048]{2,1,0:T(8,128)(2,1)} custom-call(s32[1]{0:T(128)} %bitcast.8.sec_ref, s32[1]{0:T(128)} %bitcast.1.rank_ref, bf16[8,16,2048]{2,1,0:T(8,128)(2,1)S(1)} %collective-permute-done.8.kept_ref, bf16[8,16,1024]{2,1,0:T(8,128)(2,1)S(1)} %collective-permute-done.9.refs_0_, bf16[8,16,1024]{2,1,0:T(8,128)(2,1)S(1)} %collective-permute-done.10.refs_1_, ...), custom_call_target="tpu_custom_call" | custom-call | flops 262144 | bytes 65536 | tf_op jit(solution)/shard_map/arrange/pallas_call | solution.py:489
  93.2 2.4 %collective-permute-done.12.refs_0_ = s16[136,2048]{1,0:T(8,128)(2,1)S(1)} collective-permute-done((s16[136,2048]{1,0:T(8,128)(2,1)S(1)}, s16[136,2048]{1,0:T(8,128)(2,1)S(1)}, u32[]{:S(2)}, u32[]{:S(2)}) %collective-permute-start.12) | collective-permute-done | bytes 557088 | tf_op jit(solution)/shard_map/ppermute | solution.py:520
  95.6 1.3 %collective-permute-done.13.refs_1_ = s16[136,2048]{1,0:T(8,128)(2,1)S(1)} collective-permute-done((s16[136,2048]{1,0:T(8,128)(2,1)S(1)}, s16[136,2048]{1,0:T(8,128)(2,1)S(1)}, u32[]{:S(2)}, u32[]{:S(2)}) %collective-permute-start.13) | collective-permute-done | bytes 557088 | tf_op jit(solution)/shard_map/ppermute | solution.py:520
  96.9 1.4 %finish.1 = bf16[128,2048]{1,0:T(8,128)(2,1)} custom-call(f32[2,128,1024]{2,1,0:T(8,128)S(1)} %get-tuple-element.70.num_ref, f32[2,8,1024]{2,1,0:T(8,128)S(1)} %get-tuple-element.71.refs_6_.stat_ref, s16[136,2048]{1,0:T(8,128)(2,1)S(1)} %collective-permute-done.12.refs_0_, s16[136,2048]{1,0:T(8,128)(2,1)S(1)} %collective-permute-done.13.refs_1_), custom_call_target="tpu_custom_call" | custom-call | flops 262144 | bytes 65536 | tf_op jit(solution)/shard_map/finish/pallas_call | solution.py:419
  (2 shorter events, 0.0 us)
Async XLA Ops:
  0.6 17.0 %copy-start.8 = (f32[128]{0:T(128)S(1)}, f32[128]{0:T(128)}, u32[]{:S(2)}) copy-start(f32[128]{0:T(128)} %constant.16.clone) | copy-start | bytes 1540
  0.6 17.0 %copy-start.9 = (f32[128]{0:T(128)S(1)}, f32[128]{0:T(128)}, u32[]{:S(2)}) copy-start(f32[128]{0:T(128)} %constant.24) | copy-start | bytes 1540
  0.7 19.2 %copy-start.2 = (bf16[1,128,8192]{2,1,0:T(8,128)(2,1)S(1)}, bf16[1,128,8192]{2,1,0:T(8,128)(2,1)}, u32[]{:S(2)}) copy-start(bf16[1,128,8192]{2,1,0:T(8,128)(2,1)} %param.12) | copy-start | bytes 6291460
  0.7 19.2 %copy-start.7 = (f32[1024]{0:T(1024)S(1)}, f32[1024]{0:T(1024)}, u32[]{:S(2)}) copy-start(f32[1024]{0:T(1024)} %param.14) | copy-start | bytes 12292
  8.5 20.8 %collective-permute-start.3 = (bf16[3,8,16,1024]{3,2,1,0:T(8,128)(2,1)}, bf16[3,8,16,1024]{3,2,1,0:T(8,128)(2,1)S(1)}, u32[]{:S(2)}, u32[]{:S(2)}) collective-permute-start(bf16[3,8,16,1024]{3,2,1,0:T(8,128)(2,1)} %get-tuple-element.48), channel_id=1, source_target_pairs={{0,16},{16,0},{1,17},{17,1},{2,18},{18,2},{3,19},{19,3},{4,20},{20... | collective-permute-start | bytes 2359304 | tf_op jit(solution)/shard_map/ppermute | solution.py:523
  11.5 17.9 %collective-permute-start = (f32[32,2048]{1,0:T(8,128)}, f32[32,2048]{1,0:T(8,128)S(1)}, u32[]{:S(2)}, u32[]{:S(2)}) collective-permute-start(f32[32,2048]{1,0:T(8,128)} %get-tuple-element.38), channel_id=1, source_target_pairs={{0,1},{1,2},{2,3},{3,0},{4,5},{5,6},{6,7},{7,4},{8,9},{9,10},{10,1... | collective-permute-start | bytes 786440 | tf_op jit(solution)/shard_map/ppermute | solution.py:517
  13.0 19.6 %collective-permute-start.1 = (f32[32,2048]{1,0:T(8,128)}, f32[32,2048]{1,0:T(8,128)S(1)}, u32[]{:S(2)}, u32[]{:S(2)}) collective-permute-start(f32[32,2048]{1,0:T(8,128)} %get-tuple-element.39), channel_id=1, source_target_pairs={{0,2},{1,3},{2,0},{3,1},{4,6},{5,7},{6,4},{7,5},{8,10},{9,11},{10,... | collective-permute-start | bytes 786440 | tf_op jit(solution)/shard_map/ppermute | solution.py:517
  15.6 17.0 %collective-permute-start.2 = (f32[32,2048]{1,0:T(8,128)}, f32[32,2048]{1,0:T(8,128)}, u32[]{:S(2)}, u32[]{:S(2)}) collective-permute-start(f32[32,2048]{1,0:T(8,128)} %get-tuple-element.40), channel_id=1, source_target_pairs={{0,3},{1,0},{2,1},{3,2},{4,7},{5,4},{6,5},{7,6},{8,11},{9,8},{10,9... | collective-permute-start | bytes 786440 | tf_op jit(solution)/shard_map/ppermute | solution.py:517
  19.9 2.2 %copy-start = (bf16[1,1024,2048]{2,1,0:T(8,128)(2,1)S(1)}, bf16[1,1024,2048]{2,1,0:T(8,128)(2,1)}, u32[]{:S(2)}) copy-start(bf16[1,1024,2048]{2,1,0:T(8,128)(2,1)} %param.13) | copy-start | bytes 12582916
  22.1 7.1 %copy-start.4 = (bf16[8,16,1024]{2,1,0:T(8,128)(2,1)S(1)}, bf16[8,16,1024]{2,1,0:T(8,128)(2,1)}, u32[]{:S(2)}) copy-start(bf16[8,16,1024]{2,1,0:T(8,128)(2,1)} %get-tuple-element.45.refs_0_) | copy-start | bytes 786436
  22.1 7.1 %copy-start.5 = (bf16[8,16,1024]{2,1,0:T(8,128)(2,1)S(1)}, bf16[8,16,1024]{2,1,0:T(8,128)(2,1)}, u32[]{:S(2)}) copy-start(bf16[8,16,1024]{2,1,0:T(8,128)(2,1)} %get-tuple-element.46.refs_1_) | copy-start | bytes 786436
  22.1 7.1 %copy-start.6 = (bf16[8,16,1024]{2,1,0:T(8,128)(2,1)S(1)}, bf16[8,16,1024]{2,1,0:T(8,128)(2,1)}, u32[]{:S(2)}) copy-start(bf16[8,16,1024]{2,1,0:T(8,128)(2,1)} %get-tuple-element.47.refs_2_) | copy-start | bytes 786436
  22.1 17.7 %copy-start.3 = (f32[32,2048]{1,0:T(8,128)S(1)}, f32[32,2048]{1,0:T(8,128)}, u32[]{:S(2)}) copy-start(f32[32,2048]{1,0:T(8,128)} %get-tuple-element.53.refs_0_) | copy-start | bytes 786436
  22.1 18.8 %copy-start.1 = (bf16[1,1024,2048]{2,1,0:T(8,128)(2,1)S(1)}, bf16[1,1024,2048]{2,1,0:T(8,128)(2,1)}, u32[]{:S(2)}) copy-start(bf16[1,1024,2048]{2,1,0:T(8,128)(2,1)} %param.13) | copy-start | bytes 12582916
  32.7 21.0 %collective-permute-start.4 = (bf16[8,16,1024]{2,1,0:T(8,128)(2,1)S(1)}, bf16[8,16,1024]{2,1,0:T(8,128)(2,1)S(1)}, u32[]{:S(2)}, u32[]{:S(2)}) collective-permute-start(bf16[8,16,1024]{2,1,0:T(8,128)(2,1)S(1)} %get-tuple-element.59.refs_0_), channel_id=1, source_target_pairs={{0,1},{1,2},{2,3},{3,0},{4,5},{5,6},{6,7},{7,4},{8,9},{9,10},{10,1... | collective-permute-start | bytes 786440 | tf_op jit(solution)/shard_map/ppermute | solution.py:517
  38.9 17.4 %collective-permute-start.5 = (bf16[8,16,1024]{2,1,0:T(8,128)(2,1)S(1)}, bf16[8,16,1024]{2,1,0:T(8,128)(2,1)S(1)}, u32[]{:S(2)}, u32[]{:S(2)}) collective-permute-start(bf16[8,16,1024]{2,1,0:T(8,128)(2,1)S(1)} %get-tuple-element.60), channel_id=1, source_target_pairs={{0,3},{1,0},{2,1},{3,2},{4,7},{5,4},{6,5},{7,6},{8,11},{9,8},{10,9... | collective-permute-start | bytes 786440 | tf_op jit(solution)/shard_map/ppermute | solution.py:517
  40.9 6.1 %copy-start.10 = (bf16[8,16,2048]{2,1,0:T(8,128)(2,1)S(1)}, bf16[8,16,2048]{2,1,0:T(8,128)(2,1)}, u32[]{:S(2)}) copy-start(bf16[8,16,2048]{2,1,0:T(8,128)(2,1)} %get-tuple-element.69) | copy-start | bytes 1572868
  45.9 22.2 %collective-permute-start.6 = (s16[136,2048]{1,0:T(8,128)(2,1)S(1)}, s16[136,2048]{1,0:T(8,128)(2,1)S(1)}, u32[]{:S(2)}, u32[]{:S(2)}) collective-permute-start(s16[136,2048]{1,0:T(8,128)(2,1)S(1)} %attend.1.refs_0_), channel_id=1, source_target_pairs={{0,1},{1,0},{2,3},{3,2},{4,5},{5,4},{6,7},{7,6},{8,9},{9,8},{10,11... | collective-permute-start | bytes 1671176 | tf_op jit(solution)/shard_map/ppermute | solution.py:520
  47.0 28.1 %collective-permute-start.8 = (bf16[8,16,2048]{2,1,0:T(8,128)(2,1)S(1)}, bf16[8,16,2048]{2,1,0:T(8,128)(2,1)S(1)}, u32[]{:S(2)}, u32[]{:S(2)}) collective-permute-start(bf16[8,16,2048]{2,1,0:T(8,128)(2,1)S(1)} %copy-done.10), channel_id=1, source_target_pairs={{0,16},{16,0},{1,17},{17,1},{2,18},{18,2},{3,19},{19,3},{4,20},{20... | collective-permute-start | bytes 1572872 | tf_op jit(solution)/shard_map/ppermute | solution.py:523
  47.6 21.1 %collective-permute-start.7 = (bf16[8,16,1024]{2,1,0:T(8,128)(2,1)S(1)}, bf16[8,16,1024]{2,1,0:T(8,128)(2,1)S(1)}, u32[]{:S(2)}, u32[]{:S(2)}) collective-permute-start(bf16[8,16,1024]{2,1,0:T(8,128)(2,1)S(1)} %get-tuple-element.65), channel_id=1, source_target_pairs={{0,2},{1,3},{2,0},{3,1},{4,6},{5,7},{6,4},{7,5},{8,10},{9,11},{10,... | collective-permute-start | bytes 786440 | tf_op jit(solution)/shard_map/ppermute | solution.py:517
  69.1 26.5 %collective-permute-start.12 = (s16[136,2048]{1,0:T(8,128)(2,1)S(1)}, s16[136,2048]{1,0:T(8,128)(2,1)S(1)}, u32[]{:S(2)}, u32[]{:S(2)}) collective-permute-start(s16[136,2048]{1,0:T(8,128)(2,1)S(1)} %close.3.refs_0_), channel_id=1, source_target_pairs={{0,1},{1,0},{2,3},{3,2},{4,5},{5,4},{6,7},{7,6},{8,9},{9,8},{10,11... | collective-permute-start | bytes 1671176 | tf_op jit(solution)/shard_map/ppermute | solution.py:520
  69.2 27.7 %collective-permute-start.13 = (s16[136,2048]{1,0:T(8,128)(2,1)S(1)}, s16[136,2048]{1,0:T(8,128)(2,1)S(1)}, u32[]{:S(2)}, u32[]{:S(2)}) collective-permute-start(s16[136,2048]{1,0:T(8,128)(2,1)S(1)} %close.2.refs_0_), channel_id=1, source_target_pairs={{0,2},{1,3},{2,0},{3,1},{4,6},{5,7},{6,4},{7,5},{8,10},{9,11},{10,... | collective-permute-start | bytes 1671176 | tf_op jit(solution)/shard_map/ppermute | solution.py:520
  73.1 9.2 %collective-permute-start.10 = (bf16[8,16,1024]{2,1,0:T(8,128)(2,1)S(1)}, bf16[8,16,1024]{2,1,0:T(8,128)(2,1)S(1)}, u32[]{:S(2)}, u32[]{:S(2)}) collective-permute-start(bf16[8,16,1024]{2,1,0:T(8,128)(2,1)S(1)} %collective-permute-done.7.refs_1_.refs_4_), channel_id=1, source_target_pairs={{0,16},{16,0},{1,17},{17,1},{2,18},{18,2},{3,19},{19,3},{4,20},{20... | collective-permute-start | bytes 786440 | tf_op jit(solution)/shard_map/ppermute | solution.py:523
  73.6 14.3 %collective-permute-start.11 = (bf16[8,16,1024]{2,1,0:T(8,128)(2,1)S(1)}, bf16[8,16,1024]{2,1,0:T(8,128)(2,1)S(1)}, u32[]{:S(2)}, u32[]{:S(2)}) collective-permute-start(bf16[8,16,1024]{2,1,0:T(8,128)(2,1)S(1)} %collective-permute-done.5.refs_1_.refs_5_), channel_id=1, source_target_pairs={{0,16},{16,0},{1,17},{17,1},{2,18},{18,2},{3,19},{19,3},{4,20},{20... | collective-permute-start | bytes 786440 | tf_op jit(solution)/shard_map/ppermute | solution.py:523
  75.1 16.2 %collective-permute-start.9 = (bf16[8,16,1024]{2,1,0:T(8,128)(2,1)S(1)}, bf16[8,16,1024]{2,1,0:T(8,128)(2,1)S(1)}, u32[]{:S(2)}, u32[]{:S(2)}) collective-permute-start(bf16[8,16,1024]{2,1,0:T(8,128)(2,1)S(1)} %collective-permute-done.4.refs_0_.refs_3_), channel_id=1, source_target_pairs={{0,16},{16,0},{1,17},{17,1},{2,18},{18,2},{3,19},{19,3},{4,20},{20... | collective-permute-start | bytes 786440 | tf_op jit(solution)/shard_map/ppermute | solution.py:523
